TPU v7x, 32 devices: a whole 2x2x4 slice. The times are simulated.
32 devices in a mesh: row: 4 (over z), col: 8 (over y, x, core).
Axes of the slice: x: 2, y: 2, z: 4, core: 2. Of those that a mesh axis runs over, the one named last changes fastest.
Arguments:
- children: float32 [2, 1024, 4096], P(None, 'row', 'col'), may hold values from -1 to 6, as said below
- block_maps: int32 [2, 16], replicated, may hold values from 0 to 15, each once within a row
Outputs:
- panel_rows: float32 [512, 4096], P(None, 'col')
- trailing: float32 [2, 1024, 4096], P(None, 'row', 'col')
Inputs may be any that keep to these rules, and one draw needn't show every extreme that they name: Each row of block_maps names every parent column block once. `children`: each child's block is upper triangular in its own column order: entry (i, j) is zero where j < i.
All inputs are finite; a program needn't handle non-finite values.
Results may differ from a plain program's by a relative error of at most 0.000078.
Values sent between devices are 32-bit elements; how exact they have to be, the bound alone decides.
No kernel may reach another device: no remote copies, remote signals or barrier semaphores. Data moves between devices by JAX's collectives and lax.ppermute only.
A program may use at most 64 MiB of HBM per device.

v0:
```python
import jax
import jax.numpy as jnp
from jax import lax
from jax.experimental import pallas as pl
from jax.experimental.pallas import tpu as pltpu
from jax.sharding import PartitionSpec as P

PANEL = 256
LANES = 128
SUBS = 8


def dot(left, right, contract):
    return lax.dot_general(
        left,
        right,
        (contract, ((), ())),
        precision=lax.Precision.HIGHEST,
        preferred_element_type=jnp.float32,
    )


def row_of(x, i):
    return jnp.broadcast_to(x[i : i + 1, :], (SUBS, LANES))


def column_of(x, j):
    return jnp.broadcast_to(x[:, j : j + 1], (SUBS, LANES))


def combined(weights, rows):
    p = [w * r for w, r in zip(weights, rows)]
    return ((p[0] + p[1]) + (p[2] + p[3])) + ((p[4] + p[5]) + (p[6] + p[7]))


def small_inverse(cols):
    sub = lax.broadcasted_iota(jnp.int32, (SUBS, LANES), 0)
    x = list(cols)
    t = [jnp.zeros((SUBS, LANES), jnp.float32) for _ in range(SUBS)]
    for j in range(SUBS):
        pivot = row_of(x[j], j)
        reciprocal = 1.0 / pivot
        root = lax.rsqrt(pivot)
        here = sub == j
        xj = x[j]
        for k in range(SUBS):
            if k == j:
                continue
            b = row_of(x[k], j)
            if k < j:
                t[k] = jnp.where(here, root * b, t[k])
            b = b * reciprocal
            x[k] = jnp.where(here, b, x[k] - xj * b)
        t[j] = jnp.where(here, root, t[j])
        x[j] = jnp.where(here, reciprocal, -xj * reciprocal)
    return x, t


def factor_inverse(block):
    steps = LANES // SUBS
    lane = lax.broadcasted_iota(jnp.int32, (SUBS, LANES), 1)
    sub = lax.broadcasted_iota(jnp.int32, (SUBS, LANES), 0)
    a = [block[SUBS * i : SUBS * (i + 1), :] for i in range(steps)]
    e = [jnp.where(lane == sub + SUBS * i, 1.0, 0.0).astype(jnp.float32) for i in range(steps)]
    out = []
    for s in range(steps):
        inv, t = small_inverse([column_of(a[s], SUBS * s + k) for k in range(SUBS)])
        rows_a = [row_of(a[s], k) for k in range(SUBS)]
        rows_e = [row_of(e[s], k) for k in range(SUBS)]
        out.append(combined(t, rows_e))
        if s + 1 < steps:
            scaled_a, scaled_e = combined(inv, rows_a), combined(inv, rows_e)
            scaled_a = [row_of(scaled_a, k) for k in range(SUBS)]
            scaled_e = [row_of(scaled_e, k) for k in range(SUBS)]
            for i in range(s + 1, steps):
                c = [column_of(a[i], SUBS * s + k) for k in range(SUBS)]
                a[i] = a[i] - combined(c, scaled_a)
                e[i] = e[i] - combined(c, scaled_e)
    return jnp.concatenate(out, 0)


def cholesky_inverse_kernel(gram_ref, out_ref, a_ref):
    size = gram_ref.shape[0]
    a_ref[...] = gram_ref[...]
    out_ref[...] = jnp.zeros_like(out_ref)
    for lo in range(0, size, LANES):
        hi = lo + LANES
        inv = factor_inverse(a_ref[lo:hi, lo:hi])
        if lo > 0:
            out_ref[lo:hi, :lo] = dot(inv, out_ref[lo:hi, :lo], ((1,), (0,)))
        out_ref[lo:hi, lo:hi] = inv
        if hi < size:
            right = dot(inv, a_ref[lo:hi, hi:], ((1,), (0,)))
            a_ref[hi:, hi:] = a_ref[hi:, hi:] - dot(right, right, ((0,), (0,)))
            out_ref[hi:, :hi] = out_ref[hi:, :hi] - dot(right, out_ref[lo:hi, :hi], ((0,), (0,)))


def cholesky_inverse(gram):
    size = gram.shape[0]
    return pl.pallas_call(
        cholesky_inverse_kernel,
        out_shape=jax.ShapeDtypeStruct((size, size), jnp.float32),
        in_specs=[pl.BlockSpec(memory_space=pltpu.VMEM)],
        out_specs=pl.BlockSpec(memory_space=pltpu.VMEM),
        scratch_shapes=[pltpu.VMEM((size, size), jnp.float32)],
        compiler_params=pltpu.CompilerParams(vmem_limit_bytes=32 << 20),
        cost_estimate=pl.CostEstimate(
            flops=20_000_000_000, bytes_accessed=8 * size * size, transcendentals=size
        ),
    )(gram)


def pairs_xor(size, mask):
    return [(i, i ^ mask) for i in range(size)]


def gather_col(piece, size):
    even = [piece] + [lax.ppermute(piece, "col", pairs_xor(size, k)) for k in range(2, size, 2)]
    near = jnp.stack(even)
    far = lax.ppermute(near, "col", pairs_xor(size, 1))
    return jnp.stack([near, far], axis=1).reshape((size,) + piece.shape)


def by_position(pieces, size):
    me = lax.axis_index("col")
    return jnp.take(pieces, jnp.arange(size, dtype=jnp.int32) ^ me, axis=0)


def sum_row_small(value, size):
    span = 2
    while span <= size:
        value = value + lax.ppermute(value, "row", pairs_xor(size, span - 1))
        span *= 2
    return value


def sum_row_chain(value, size):
    place = lax.axis_index("row")
    half = size // 2
    for hop in range(half - 1):
        value = value + lax.ppermute(
            value, "row", [(hop, hop + 1), (size - 1 - hop, size - 2 - hop)]
        )
    value = value + lax.ppermute(value, "row", [(half - 1, half), (half, half - 1)])
    for hop in range(half - 1):
        low, high = half - 1 - hop, half + hop
        came = lax.ppermute(value, "row", [(low, low - 1), (high, high + 1)])
        value = jnp.where((place == low - 1) | (place == high + 1), came, value)
    return value


def inverted(mapping, block_count):
    return (
        jnp.zeros((block_count,), jnp.int32)
        .at[mapping]
        .set(jnp.arange(block_count, dtype=jnp.int32))
    )


def per_device(children, block_maps):
    cols = lax.axis_size("col")
    rows = lax.axis_size("row")
    me = lax.axis_index("col")
    rows_dev, width = children.shape[1], children.shape[2]
    blocks_dev = width // PANEL
    block_count = blocks_dev * cols
    part = rows_dev // cols
    inverse = jnp.stack([inverted(block_maps[c], block_count) for c in range(2)])

    outgoing = children.reshape(2, cols, part, width).transpose(1, 0, 2, 3)
    spread = lax.all_to_all(outgoing, "col", 0, 0, tiled=True)
    blocks = spread.reshape(cols, 2, part, blocks_dev, PANEL).transpose(1, 0, 3, 2, 4)
    blocks = blocks.reshape(2, block_count, part, PANEL)
    ordered = jnp.stack([jnp.take(blocks[c], inverse[c], axis=0) for c in range(2)])
    ordered = ordered.reshape(2, cols, blocks_dev, part, PANEL)

    both = 2 * PANEL
    mine = ordered[:, 0].transpose(0, 2, 1, 3).reshape(2 * part, both)
    pieces = gather_col(mine, cols)
    panels = by_position(pieces, cols).reshape(cols * 2 * part, both)

    onward = ordered.transpose(1, 0, 3, 2, 4)
    settled = lax.all_to_all(onward, "col", 0, 0, tiled=True)
    front = settled.reshape(cols * 2 * part, width)

    groups = cols // (both // LANES)
    height = both // groups
    left = lax.dynamic_slice_in_dim(panels, (me % groups) * height, height, axis=1)
    right = lax.dynamic_slice_in_dim(panels, (me // groups) * LANES, LANES, axis=1)
    tile = sum_row_small(dot(left, right, ((0,), (0,))), rows)
    tiles = by_position(gather_col(tile, cols), cols)
    gram = tiles.reshape(both // LANES, groups, height, LANES).transpose(1, 2, 0, 3)
    gram = gram.reshape(both, both)

    inv = cholesky_inverse(gram)
    basis = dot(panels, inv, ((1,), (1,)))

    outs, fronts = [], []
    for b in range(blocks_dev):
        block = front[:, b * PANEL : (b + 1) * PANEL]
        summed = [
            sum_row_chain(dot(panels[:, p * PANEL : (p + 1) * PANEL], block, ((0,), (0,))), rows)
            for p in range(2)
        ]
        upper = dot(inv, jnp.concatenate(summed, axis=0), ((1,), (0,)))
        outs.append(upper)
        fronts.append(block - dot(basis, upper, ((1,), (0,))))
    upper_rows = jnp.concatenate(outs, axis=1)
    result = jnp.concatenate(fronts, axis=1).reshape(cols, 2, part, width)
    result = result.transpose(1, 0, 2, 3).reshape(2, rows_dev, width)
    return (upper_rows, result)


def solution(mesh):
    placed = (P(None, "row", "col"), P())
    return jax.shard_map(
        per_device,
        mesh=mesh,
        in_specs=placed,
        out_specs=(P(None, "col"), P(None, "row", "col")),
        check_vma=False,
    )
```

profile of v0, /device:TPU:10, one launch (start us, length us, event | category | flops | bytes accessed | tf_op | source)
XLA Modules:
  0.0 151.5 jit_solution(11611561307822216656)
XLA Ops:
  0.6 2.3 %copy.53 = f32[2,8,32,512]{3,2,0,1:T(8,128)} copy(f32[2,8,32,512]{3,2,1,0:T(8,128)} %bitcast.92) | data formatting | bytes 2097152 | tf_op jit(solution)/shard_map/reshape | solution.py:170
  2.9 4.4 %all-to-all-start = ((f32[8,2,32,512]{3,2,1,0:T(8,128)}), f32[8,2,32,512]{3,2,1,0:T(8,128)S(1)}, u32[]{:S(2)}, u32[]{:S(2)}) async-start(f32[8,2,32,512]{3,2,1,0:T(8,128)} %bitcast.69), calls=%async_computation | async-start | bytes 2097152 | tf_op jit(solution)/shard_map/all_to_all | solution.py:171
  8.7 12.6 %all-to-all-done = f32[8,2,32,512]{3,2,1,0:T(8,128)S(1)} async-done(((f32[8,2,32,512]{3,2,1,0:T(8,128)}), f32[8,2,32,512]{3,2,1,0:T(8,128)S(1)}, u32[]{:S(2)}, u32[]{:S(2)}) %all-to-all-start) | async-done | bytes 1048608 | tf_op jit(solution)/shard_map/all_to_all | solution.py:171
  24.0 1.6 %collective-permute-start.2 = (f32[64,512]{1,0:T(8,128)S(1)}, f32[64,512]{1,0:T(8,128)S(1)}, u32[]{:S(2)}, u32[]{:S(2)}) collective-permute-start(f32[64,512]{1,0:T(8,128)S(1)} %bitcast.99), channel_id=1, source_target_pairs={{0,6},{1,7},{2,4},{3,5},{4,2},{5,3},{6,0},{7,1},{8,14},{9,15},{10,... | collective-permute-start | bytes 393224 | tf_op jit(solution)/shard_map/ppermute | solution.py:118
  25.6 1.5 collective-permute-start.1
  27.7 3.7 %collective-permute-done.2 = f32[64,512]{1,0:T(8,128)S(1)} collective-permute-done((f32[64,512]{1,0:T(8,128)S(1)}, f32[64,512]{1,0:T(8,128)S(1)}, u32[]{:S(2)}, u32[]{:S(2)}) %collective-permute-start.2) | collective-permute-done | bytes 131104 | tf_op jit(solution)/shard_map/ppermute | solution.py:118
  31.4 1.1 collective-permute-done.1
  33.5 1.1 copy.38
  34.6 4.5 %all-to-all-start.1 = ((f32[8,2,32,2,256]{4,2,3,1,0:T(8,128)}), f32[8,2,32,2,256]{4,2,3,1,0:T(8,128)S(1)}, u32[]{:S(2)}, u32[]{:S(2)}) async-start(f32[8,2,32,2,256]{4,2,3,1,0:T(8,128)} %copy.38), calls=%async_computation.1 | async-start | bytes 2097152 | tf_op jit(solution)/shard_map/all_to_all | solution.py:183
  40.3 1.0 fusion.9
  41.8 5.1 %collective-permute-done.4 = f32[256,128]{1,0:T(8,128)S(1)} collective-permute-done((f32[256,128]{1,0:T(8,128)S(1)}, f32[256,128]{1,0:T(8,128)S(1)}, u32[]{:S(2)}, u32[]{:S(2)}) %collective-permute-start.4) | collective-permute-done | bytes 131104 | tf_op jit(solution)/shard_map/ppermute | solution.py:132
  47.0 1.6 %collective-permute-start.5 = (f32[256,128]{1,0:T(8,128)S(1)}, f32[256,128]{1,0:T(8,128)S(1)}, u32[]{:S(2)}, u32[]{:S(2)}) collective-permute-start(f32[256,128]{1,0:T(8,128)S(1)} %add.93), channel_id=1, source_target_pairs={{0,24},{8,16},{16,8},{24,0},{1,25},{9,17},{17,9},{25,1},{2,26},{10... | collective-permute-start | bytes 393224 | tf_op jit(solution)/shard_map/ppermute | solution.py:132
  48.6 6.0 %collective-permute-done.5 = f32[256,128]{1,0:T(8,128)S(1)} collective-permute-done((f32[256,128]{1,0:T(8,128)S(1)}, f32[256,128]{1,0:T(8,128)S(1)}, u32[]{:S(2)}, u32[]{:S(2)}) %collective-permute-start.5) | collective-permute-done | bytes 131104 | tf_op jit(solution)/shard_map/ppermute | solution.py:132
  54.6 1.6 %collective-permute-start.8 = (f32[256,128]{1,0:T(8,128)S(1)}, f32[256,128]{1,0:T(8,128)}, u32[]{:S(2)}, u32[]{:S(2)}) collective-permute-start(f32[256,128]{1,0:T(8,128)S(1)} %add.94), channel_id=1, source_target_pairs={{0,6},{1,7},{2,4},{3,5},{4,2},{5,3},{6,0},{7,1},{8,14},{9,15},{10,... | collective-permute-start | bytes 393224 | tf_op jit(solution)/shard_map/ppermute | solution.py:118
  56.9 1.3 collective-permute-start.6
  59.0 1.0 fusion.11
  61.1 1.7 %fusion.15 = f32[256,256]{1,0:T(8,128)} fusion(f32[512,512]{1,0:T(8,128)S(1)} %bitcast_select_fusion, f32[512,512]{1,0:T(8,128)S(1)} %bitcast.75), kind=kOutput, calls=%fused_computation.36 | convolution fusion | flops 402653184 | bytes 1310720 | tf_op jit(solution)/shard_map/dot_general | solution.py:14
  62.8 1.3 collective-permute-start.16
  64.0 1.3 collective-permute-start.10
  66.4 1.3 collective-permute-start.13
  67.7 1.3 collective-permute-start.19
  69.0 1.9 %fusion.36 = (f32[4,1,256,128]{3,2,0,1:T(8,128)S(1)}, f32[4,256,128]{2,1,0:T(8,128)}) fusion(f32[1,256,128]{2,1,0:T(8,128)} %bitcast.25, f32[1,256,128]{2,1,0:T(8,128)} %bitcast.24, f32[1,256,128]{2,1,0:T(8,128)} %bitcast.23, f32[1,256,128]{2,1,0:T(8,128)S(1)} %bitcast.94), kind=kLoop, calls=%fused_computation.77 | loop fusion | flops 393216 | bytes 1572864 | tf_op jit(solution)/shard_map/stack | solution.py:121
  70.9 3.3 %collective-permute-done.16 = f32[256,256]{1,0:T(8,128)} collective-permute-done((f32[256,256]{1,0:T(8,128)}, f32[256,256]{1,0:T(8,128)}, u32[]{:S(2)}, u32[]{:S(2)}) %collective-permute-start.16) | collective-permute-done | bytes 262176 | tf_op jit(solution)/shard_map/ppermute | solution.py:141
  74.2 1.8 %add.99 = f32[256,256]{1,0:T(8,128)} add(f32[256,256]{1,0:T(8,128)} %fusion.15, f32[256,256]{1,0:T(8,128)} %collective-permute-done.16) | non-fusion elementwise | flops 65536 | bytes 786432 | tf_op jit(solution)/shard_map/add | solution.py:141
  76.0 3.7 %collective-permute-start.17 = (f32[256,256]{1,0:T(8,128)}, f32[256,256]{1,0:T(8,128)}, u32[]{:S(2)}, u32[]{:S(2)}) collective-permute-start(f32[256,256]{1,0:T(8,128)} %add.99), channel_id=1, source_target_pairs={{8,16},{16,8},{9,17},{17,9},{10,18},{18,10},{11,19},{19,11},{12,20... | collective-permute-start | bytes 786440 | tf_op jit(solution)/shard_map/ppermute | solution.py:144
  79.8 1.7 %add.95 = f32[256,256]{1,0:T(8,128)} add(f32[256,256]{1,0:T(8,128)S(1)} %fusion.17, f32[256,256]{1,0:T(8,128)} %collective-permute-done.10) | non-fusion elementwise | flops 65536 | bytes 786432 | tf_op jit(solution)/shard_map/add | solution.py:141
  81.5 3.7 %collective-permute-start.11 = (f32[256,256]{1,0:T(8,128)}, f32[256,256]{1,0:T(8,128)}, u32[]{:S(2)}, u32[]{:S(2)}) collective-permute-start(f32[256,256]{1,0:T(8,128)} %add.95), channel_id=1, source_target_pairs={{8,16},{16,8},{9,17},{17,9},{10,18},{18,10},{11,19},{19,11},{12,20... | collective-permute-start | bytes 786440 | tf_op jit(solution)/shard_map/ppermute | solution.py:144
  85.4 1.7 %add.97 = f32[256,256]{1,0:T(8,128)} add(f32[256,256]{1,0:T(8,128)S(1)} %fusion.13, f32[256,256]{1,0:T(8,128)} %collective-permute-done.13) | non-fusion elementwise | flops 65536 | bytes 786432 | tf_op jit(solution)/shard_map/add | solution.py:141
  87.1 1.9 %collective-permute-start.14 = (f32[256,256]{1,0:T(8,128)}, f32[256,256]{1,0:T(8,128)}, u32[]{:S(2)}, u32[]{:S(2)}) collective-permute-start(f32[256,256]{1,0:T(8,128)} %add.97), channel_id=1, source_target_pairs={{8,16},{16,8},{9,17},{17,9},{10,18},{18,10},{11,19},{19,11},{12,20... | collective-permute-start | bytes 786440 | tf_op jit(solution)/shard_map/ppermute | solution.py:144
  90.0 3.9 %collective-permute-start.20 = (f32[256,256]{1,0:T(8,128)S(1)}, f32[256,256]{1,0:T(8,128)}, u32[]{:S(2)}, u32[]{:S(2)}) collective-permute-start(f32[256,256]{1,0:T(8,128)S(1)} %add.101), channel_id=1, source_target_pairs={{8,16},{16,8},{9,17},{17,9},{10,18},{18,10},{11,19},{19,11},{12,20... | collective-permute-start | bytes 786440 | tf_op jit(solution)/shard_map/ppermute | solution.py:144
  94.8 2.0 %copy.45 = f32[512,256]{0,1:T(8,128)} copy(f32[512,256]{1,0:T(8,128)} %get-tuple-element.11) | data formatting | bytes 1048576
  97.9 1.8 %add.100 = f32[256,256]{1,0:T(8,128)} add(f32[256,256]{1,0:T(8,128)} %add.99, f32[256,256]{1,0:T(8,128)} %collective-permute-done.17) | non-fusion elementwise | flops 65536 | bytes 786432 | tf_op jit(solution)/shard_map/add | solution.py:144
  99.7 2.0 %collective-permute-start.18 = (f32[256,256]{1,0:T(8,128)}, f32[256,256]{1,0:T(8,128)}, u32[]{:S(2)}, u32[]{:S(2)}) collective-permute-start(f32[256,256]{1,0:T(8,128)} %add.100), channel_id=1, source_target_pairs={{8,0},{16,24},{9,1},{17,25},{10,2},{18,26},{11,3},{19,27},{12,4},{... | collective-permute-start | bytes 786440 | tf_op jit(solution)/shard_map/ppermute | solution.py:147
  101.7 1.8 %add.96 = f32[256,256]{1,0:T(8,128)} add(f32[256,256]{1,0:T(8,128)} %add.95, f32[256,256]{1,0:T(8,128)} %collective-permute-done.11) | non-fusion elementwise | flops 65536 | bytes 786432 | tf_op jit(solution)/shard_map/add | solution.py:144
  103.4 2.0 %collective-permute-start.12 = (f32[256,256]{1,0:T(8,128)}, f32[256,256]{1,0:T(8,128)}, u32[]{:S(2)}, u32[]{:S(2)}) collective-permute-start(f32[256,256]{1,0:T(8,128)} %add.96), channel_id=1, source_target_pairs={{8,0},{16,24},{9,1},{17,25},{10,2},{18,26},{11,3},{19,27},{12,4},{... | collective-permute-start | bytes 786440 | tf_op jit(solution)/shard_map/ppermute | solution.py:147
  105.4 1.8 %add.98 = f32[256,256]{1,0:T(8,128)} add(f32[256,256]{1,0:T(8,128)} %add.97, f32[256,256]{1,0:T(8,128)} %collective-permute-done.14) | non-fusion elementwise | flops 65536 | bytes 786432 | tf_op jit(solution)/shard_map/add | solution.py:144
  107.2 2.0 %collective-permute-start.15 = (f32[256,256]{1,0:T(8,128)}, f32[256,256]{1,0:T(8,128)}, u32[]{:S(2)}, u32[]{:S(2)}) collective-permute-start(f32[256,256]{1,0:T(8,128)} %add.98), channel_id=1, source_target_pairs={{8,0},{16,24},{9,1},{17,25},{10,2},{18,26},{11,3},{19,27},{12,4},{... | collective-permute-start | bytes 786440 | tf_op jit(solution)/shard_map/ppermute | solution.py:147
  109.2 1.7 %add.102 = f32[256,256]{1,0:T(8,128)} add(f32[256,256]{1,0:T(8,128)S(1)} %add.101, f32[256,256]{1,0:T(8,128)} %collective-permute-done.20) | non-fusion elementwise | flops 65536 | bytes 786432 | tf_op jit(solution)/shard_map/add | solution.py:144
  110.9 1.5 collective-permute-start.21
  112.4 1.1 pad_maximum_fusion.2
  115.1 22.2 %shard_map.41 = f32[512,512]{1,0:T(8,128)S(1)} custom-call(f32[512,512]{1,0:T(8,128)S(1)} %bitcast.72), custom_call_target="tpu_custom_call" | custom-call | flops 20000000000 | bytes 2097152 | tf_op jit(solution)/shard_map/pallas_call | solution.py:100
  137.3 1.9 %fusion.40 = f32[512,512]{1,0:T(8,128)S(1)} fusion(f32[512,512]{1,0:T(8,128)S(1)} %bitcast_select_fusion, f32[512,512]{1,0:T(8,128)S(1)} %shard_map.41), kind=kOutput, calls=%fused_computation.81 | convolution fusion | flops 1610612736 | bytes 3145728 | tf_op jit(solution)/shard_map/dot_general | solution.py:14
  142.2 1.1 fusion.5
  144.4 1.1 fusion.1
  146.5 1.1 convolution_subtract_fusion.1
  147.6 1.1 convolution_subtract_fusion
  148.7 1.3 copy.44
  150.4 1.1 copy.43
  (85 shorter events, 21.2 us)
Async XLA Ops:
  2.9 4.4 %copy-start.3 = (s32[2,16]{1,0:T(2,128)S(1)}, s32[2,16]{1,0:T(2,128)}, u32[]{:S(2)}) copy-start(s32[2,16]{1,0:T(2,128)} %param.5) | copy-start | bytes 388
  2.9 18.3 %all-to-all-start = ((f32[8,2,32,512]{3,2,1,0:T(8,128)}), f32[8,2,32,512]{3,2,1,0:T(8,128)S(1)}, u32[]{:S(2)}, u32[]{:S(2)}) async-start(f32[8,2,32,512]{3,2,1,0:T(8,128)} %bitcast.69), calls=%async_computation | async-start | bytes 2097152 | tf_op jit(solution)/shard_map/all_to_all | solution.py:171
  24.0 7.4 %collective-permute-start.2 = (f32[64,512]{1,0:T(8,128)S(1)}, f32[64,512]{1,0:T(8,128)S(1)}, u32[]{:S(2)}, u32[]{:S(2)}) collective-permute-start(f32[64,512]{1,0:T(8,128)S(1)} %bitcast.99), channel_id=1, source_target_pairs={{0,6},{1,7},{2,4},{3,5},{4,2},{5,3},{6,0},{7,1},{8,14},{9,15},{10,... | collective-permute-start | bytes 393224 | tf_op jit(solution)/shard_map/ppermute | solution.py:118
  25.6 6.9 %collective-permute-start.1 = (f32[64,512]{1,0:T(8,128)S(1)}, f32[64,512]{1,0:T(8,128)S(1)}, u32[]{:S(2)}, u32[]{:S(2)}) collective-permute-start(f32[64,512]{1,0:T(8,128)S(1)} %bitcast.100), channel_id=1, source_target_pairs={{0,4},{1,5},{2,6},{3,7},{4,0},{5,1},{6,2},{7,3},{8,12},{9,13},{10,... | collective-permute-start | bytes 393224 | tf_op jit(solution)/shard_map/ppermute | solution.py:118
  27.1 5.4 %collective-permute-start = (f32[64,512]{1,0:T(8,128)S(1)}, f32[64,512]{1,0:T(8,128)S(1)}, u32[]{:S(2)}, u32[]{:S(2)}) collective-permute-start(f32[64,512]{1,0:T(8,128)S(1)} %bitcast.101), channel_id=1, source_target_pairs={{0,2},{1,3},{2,0},{3,1},{4,6},{5,7},{6,4},{7,5},{8,10},{9,11},{10,... | collective-permute-start | bytes 393224 | tf_op jit(solution)/shard_map/ppermute | solution.py:118
  33.4 5.9 %collective-permute-start.3 = (f32[4,64,512]{2,1,0:T(8,128)S(1)}, f32[4,64,512]{2,1,0:T(8,128)S(1)}, u32[]{:S(2)}, u32[]{:S(2)}) collective-permute-start(f32[4,64,512]{2,1,0:T(8,128)S(1)} %get-tuple-element.18), channel_id=1, source_target_pairs={{0,1},{1,0},{2,3},{3,2},{4,5},{5,4},{6,7},{7,6},{8,9},{9,8},{10,11... | collective-permute-start | bytes 1572872 | tf_op jit(solution)/shard_map/ppermute | solution.py:120
  34.6 4.7 %copy-start.2 = (f32[4,1,64,512]{3,2,0,1:T(8,128)S(1)}, f32[4,1,64,512]{3,2,0,1:T(8,128)}, u32[]{:S(2)}) copy-start(f32[4,1,64,512]{3,2,0,1:T(8,128)} %get-tuple-element.17) | copy-start | bytes 1572868
  34.6 23.6 %all-to-all-start.1 = ((f32[8,2,32,2,256]{4,2,3,1,0:T(8,128)}), f32[8,2,32,2,256]{4,2,3,1,0:T(8,128)S(1)}, u32[]{:S(2)}, u32[]{:S(2)}) async-start(f32[8,2,32,2,256]{4,2,3,1,0:T(8,128)} %copy.38), calls=%async_computation.1 | async-start | bytes 2097152 | tf_op jit(solution)/shard_map/all_to_all | solution.py:183
  41.3 5.6 %collective-permute-start.4 = (f32[256,128]{1,0:T(8,128)S(1)}, f32[256,128]{1,0:T(8,128)S(1)}, u32[]{:S(2)}, u32[]{:S(2)}) collective-permute-start(f32[256,128]{1,0:T(8,128)S(1)} %fusion.9), channel_id=1, source_target_pairs={{0,8},{8,0},{16,24},{24,16},{1,9},{9,1},{17,25},{25,17},{2,10},{10... | collective-permute-start | bytes 393224 | tf_op jit(solution)/shard_map/ppermute | solution.py:132
  47.0 7.6 %collective-permute-start.5 = (f32[256,128]{1,0:T(8,128)S(1)}, f32[256,128]{1,0:T(8,128)S(1)}, u32[]{:S(2)}, u32[]{:S(2)}) collective-permute-start(f32[256,128]{1,0:T(8,128)S(1)} %add.93), channel_id=1, source_target_pairs={{0,24},{8,16},{16,8},{24,0},{1,25},{9,17},{17,9},{25,1},{2,26},{10... | collective-permute-start | bytes 393224 | tf_op jit(solution)/shard_map/ppermute | solution.py:132
  54.6 11.8 %collective-permute-start.8 = (f32[256,128]{1,0:T(8,128)S(1)}, f32[256,128]{1,0:T(8,128)}, u32[]{:S(2)}, u32[]{:S(2)}) collective-permute-start(f32[256,128]{1,0:T(8,128)S(1)} %add.94), channel_id=1, source_target_pairs={{0,6},{1,7},{2,4},{3,5},{4,2},{5,3},{6,0},{7,1},{8,14},{9,15},{10,... | collective-permute-start | bytes 393224 | tf_op jit(solution)/shard_map/ppermute | solution.py:118
  56.1 11.5 %collective-permute-start.7 = (f32[256,128]{1,0:T(8,128)S(1)}, f32[256,128]{1,0:T(8,128)}, u32[]{:S(2)}, u32[]{:S(2)}) collective-permute-start(f32[256,128]{1,0:T(8,128)S(1)} %add.94), channel_id=1, source_target_pairs={{0,4},{1,5},{2,6},{3,7},{4,0},{5,1},{6,2},{7,3},{8,12},{9,13},{10,... | collective-permute-start | bytes 393224 | tf_op jit(solution)/shard_map/ppermute | solution.py:118
  56.9 12.1 %collective-permute-start.6 = (f32[256,128]{1,0:T(8,128)S(1)}, f32[256,128]{1,0:T(8,128)}, u32[]{:S(2)}, u32[]{:S(2)}) collective-permute-start(f32[256,128]{1,0:T(8,128)S(1)} %add.94), channel_id=1, source_target_pairs={{0,2},{1,3},{2,0},{3,1},{4,6},{5,7},{6,4},{7,5},{8,10},{9,11},{10,... | collective-permute-start | bytes 393224 | tf_op jit(solution)/shard_map/ppermute | solution.py:118
  62.8 11.4 %collective-permute-start.16 = (f32[256,256]{1,0:T(8,128)}, f32[256,256]{1,0:T(8,128)}, u32[]{:S(2)}, u32[]{:S(2)}) collective-permute-start(f32[256,256]{1,0:T(8,128)} %fusion.15), channel_id=1, source_target_pairs={{0,8},{24,16},{1,9},{25,17},{2,10},{26,18},{3,11},{27,19},{4,12},{... | collective-permute-start | bytes 786440 | tf_op jit(solution)/shard_map/ppermute | solution.py:141
  64.0 15.8 %collective-permute-start.10 = (f32[256,256]{1,0:T(8,128)S(1)}, f32[256,256]{1,0:T(8,128)}, u32[]{:S(2)}, u32[]{:S(2)}) collective-permute-start(f32[256,256]{1,0:T(8,128)S(1)} %fusion.17), channel_id=1, source_target_pairs={{0,8},{24,16},{1,9},{25,17},{2,10},{26,18},{3,11},{27,19},{4,12},{... | collective-permute-start | bytes 786440 | tf_op jit(solution)/shard_map/ppermute | solution.py:141
  66.4 19.1 %collective-permute-start.13 = (f32[256,256]{1,0:T(8,128)S(1)}, f32[256,256]{1,0:T(8,128)}, u32[]{:S(2)}, u32[]{:S(2)}) collective-permute-start(f32[256,256]{1,0:T(8,128)S(1)} %fusion.13), channel_id=1, source_target_pairs={{0,8},{24,16},{1,9},{25,17},{2,10},{26,18},{3,11},{27,19},{4,12},{... | collective-permute-start | bytes 786440 | tf_op jit(solution)/shard_map/ppermute | solution.py:141
  67.7 21.4 %collective-permute-start.19 = (f32[256,256]{1,0:T(8,128)S(1)}, f32[256,256]{1,0:T(8,128)}, u32[]{:S(2)}, u32[]{:S(2)}) collective-permute-start(f32[256,256]{1,0:T(8,128)S(1)} %fusion.11), channel_id=1, source_target_pairs={{0,8},{24,16},{1,9},{25,17},{2,10},{26,18},{3,11},{27,19},{4,12},{... | collective-permute-start | bytes 786440 | tf_op jit(solution)/shard_map/ppermute | solution.py:141
  70.9 41.5 %collective-permute-start.9 = (f32[4,256,128]{2,1,0:T(8,128)}, f32[4,256,128]{2,1,0:T(8,128)}, u32[]{:S(2)}, u32[]{:S(2)}) collective-permute-start(f32[4,256,128]{2,1,0:T(8,128)} %get-tuple-element.16), channel_id=1, source_target_pairs={{0,1},{1,0},{2,3},{3,2},{4,5},{5,4},{6,7},{7,6},{8,9},{9,8},{10,11... | collective-permute-start | bytes 1572872 | tf_op jit(solution)/shard_map/ppermute | solution.py:120
  76.0 21.9 %collective-permute-start.17 = (f32[256,256]{1,0:T(8,128)}, f32[256,256]{1,0:T(8,128)}, u32[]{:S(2)}, u32[]{:S(2)}) collective-permute-start(f32[256,256]{1,0:T(8,128)} %add.99), channel_id=1, source_target_pairs={{8,16},{16,8},{9,17},{17,9},{10,18},{18,10},{11,19},{19,11},{12,20... | collective-permute-start | bytes 786440 | tf_op jit(solution)/shard_map/ppermute | solution.py:144
  81.5 20.1 %collective-permute-start.11 = (f32[256,256]{1,0:T(8,128)}, f32[256,256]{1,0:T(8,128)}, u32[]{:S(2)}, u32[]{:S(2)}) collective-permute-start(f32[256,256]{1,0:T(8,128)} %add.95), channel_id=1, source_target_pairs={{8,16},{16,8},{9,17},{17,9},{10,18},{18,10},{11,19},{19,11},{12,20... | collective-permute-start | bytes 786440 | tf_op jit(solution)/shard_map/ppermute | solution.py:144
  87.1 18.3 %collective-permute-start.14 = (f32[256,256]{1,0:T(8,128)}, f32[256,256]{1,0:T(8,128)}, u32[]{:S(2)}, u32[]{:S(2)}) collective-permute-start(f32[256,256]{1,0:T(8,128)} %add.97), channel_id=1, source_target_pairs={{8,16},{16,8},{9,17},{17,9},{10,18},{18,10},{11,19},{19,11},{12,20... | collective-permute-start | bytes 786440 | tf_op jit(solution)/shard_map/ppermute | solution.py:144
  90.0 19.2 %collective-permute-start.20 = (f32[256,256]{1,0:T(8,128)S(1)}, f32[256,256]{1,0:T(8,128)}, u32[]{:S(2)}, u32[]{:S(2)}) collective-permute-start(f32[256,256]{1,0:T(8,128)S(1)} %add.101), channel_id=1, source_target_pairs={{8,16},{16,8},{9,17},{17,9},{10,18},{18,10},{11,19},{19,11},{12,20... | collective-permute-start | bytes 786440 | tf_op jit(solution)/shard_map/ppermute | solution.py:144
  99.7 39.6 %collective-permute-start.18 = (f32[256,256]{1,0:T(8,128)}, f32[256,256]{1,0:T(8,128)}, u32[]{:S(2)}, u32[]{:S(2)}) collective-permute-start(f32[256,256]{1,0:T(8,128)} %add.100), channel_id=1, source_target_pairs={{8,0},{16,24},{9,1},{17,25},{10,2},{18,26},{11,3},{19,27},{12,4},{... | collective-permute-start | bytes 786440 | tf_op jit(solution)/shard_map/ppermute | solution.py:147
  103.4 36.8 %collective-permute-start.12 = (f32[256,256]{1,0:T(8,128)}, f32[256,256]{1,0:T(8,128)}, u32[]{:S(2)}, u32[]{:S(2)}) collective-permute-start(f32[256,256]{1,0:T(8,128)} %add.96), channel_id=1, source_target_pairs={{8,0},{16,24},{9,1},{17,25},{10,2},{18,26},{11,3},{19,27},{12,4},{... | collective-permute-start | bytes 786440 | tf_op jit(solution)/shard_map/ppermute | solution.py:147
  107.2 36.1 %collective-permute-start.15 = (f32[256,256]{1,0:T(8,128)}, f32[256,256]{1,0:T(8,128)}, u32[]{:S(2)}, u32[]{:S(2)}) collective-permute-start(f32[256,256]{1,0:T(8,128)} %add.98), channel_id=1, source_target_pairs={{8,0},{16,24},{9,1},{17,25},{10,2},{18,26},{11,3},{19,27},{12,4},{... | collective-permute-start | bytes 786440 | tf_op jit(solution)/shard_map/ppermute | solution.py:147
  110.9 30.3 %collective-permute-start.21 = (f32[256,256]{1,0:T(8,128)}, f32[256,256]{1,0:T(8,128)S(1)}, u32[]{:S(2)}, u32[]{:S(2)}) collective-permute-start(f32[256,256]{1,0:T(8,128)} %add.102), channel_id=1, source_target_pairs={{8,0},{16,24},{9,1},{17,25},{10,2},{18,26},{11,3},{19,27},{12,4},{... | collective-permute-start | bytes 786440 | tf_op jit(solution)/shard_map/ppermute | solution.py:147
  145.5 1.0 copy-start
  146.5 1.1 copy-start.1
where the time goes:
time: 153 us; the launch traced here: 152 us
  starting transfers between devices  44.1 us (29%)
  waiting for transfers between devices  32 us (21%)
  Pallas kernels  22.2 us (15%)
  other arithmetic  21.9 us (14%)
  local copies, waits for them, and re-layouts  18.1 us (12%)
  matrix products  12 us (8%)
    pallas_call x1, Pallas kernels, cholesky_inverse(): pl.pallas_call(cholesky_inverse_kernel, out_shape=jax.ShapeDtypeStruct((s...  22.2 us
    ppermute x4, starting transfers between devices, sum_row_chain(): lax.ppermute(value, 'row', [(half - 1, half), (half, half - 1)])  13.3 us
    all_to_all x1, waiting for transfers between devices, per_device(): spread = lax.all_to_all(outgoing, 'col', 0, 0, tiled=True)  12.6 us
    dot_general x10, matrix products, dot(): lax.dot_general(left, right, (contract, ((), ())), precision=lax.Precisio...  12 us
    ppermute x2, waiting for transfers between devices, sum_row_small(): value = value + lax.ppermute(value, 'row', pairs_xor(size, span - 1))  11.1 us
    ppermute x4, starting transfers between devices, sum_row_chain(): came = lax.ppermute(value, 'row', [(low, low - 1), (high, high + 1)])  7.5 us
    ppermute x6, starting transfers between devices, gather_col(): lax.ppermute(piece, 'col', pairs_xor(size, k))  7.11 us
    add x4, other arithmetic, sum_row_chain(): value + lax.ppermute(value, 'row', [(half - 1, half), (half, half - 1)])  6.98 us
  transfers between devices with their start and end apart: 24, of which 8 were waited for; matrix products, arithmetic and copies ran while one was open for 25% of the time, Pallas kernels for 15%

commit v1 on v0

v1 whole, which is shorter than its diff:
```python
import jax
import jax.numpy as jnp
from jax import lax
from jax.experimental import pallas as pl
from jax.experimental.pallas import tpu as pltpu
from jax.sharding import PartitionSpec as P

PANEL = 256
LANES = 128
SUBS = 8
ANY = pl.BlockSpec(memory_space=pl.ANY)
VMEM = pl.BlockSpec(memory_space=pltpu.VMEM)
SMEM = pl.BlockSpec(memory_space=pltpu.SMEM)
KERNEL = pltpu.CompilerParams(vmem_limit_bytes=24 << 20)
F32 = jnp.float32


def dot(left, right, contract):
    return lax.dot_general(
        left,
        right,
        (contract, ((), ())),
        precision=lax.Precision.HIGHEST,
        preferred_element_type=F32,
    )


def shape(*dims):
    return jax.ShapeDtypeStruct(dims, F32)


def cost(flops, size):
    return pl.CostEstimate(flops=flops, bytes_accessed=size, transcendentals=0)


def run_copies(copies):
    for copy in copies:
        copy.start()
    for copy in copies:
        copy.wait()


def pack_kernel(children_ref, out_ref, sems):
    parts, _, part, _ = out_ref.shape
    run_copies(
        [
            pltpu.make_async_copy(
                children_ref.at[:, pl.ds(part * d, part), :], out_ref.at[d], sems.at[d]
            )
            for d in range(parts)
        ]
    )


def pack(children, parts):
    two, rows_dev, width = children.shape
    return pl.pallas_call(
        pack_kernel,
        out_shape=shape(parts, two, rows_dev // parts, width),
        in_specs=[ANY],
        out_specs=ANY,
        scratch_shapes=[pltpu.SemaphoreType.DMA((parts,))],
        compiler_params=KERNEL,
        cost_estimate=cost(0, 8 * children.size),
    )(children)


def order_kernel(maps_ref, spread_ref, out_ref, sems):
    owners, _, _, width = out_ref.shape
    per = width // PANEL
    copies = []
    for child in range(2):
        for block in range(owners * per):
            to = maps_ref[child, block]
            from_lane = (block % per) * PANEL
            to_lane = pl.multiple_of(lax.rem(to, per) * PANEL, PANEL)
            copies.append(
                pltpu.make_async_copy(
                    spread_ref.at[block // per, child, :, pl.ds(from_lane, PANEL)],
                    out_ref.at[lax.div(to, per), child, :, pl.ds(to_lane, PANEL)],
                    sems.at[child, block],
                )
            )
    run_copies(copies)


def order(spread, maps):
    return pl.pallas_call(
        order_kernel,
        out_shape=shape(*spread.shape),
        in_specs=[SMEM, ANY],
        out_specs=ANY,
        scratch_shapes=[pltpu.SemaphoreType.DMA(maps.shape)],
        compiler_params=KERNEL,
        cost_estimate=cost(0, 8 * spread.size),
    )(maps, spread)


def tile_kernel(near_ref, far_ref, panels_ref, tile_ref):
    me = lax.axis_index("col")
    half, part, both = near_ref.shape
    height = tile_ref.shape[0]
    groups = both // height
    for i in range(half):
        for ref, k in ((near_ref, 2 * i), (far_ref, 2 * i + 1)):
            at = pl.multiple_of(lax.bitwise_xor(me, k) * part, part)
            panels_ref[pl.ds(at, part), :] = ref[i]
    if height % LANES == 0:
        left = panels_ref[:, pl.ds(pl.multiple_of(lax.rem(me, groups) * height, height), height)]
    else:
        per = LANES // height
        group = lax.rem(me, groups)
        wide = panels_ref[:, pl.ds(pl.multiple_of(lax.div(group, per) * LANES, LANES), LANES)]
        left = wide[:, :height]
        for step in range(1, per):
            piece = wide[:, step * height : (step + 1) * height]
            left = jnp.where(lax.rem(group, per) == step, piece, left)
    right = panels_ref[:, pl.ds(pl.multiple_of(lax.div(me, groups) * LANES, LANES), LANES)]
    tile_ref[...] = dot(left, right, ((0,), (0,)))


def gram_tile(near, far):
    half, part, both = near.shape
    height = both * both // (2 * half * LANES)
    rows_dev = 2 * half * part
    return pl.pallas_call(
        tile_kernel,
        out_shape=(shape(rows_dev, both), shape(height, LANES)),
        in_specs=[VMEM, VMEM],
        out_specs=(VMEM, VMEM),
        compiler_params=KERNEL,
        cost_estimate=cost(12 * rows_dev * height * LANES, 12 * rows_dev * both),
    )(near, far)


def row_of(x, i):
    return jnp.broadcast_to(x[i : i + 1, :], (SUBS, LANES))


def column_of(x, j):
    return jnp.broadcast_to(x[:, j : j + 1], (SUBS, LANES))


def combined(weights, rows):
    p = [w * r for w, r in zip(weights, rows)]
    return ((p[0] + p[1]) + (p[2] + p[3])) + ((p[4] + p[5]) + (p[6] + p[7]))


def small_inverse(cols):
    sub = lax.broadcasted_iota(jnp.int32, (SUBS, LANES), 0)
    x = list(cols)
    t = [jnp.zeros((SUBS, LANES), F32) for _ in range(SUBS)]
    for j in range(SUBS):
        pivot = row_of(x[j], j)
        reciprocal = 1.0 / pivot
        root = lax.rsqrt(pivot)
        here = sub == j
        xj = x[j]
        for k in range(SUBS):
            if k == j:
                continue
            b = row_of(x[k], j)
            if k < j:
                t[k] = jnp.where(here, root * b, t[k])
            b = b * reciprocal
            x[k] = jnp.where(here, b, x[k] - xj * b)
        t[j] = jnp.where(here, root, t[j])
        x[j] = jnp.where(here, reciprocal, -xj * reciprocal)
    return x, t


def factor_inverse(block):
    steps = LANES // SUBS
    lane = lax.broadcasted_iota(jnp.int32, (SUBS, LANES), 1)
    sub = lax.broadcasted_iota(jnp.int32, (SUBS, LANES), 0)
    a = [block[SUBS * i : SUBS * (i + 1), :] for i in range(steps)]
    e = [jnp.where(lane == sub + SUBS * i, 1.0, 0.0).astype(F32) for i in range(steps)]
    out = []
    for s in range(steps):
        inv, t = small_inverse([column_of(a[s], SUBS * s + k) for k in range(SUBS)])
        rows_a = [row_of(a[s], k) for k in range(SUBS)]
        rows_e = [row_of(e[s], k) for k in range(SUBS)]
        out.append(combined(t, rows_e))
        if s + 1 < steps:
            scaled_a, scaled_e = combined(inv, rows_a), combined(inv, rows_e)
            scaled_a = [row_of(scaled_a, k) for k in range(SUBS)]
            scaled_e = [row_of(scaled_e, k) for k in range(SUBS)]
            for i in range(s + 1, steps):
                c = [column_of(a[i], SUBS * s + k) for k in range(SUBS)]
                a[i] = a[i] - combined(c, scaled_a)
                e[i] = e[i] - combined(c, scaled_e)
    return jnp.concatenate(out, 0)


def eliminate(lo, a_ref, out_ref):
    size, hi = a_ref.shape[0], lo + LANES
    inv = factor_inverse(a_ref[lo:hi, lo:hi])
    if lo > 0:
        out_ref[lo:hi, :lo] = dot(inv, out_ref[lo:hi, :lo], ((1,), (0,)))
    out_ref[lo:hi, lo:hi] = inv
    if hi < size:
        right = dot(inv, a_ref[lo:hi, hi:], ((1,), (0,)))
        a_ref[hi:, hi:] = a_ref[hi:, hi:] - dot(right, right, ((0,), (0,)))
        out_ref[hi:, :hi] = out_ref[hi:, :hi] - dot(right, out_ref[lo:hi, :hi], ((0,), (0,)))


def stage_kernel(index, adds, *refs):
    taken = refs[: 2 + 2 * adds]
    a_ref, out_ref = refs[2 + 2 * adds : 4 + 2 * adds]
    sums = refs[4 + 2 * adds : 4 + 3 * adds]
    landed, sems = refs[4 + 3 * adds :]
    copies = [
        pltpu.make_async_copy(taken[3 + 2 * i], landed.at[i], sems.at[i]) for i in range(adds)
    ]
    for copy in copies:
        copy.start()
    if index == 0:
        me = lax.axis_index("col")
        near_ref, far_ref = taken[:2]
        half, height, _ = near_ref.shape
        groups = a_ref.shape[0] // height
        for i in range(half):
            for ref, k in ((near_ref, 2 * i), (far_ref, 2 * i + 1)):
                at = lax.bitwise_xor(me, k)
                row = pl.multiple_of(lax.rem(at, groups) * height, height)
                lane = pl.multiple_of(lax.div(at, groups) * LANES, LANES)
                a_ref[pl.ds(row, height), pl.ds(lane, LANES)] = ref[i]
        out_ref[...] = jnp.zeros_like(out_ref)
    eliminate(index * LANES, a_ref, out_ref)
    for i, copy in enumerate(copies):
        copy.wait()
        sums[i][...] = taken[2 + 2 * i][...] + landed[i]


def stage(index, size, state, adds):
    flat = [ref for pair in adds for ref in pair]
    chunk = (PANEL, PANEL)
    outs = pl.pallas_call(
        lambda *refs: stage_kernel(index, len(adds), *refs),
        out_shape=[shape(size, size)] * 2 + [shape(*chunk)] * len(adds),
        in_specs=[VMEM, VMEM] + [VMEM, ANY] * len(adds),
        out_specs=[VMEM] * (2 + len(adds)),
        input_output_aliases={0: 0, 1: 1} if index > 0 else {},
        scratch_shapes=[
            pltpu.VMEM((max(len(adds), 1),) + chunk, F32),
            pltpu.SemaphoreType.DMA((max(len(adds), 1),)),
        ],
        compiler_params=KERNEL,
        cost_estimate=cost(6_000_000_000, 8 * size * size),
        name="factor",
    )(*state, *flat)
    return outs[:2], outs[2:]


def finish_kernel(index, inv_ref, basis_ref, front_ref, *refs):
    given = 6 if index > 0 else 4
    chunks = refs[:4]
    upper_ref, trail_ref, m_ref, w_ref, f_ref, sems = refs[given:]
    rows = lax.axis_size("row")
    place = lax.axis_index("row")
    outer = (place == 0) | (place == rows - 1)
    for p in range(2):
        own, came = chunks[2 * p], chunks[2 * p + 1]
        into = m_ref.at[pl.ds(PANEL * p, PANEL), :]

        @pl.when(outer)
        def _():
            pltpu.make_async_copy(came, into, sems.at[p]).start()

        @pl.when(jnp.logical_not(outer))
        def _():
            pltpu.make_async_copy(own, into, sems.at[p]).start()

    for p in range(2):
        into = m_ref.at[pl.ds(PANEL * p, PANEL), :]
        pltpu.make_async_copy(chunks[2 * p], into, sems.at[p]).wait()
    w_ref[...] = dot(inv_ref[...], m_ref[...], ((1,), (0,)))
    columns = pl.ds(PANEL * index, PANEL)
    upper_copy = pltpu.make_async_copy(w_ref, upper_ref.at[:, columns], sems.at[0])
    upper_copy.start()
    product = dot(basis_ref[...], w_ref[...], ((1,), (0,)))
    owners, two, part = front_ref.shape[:3]
    for owner in range(owners):
        for child in range(two):
            at = (owner * two + child) * part
            f_ref[child, owner * part : (owner + 1) * part, :] = (
                front_ref[owner, child, :, PANEL * index : PANEL * (index + 1)]
                - product[at : at + part, :]
            )
    trail_copy = pltpu.make_async_copy(f_ref, trail_ref.at[:, :, columns], sems.at[1])
    trail_copy.start()
    upper_copy.wait()
    trail_copy.wait()


def finish(index, inv, basis, front, chunks, given):
    owners, two, part, width = front.shape
    both = inv.shape[0]
    outs = (shape(both, width), shape(two, owners * part, width))
    return pl.pallas_call(
        lambda *refs: finish_kernel(index, *refs),
        out_shape=outs,
        in_specs=[VMEM, VMEM, VMEM] + [ANY] * (4 + len(given)),
        out_specs=(ANY, ANY),
        input_output_aliases={7: 0, 8: 1} if given else {},
        scratch_shapes=[
            pltpu.VMEM((both, PANEL), F32),
            pltpu.VMEM((both, PANEL), F32),
            pltpu.VMEM((two, owners * part, PANEL), F32),
            pltpu.SemaphoreType.DMA((2,)),
        ],
        compiler_params=KERNEL,
        cost_estimate=cost(24 * both * both * PANEL, 24 * both * PANEL),
        name="finish",
    )(inv, basis, front, *chunks, *given)


def pairs_xor(size, mask):
    return [(i, i ^ mask) for i in range(size)]


def gather_col(piece, size):
    even = [piece] + [lax.ppermute(piece, "col", pairs_xor(size, k)) for k in range(2, size, 2)]
    near = jnp.stack(even)
    return near, lax.ppermute(near, "col", pairs_xor(size, 1))


def sum_row_small(value, size):
    span = 2
    while span <= size:
        value = value + lax.ppermute(value, "row", pairs_xor(size, span - 1))
        span *= 2
    return value


def inwards(value, size):
    for hop in range(size // 2 - 1):
        came = lax.ppermute(value, "row", [(hop, hop + 1), (size - 1 - hop, size - 2 - hop)])
        if hop == size // 2 - 2:
            return value, came
        value = value + came


def across(value, size):
    half = size // 2
    return value, lax.ppermute(value, "row", [(half - 1, half), (half, half - 1)])


def outwards(value, size):
    half = size // 2
    place = lax.axis_index("row")
    for hop in range(half - 1):
        low, high = half - 1 - hop, half + hop
        came = lax.ppermute(value, "row", [(low, low - 1), (high, high + 1)])
        if hop == half - 2:
            return value, came
        value = jnp.where((place == low - 1) | (place == high + 1), came, value)


def per_device(children, block_maps):
    cols = lax.axis_size("col")
    rows = lax.axis_size("row")
    rows_dev, width = children.shape[1], children.shape[2]
    blocks_dev = width // PANEL
    part = rows_dev // cols
    both = 2 * PANEL

    spread = lax.all_to_all(pack(children, cols), "col", 0, 0, tiled=True)
    ordered = order(spread, block_maps)
    front = lax.all_to_all(ordered, "col", 0, 0, tiled=True)
    near, far = gather_col(ordered[0].reshape(2 * part, both), cols)
    panels, tile = gram_tile(near, far)
    state = gather_col(sum_row_small(tile, rows), cols)

    flat = front.reshape(cols * 2 * part, width)
    sums = []
    for b in range(blocks_dev):
        for p in range(2):
            left = panels[:, p * PANEL : (p + 1) * PANEL]
            right = flat[:, b * PANEL : (b + 1) * PANEL]
            sums.append(inwards(dot(left, right, ((0,), (0,))), rows))
    state, (one,) = stage(0, both, state, [sums[0]])
    one = across(one, rows)
    state, (two,) = stage(1, both, state, [sums[1]])
    two = across(two, rows)
    state, (three, one) = stage(2, both, state, [sums[2], one])
    one, three = outwards(one, rows), across(three, rows)
    state, (four, two) = stage(3, both, state, [sums[3], two])
    two, four = outwards(two, rows), across(four, rows)
    inv = state[1]
    basis = dot(panels, inv, ((1,), (1,)))
    three = outwards(three[0] + three[1], rows)
    four = outwards(four[0] + four[1], rows)
    outs = finish(0, inv, basis, front, (*one, *two), ())
    return finish(1, inv, basis, front, (*three, *four), outs)


def solution(mesh):
    placed = (P(None, "row", "col"), P())
    return jax.shard_map(
        per_device,
        mesh=mesh,
        in_specs=placed,
        out_specs=(P(None, "col"), P(None, "row", "col")),
        check_vma=False,
    )
```

time: 153 us -> 135 us (0.88)
  the two profiles are of different devices: /device:TPU:10 before, /device:TPU:0 now
where the time goes in v1:
time: 135 us
  waiting for transfers between devices  37.3 us (28%)
  Pallas kernels  34.8 us (26%)
  starting transfers between devices  33 us (24%)
  blocking collectives  20.3 us (15%)
  matrix products  5.88 us (4%)
  local copies, waits for them, and re-layouts  2.14 us (2%)
    pallas_call x4, Pallas kernels, stage(): pl.pallas_call(lambda *refs: stage_kernel(index, len(adds), *refs), out_s...  22.9 us
    ppermute x4, waiting for transfers between devices, outwards(): came = lax.ppermute(value, 'row', [(low, low - 1), (high, high + 1)])  22.7 us
    all_to_all x1, blocking collectives, per_device(): spread = lax.all_to_all(pack(children, cols), 'col', 0, 0, tiled=True)  20.3 us
    ppermute x4, starting transfers between devices, inwards(): lax.ppermute(value, 'row', [(hop, hop + 1), (size - 1 - hop, size - 2 - h...  8.63 us
    pallas_call x2, Pallas kernels, finish(): pl.pallas_call(lambda *refs: finish_kernel(index, *refs), out_shape=outs,...  8.6 us
    ppermute x2, waiting for transfers between devices, sum_row_small(): value = value + lax.ppermute(value, 'row', pairs_xor(size, span - 1))  7.2 us
    ppermute x6, starting transfers between devices, gather_col(): lax.ppermute(piece, 'col', pairs_xor(size, k))  7.11 us
    dot_general x5, matrix products, dot(): lax.dot_general(left, right, (contract, ((), ())), precision=lax.Precisio...  5.88 us
  transfers between devices with their start and end apart: 23, of which 12 were waited for; matrix products, arithmetic and copies ran while one was open for 4% of the time, Pallas kernels for 17%

profile of v1, /device:TPU:0, one launch (start us, length us, event | category | flops | bytes accessed | tf_op | source)
XLA Modules:
  0.0 134.8 jit_solution(9781344346627734480)
XLA Ops:
  0.6 1.2 copy-done
  1.9 0.7 shard_map.41
  2.6 20.3 %all_to_all.10.spread_ref = f32[8,2,32,512]{3,2,1,0:T(8,128)S(1)} all-to-all(f32[8,2,32,512]{3,2,1,0:T(8,128)S(1)} %shard_map.41), channel_id=1, replica_groups=mesh['row'=4,'col'=8] {'col'}, dimensions={0} | all-to-all | bytes 2097152 | tf_op jit(solution)/shard_map/all_to_all | solution.py:368
  22.9 1.8 %shard_map.42 = f32[8,2,32,512]{3,2,1,0:T(8,128)} custom-call(s32[2,16]{1,0:T(2,128)S(1)} %copy-done.1, f32[8,2,32,512]{3,2,1,0:T(8,128)S(1)} %all_to_all.10.spread_ref), custom_call_target="tpu_custom_call" | custom-call | bytes 2097152 | tf_op jit(solution)/shard_map/pallas_call | solution.py:88
  24.7 0.9 slice.24
  25.7 0.6 collective-permute-start
  26.9 2.4 %collective-permute-start.2 = (f32[64,512]{1,0:T(8,128)S(1)}, f32[64,512]{1,0:T(8,128)S(1)}, u32[]{:S(2)}, u32[]{:S(2)}) collective-permute-start(f32[64,512]{1,0:T(8,128)S(1)} %bitcast.19), channel_id=1, source_target_pairs={{0,6},{1,7},{2,4},{3,5},{4,2},{5,3},{6,0},{7,1},{8,14},{9,15},{10,... | collective-permute-start | bytes 393224 | tf_op jit(solution)/shard_map/ppermute | solution.py:323
  29.2 3.6 %all-to-all-start.1 = ((f32[8,2,32,512]{3,2,1,0:T(8,128)}), f32[8,2,32,512]{3,2,1,0:T(8,128)S(1)}, u32[]{:S(2)}, u32[]{:S(2)}) async-start(f32[8,2,32,512]{3,2,1,0:T(8,128)} %shard_map.42), calls=%async_computation.1 | async-start | bytes 2097152 | tf_op jit(solution)/shard_map/all_to_all | solution.py:370
  32.8 1.4 %collective-permute-done.1 = f32[64,512]{1,0:T(8,128)S(1)} collective-permute-done((f32[64,512]{1,0:T(8,128)S(1)}, f32[64,512]{1,0:T(8,128)S(1)}, u32[]{:S(2)}, u32[]{:S(2)}) %collective-permute-start.1) | collective-permute-done | bytes 131104 | tf_op jit(solution)/shard_map/ppermute | solution.py:323
  34.3 1.9 %collective-permute-done.3.far_ref = f32[4,64,512]{2,1,0:T(8,128)S(1)} collective-permute-done((f32[4,64,512]{2,1,0:T(8,128)S(1)}, f32[4,64,512]{2,1,0:T(8,128)S(1)}, u32[]{:S(2)}, u32[]{:S(2)}) %collective-permute-start.3) | collective-permute-done | bytes 524320 | tf_op jit(solution)/shard_map/ppermute | solution.py:325
  36.2 0.8 shard_map.43
  37.0 1.6 %collective-permute-start.4 = (f32[256,128]{1,0:T(8,128)S(1)}, f32[256,128]{1,0:T(8,128)S(1)}, u32[]{:S(2)}, u32[]{:S(2)}) collective-permute-start(f32[256,128]{1,0:T(8,128)S(1)} %get-tuple-element.19), channel_id=1, source_target_pairs={{0,8},{8,0},{16,24},{24,16},{1,9},{9,1},{17,25},{25,17},{2,10},{10... | collective-permute-start | bytes 393224 | tf_op jit(solution)/shard_map/ppermute | solution.py:331
  38.6 4.0 %collective-permute-done.4 = f32[256,128]{1,0:T(8,128)S(1)} collective-permute-done((f32[256,128]{1,0:T(8,128)S(1)}, f32[256,128]{1,0:T(8,128)S(1)}, u32[]{:S(2)}, u32[]{:S(2)}) %collective-permute-start.4) | collective-permute-done | bytes 131104 | tf_op jit(solution)/shard_map/ppermute | solution.py:331
  42.6 3.7 %collective-permute-start.5 = (f32[256,128]{1,0:T(8,128)S(1)}, f32[256,128]{1,0:T(8,128)S(1)}, u32[]{:S(2)}, u32[]{:S(2)}) collective-permute-start(f32[256,128]{1,0:T(8,128)S(1)} %add.12), channel_id=1, source_target_pairs={{0,24},{8,16},{16,8},{24,0},{1,25},{9,17},{17,9},{25,1},{2,26},{10... | collective-permute-start | bytes 393224 | tf_op jit(solution)/shard_map/ppermute | solution.py:331
  46.2 3.2 %collective-permute-done.5 = f32[256,128]{1,0:T(8,128)S(1)} collective-permute-done((f32[256,128]{1,0:T(8,128)S(1)}, f32[256,128]{1,0:T(8,128)S(1)}, u32[]{:S(2)}, u32[]{:S(2)}) %collective-permute-start.5) | collective-permute-done | bytes 131104 | tf_op jit(solution)/shard_map/ppermute | solution.py:331
  49.5 1.0 collective-permute-start.6
  50.5 1.2 collective-permute-start.7
  51.7 1.4 %collective-permute-start.8 = (f32[256,128]{1,0:T(8,128)S(1)}, f32[256,128]{1,0:T(8,128)S(1)}, u32[]{:S(2)}, u32[]{:S(2)}) collective-permute-start(f32[256,128]{1,0:T(8,128)S(1)} %add.13), channel_id=1, source_target_pairs={{0,6},{1,7},{2,4},{3,5},{4,2},{5,3},{6,0},{7,1},{8,14},{9,15},{10,... | collective-permute-start | bytes 393224 | tf_op jit(solution)/shard_map/ppermute | solution.py:323
  53.1 1.0 fusion.6.refs_2_
  54.1 1.0 collective-permute-done.6
  55.1 1.0 collective-permute-done.7
  56.0 1.5 %collective-permute-done.8 = f32[256,128]{1,0:T(8,128)S(1)} collective-permute-done((f32[256,128]{1,0:T(8,128)S(1)}, f32[256,128]{1,0:T(8,128)S(1)}, u32[]{:S(2)}, u32[]{:S(2)}) %collective-permute-start.8) | collective-permute-done | bytes 131104 | tf_op jit(solution)/shard_map/ppermute | solution.py:323
  57.6 1.0 fusion.4.refs_2_
  58.6 4.7 %collective-permute-start.10 = (f32[256,256]{1,0:T(8,128)S(1)}, f32[256,256]{1,0:T(8,128)S(1)}, u32[]{:S(2)}, u32[]{:S(2)}) collective-permute-start(f32[256,256]{1,0:T(8,128)S(1)} %fusion.6.refs_2_), channel_id=1, source_target_pairs={{0,8},{24,16},{1,9},{25,17},{2,10},{26,18},{3,11},{27,19},{4,12},{... | collective-permute-start | bytes 786440 | tf_op jit(solution)/shard_map/ppermute | solution.py:338
  63.4 1.0 fusion.2.refs_2_
  64.4 1.3 collective-permute-start.11
  65.7 1.3 collective-permute-start.12
  67.0 1.0 fusion.refs_2_
  68.0 1.3 collective-permute-start.14
  70.0 6.2 %factor.4 = (f32[512,512]{1,0:T(8,128)S(1)}, f32[512,512]{1,0:T(8,128)S(1)}, f32[256,256]{1,0:T(8,128)S(1)}) custom-call(f32[4,256,128]{2,1,0:T(8,128)S(1)} %pad_maximum_fusion.1.refs_0_, f32[4,256,128]{2,1,0:T(8,128)S(1)} %collective-permute-done.9.refs_1_, f32[256,256]{1,0:T(8,128)S(1)} %fusion.6.refs_2_, f32[256,256]{1,0:T(8,128)S(1)} %collective-permute-done.10.refs_3_), custom_call_target="tpu_custom_call" | custom-call | flops 6000000000 | bytes 2097152 | tf_op jit(solution)/shard_map/factor/pallas_call | solution.py:238
  76.2 0.9 collective-permute-start.13
  77.1 5.8 %factor.5 = (f32[512,512]{1,0:T(8,128)S(1)}, f32[512,512]{1,0:T(8,128)S(1)}, f32[256,256]{1,0:T(8,128)S(1)}) custom-call(f32[512,512]{1,0:T(8,128)S(1)} %get-tuple-element.21.refs_0_, f32[512,512]{1,0:T(8,128)S(1)} %get-tuple-element.22.refs_1_, f32[256,256]{1,0:T(8,128)S(1)} %fusion.4.refs_2_, ...), custom_call_target="tpu_custom_call", output_to_operand_aliasing={{0}: (0, {}), {1}: (1, {})} | custom-call | flops 6000000000 | bytes 2097152 | tf_op jit(solution)/shard_map/factor/pallas_call | solution.py:238
  82.9 0.7 collective-permute-start.15
  83.6 5.6 %factor.6 = (f32[512,512]{1,0:T(8,128)S(1)}, f32[512,512]{1,0:T(8,128)S(1)}, f32[256,256]{1,0:T(8,128)S(1)}, f32[256,256]{1,0:T(8,128)S(1)}) custom-call(f32[512,512]{1,0:T(8,128)S(1)} %get-tuple-element.23.refs_0_, f32[512,512]{1,0:T(8,128)S(1)} %get-tuple-element.24.refs_1_, ...), custom_call_target="tpu_custom_call", output_to_operand_aliasing={{0}: (0, {}), {1}: (1, {})} | custom-call | flops 6000000000 | bytes 2097152 | tf_op jit(solution)/shard_map/factor/pallas_call | solution.py:238
  89.3 5.2 %factor.7 = (f32[512,512]{1,0:T(8,128)S(1)}, f32[512,512]{1,0:T(8,128)S(1)}, f32[256,256]{1,0:T(8,128)S(1)}, f32[256,256]{1,0:T(8,128)S(1)}) custom-call(f32[512,512]{1,0:T(8,128)S(1)} %get-tuple-element.26.refs_0_, f32[512,512]{1,0:T(8,128)S(1)} %get-tuple-element.27.refs_1_, ...), custom_call_target="tpu_custom_call", output_to_operand_aliasing={{0}: (0, {}), {1}: (1, {})} | custom-call | flops 6000000000 | bytes 2097152 | tf_op jit(solution)/shard_map/factor/pallas_call | solution.py:238
  94.5 0.7 collective-permute-start.18
  95.2 0.7 collective-permute-start.16
  95.8 1.3 collective-permute-start.21
  97.1 1.3 collective-permute-start.20
  98.5 1.5 %collective-permute-start.19 = (f32[256,256]{1,0:T(8,128)S(1)}, f32[256,256]{1,0:T(8,128)S(1)}, u32[]{:S(2)}, u32[]{:S(2)}) collective-permute-start(f32[256,256]{1,0:T(8,128)S(1)} %add.15.refs_5_), channel_id=1, source_target_pairs={{8,0},{16,24},{9,1},{17,25},{10,2},{18,26},{11,3},{19,27},{12,4},{... | collective-permute-start | bytes 786440 | tf_op jit(solution)/shard_map/ppermute | solution.py:354
  100.1 1.3 collective-permute-start.17
  101.4 1.9 %fusion.12.refs_1_ = f32[512,512]{1,0:T(8,128)S(1)} fusion(f32[512,512]{1,0:T(8,128)S(1)} %get-tuple-element.20, f32[512,512]{1,0:T(8,128)S(1)} %get-tuple-element.29.refs_0_), kind=kOutput, calls=%fused_computation.14 | convolution fusion | flops 1610612736 | bytes 3145728 | tf_op jit(solution)/shard_map/dot_general | solution.py:19
  103.2 13.4 %collective-permute-done.21.refs_6_ = f32[256,256]{1,0:T(8,128)S(1)} collective-permute-done((f32[256,256]{1,0:T(8,128)S(1)}, f32[256,256]{1,0:T(8,128)S(1)}, u32[]{:S(2)}, u32[]{:S(2)}) %collective-permute-start.21) | collective-permute-done | bytes 262176 | tf_op jit(solution)/shard_map/ppermute | solution.py:354
  116.6 5.6 %collective-permute-done.20.refs_4_ = f32[256,256]{1,0:T(8,128)S(1)} collective-permute-done((f32[256,256]{1,0:T(8,128)S(1)}, f32[256,256]{1,0:T(8,128)S(1)}, u32[]{:S(2)}, u32[]{:S(2)}) %collective-permute-start.20) | collective-permute-done | bytes 262176 | tf_op jit(solution)/shard_map/ppermute | solution.py:354
  122.2 4.3 %finish.2 = (f32[512,512]{1,0:T(8,128)}, f32[2,256,512]{2,1,0:T(8,128)}) custom-call(f32[512,512]{1,0:T(8,128)S(1)} %get-tuple-element.29.refs_0_, f32[512,512]{1,0:T(8,128)S(1)} %fusion.12.refs_1_, f32[8,2,32,512]{3,2,1,0:T(8,128)S(1)} %all-to-all-done.1.refs_2_, f32[256,256]{1,0:T(8,128)S(1)} %get-tuple-element.32.refs_3_, ...), custom_call_target="tpu_custom_call" | custom-call | flops 1610612736 | bytes 3145728 | tf_op jit(solution)/shard_map/finish/pallas_call | solution.py:300
  126.5 0.9 collective-permute-done.19.refs_6_
  127.5 2.8 %collective-permute-done.17.refs_4_ = f32[256,256]{1,0:T(8,128)S(1)} collective-permute-done((f32[256,256]{1,0:T(8,128)S(1)}, f32[256,256]{1,0:T(8,128)S(1)}, u32[]{:S(2)}, u32[]{:S(2)}) %collective-permute-start.17) | collective-permute-done | bytes 262176 | tf_op jit(solution)/shard_map/ppermute | solution.py:354
  130.3 4.3 %finish.3 = (f32[512,512]{1,0:T(8,128)}, f32[2,256,512]{2,1,0:T(8,128)}) custom-call(f32[512,512]{1,0:T(8,128)S(1)} %get-tuple-element.29.refs_0_, f32[512,512]{1,0:T(8,128)S(1)} %fusion.12.refs_1_, f32[8,2,32,512]{3,2,1,0:T(8,128)S(1)} %all-to-all-done.1.refs_2_, f32[256,256]{1,0:T(8,128)S(1)} %add.14.refs_3_, ...), custom_call_target="tpu_custom_call", output_to_operand_aliasing={{0}: (7, {}), {1}: (8, {})} | custom-call | flops 1610612736 | bytes 3145728 | tf_op jit(solution)/shard_map/finish/pallas_call | solution.py:300
  (24 shorter events, 1.5 us)
Async XLA Ops:
  0.6 1.2 copy-start
  2.6 20.3 %copy-start.1 = (s32[2,16]{1,0:T(2,128)S(1)}, s32[2,16]{1,0:T(2,128)}, u32[]{:S(2)}) copy-start(s32[2,16]{1,0:T(2,128)} %maps_ref.1) | copy-start | bytes 388
  25.7 7.1 %collective-permute-start = (f32[64,512]{1,0:T(8,128)S(1)}, f32[64,512]{1,0:T(8,128)S(1)}, u32[]{:S(2)}, u32[]{:S(2)}) collective-permute-start(f32[64,512]{1,0:T(8,128)S(1)} %bitcast.17), channel_id=1, source_target_pairs={{0,2},{1,3},{2,0},{3,1},{4,6},{5,7},{6,4},{7,5},{8,10},{9,11},{10,... | collective-permute-start | bytes 393224 | tf_op jit(solution)/shard_map/ppermute | solution.py:323
  26.3 7.9 %collective-permute-start.1 = (f32[64,512]{1,0:T(8,128)S(1)}, f32[64,512]{1,0:T(8,128)S(1)}, u32[]{:S(2)}, u32[]{:S(2)}) collective-permute-start(f32[64,512]{1,0:T(8,128)S(1)} %bitcast.18), channel_id=1, source_target_pairs={{0,4},{1,5},{2,6},{3,7},{4,0},{5,1},{6,2},{7,3},{8,12},{9,13},{10,... | collective-permute-start | bytes 393224 | tf_op jit(solution)/shard_map/ppermute | solution.py:323
  26.9 7.3 %collective-permute-start.2 = (f32[64,512]{1,0:T(8,128)S(1)}, f32[64,512]{1,0:T(8,128)S(1)}, u32[]{:S(2)}, u32[]{:S(2)}) collective-permute-start(f32[64,512]{1,0:T(8,128)S(1)} %bitcast.19), channel_id=1, source_target_pairs={{0,6},{1,7},{2,4},{3,5},{4,2},{5,3},{6,0},{7,1},{8,14},{9,15},{10,... | collective-permute-start | bytes 393224 | tf_op jit(solution)/shard_map/ppermute | solution.py:323
  29.2 23.8 %all-to-all-start.1 = ((f32[8,2,32,512]{3,2,1,0:T(8,128)}), f32[8,2,32,512]{3,2,1,0:T(8,128)S(1)}, u32[]{:S(2)}, u32[]{:S(2)}) async-start(f32[8,2,32,512]{3,2,1,0:T(8,128)} %shard_map.42), calls=%async_computation.1 | async-start | bytes 2097152 | tf_op jit(solution)/shard_map/all_to_all | solution.py:370
  34.2 2.0 %collective-permute-start.3 = (f32[4,64,512]{2,1,0:T(8,128)S(1)}, f32[4,64,512]{2,1,0:T(8,128)S(1)}, u32[]{:S(2)}, u32[]{:S(2)}) collective-permute-start(f32[4,64,512]{2,1,0:T(8,128)S(1)} %pad_maximum_fusion.near_ref), channel_id=1, source_target_pairs={{0,1},{1,0},{2,3},{3,2},{4,5},{5,4},{6,7},{7,6},{8,9},{9,8},{10,11... | collective-permute-start | bytes 1572872 | tf_op jit(solution)/shard_map/ppermute | solution.py:325
  37.0 5.6 %collective-permute-start.4 = (f32[256,128]{1,0:T(8,128)S(1)}, f32[256,128]{1,0:T(8,128)S(1)}, u32[]{:S(2)}, u32[]{:S(2)}) collective-permute-start(f32[256,128]{1,0:T(8,128)S(1)} %get-tuple-element.19), channel_id=1, source_target_pairs={{0,8},{8,0},{16,24},{24,16},{1,9},{9,1},{17,25},{25,17},{2,10},{10... | collective-permute-start | bytes 393224 | tf_op jit(solution)/shard_map/ppermute | solution.py:331
  42.6 6.9 %collective-permute-start.5 = (f32[256,128]{1,0:T(8,128)S(1)}, f32[256,128]{1,0:T(8,128)S(1)}, u32[]{:S(2)}, u32[]{:S(2)}) collective-permute-start(f32[256,128]{1,0:T(8,128)S(1)} %add.12), channel_id=1, source_target_pairs={{0,24},{8,16},{16,8},{24,0},{1,25},{9,17},{17,9},{25,1},{2,26},{10... | collective-permute-start | bytes 393224 | tf_op jit(solution)/shard_map/ppermute | solution.py:331
  49.5 5.6 %collective-permute-start.6 = (f32[256,128]{1,0:T(8,128)S(1)}, f32[256,128]{1,0:T(8,128)S(1)}, u32[]{:S(2)}, u32[]{:S(2)}) collective-permute-start(f32[256,128]{1,0:T(8,128)S(1)} %add.13), channel_id=1, source_target_pairs={{0,2},{1,3},{2,0},{3,1},{4,6},{5,7},{6,4},{7,5},{8,10},{9,11},{10,... | collective-permute-start | bytes 393224 | tf_op jit(solution)/shard_map/ppermute | solution.py:323
  50.5 5.6 %collective-permute-start.7 = (f32[256,128]{1,0:T(8,128)S(1)}, f32[256,128]{1,0:T(8,128)S(1)}, u32[]{:S(2)}, u32[]{:S(2)}) collective-permute-start(f32[256,128]{1,0:T(8,128)S(1)} %add.13), channel_id=1, source_target_pairs={{0,4},{1,5},{2,6},{3,7},{4,0},{5,1},{6,2},{7,3},{8,12},{9,13},{10,... | collective-permute-start | bytes 393224 | tf_op jit(solution)/shard_map/ppermute | solution.py:323
  51.7 5.9 %collective-permute-start.8 = (f32[256,128]{1,0:T(8,128)S(1)}, f32[256,128]{1,0:T(8,128)S(1)}, u32[]{:S(2)}, u32[]{:S(2)}) collective-permute-start(f32[256,128]{1,0:T(8,128)S(1)} %add.13), channel_id=1, source_target_pairs={{0,6},{1,7},{2,4},{3,5},{4,2},{5,3},{6,0},{7,1},{8,14},{9,15},{10,... | collective-permute-start | bytes 393224 | tf_op jit(solution)/shard_map/ppermute | solution.py:323
  57.6 12.4 %collective-permute-start.9 = (f32[4,256,128]{2,1,0:T(8,128)S(1)}, f32[4,256,128]{2,1,0:T(8,128)S(1)}, u32[]{:S(2)}, u32[]{:S(2)}) collective-permute-start(f32[4,256,128]{2,1,0:T(8,128)S(1)} %pad_maximum_fusion.1.refs_0_), channel_id=1, source_target_pairs={{0,1},{1,0},{2,3},{3,2},{4,5},{5,4},{6,7},{7,6},{8,9},{9,8},{10,11... | collective-permute-start | bytes 1572872 | tf_op jit(solution)/shard_map/ppermute | solution.py:325
  58.6 11.3 %collective-permute-start.10 = (f32[256,256]{1,0:T(8,128)S(1)}, f32[256,256]{1,0:T(8,128)S(1)}, u32[]{:S(2)}, u32[]{:S(2)}) collective-permute-start(f32[256,256]{1,0:T(8,128)S(1)} %fusion.6.refs_2_), channel_id=1, source_target_pairs={{0,8},{24,16},{1,9},{25,17},{2,10},{26,18},{3,11},{27,19},{4,12},{... | collective-permute-start | bytes 786440 | tf_op jit(solution)/shard_map/ppermute | solution.py:338
  64.4 12.7 %collective-permute-start.11 = (f32[256,256]{1,0:T(8,128)S(1)}, f32[256,256]{1,0:T(8,128)S(1)}, u32[]{:S(2)}, u32[]{:S(2)}) collective-permute-start(f32[256,256]{1,0:T(8,128)S(1)} %fusion.4.refs_2_), channel_id=1, source_target_pairs={{0,8},{24,16},{1,9},{25,17},{2,10},{26,18},{3,11},{27,19},{4,12},{... | collective-permute-start | bytes 786440 | tf_op jit(solution)/shard_map/ppermute | solution.py:338
  65.7 17.9 %collective-permute-start.12 = (f32[256,256]{1,0:T(8,128)S(1)}, f32[256,256]{1,0:T(8,128)S(1)}, u32[]{:S(2)}, u32[]{:S(2)}) collective-permute-start(f32[256,256]{1,0:T(8,128)S(1)} %fusion.2.refs_2_), channel_id=1, source_target_pairs={{0,8},{24,16},{1,9},{25,17},{2,10},{26,18},{3,11},{27,19},{4,12},{... | collective-permute-start | bytes 786440 | tf_op jit(solution)/shard_map/ppermute | solution.py:338
  68.0 21.2 %collective-permute-start.14 = (f32[256,256]{1,0:T(8,128)S(1)}, f32[256,256]{1,0:T(8,128)S(1)}, u32[]{:S(2)}, u32[]{:S(2)}) collective-permute-start(f32[256,256]{1,0:T(8,128)S(1)} %fusion.refs_2_), channel_id=1, source_target_pairs={{0,8},{24,16},{1,9},{25,17},{2,10},{26,18},{3,11},{27,19},{4,12},{... | collective-permute-start | bytes 786440 | tf_op jit(solution)/shard_map/ppermute | solution.py:338
  76.2 7.4 %collective-permute-start.13 = (f32[256,256]{1,0:T(8,128)S(1)}, f32[256,256]{1,0:T(8,128)S(1)}, u32[]{:S(2)}, u32[]{:S(2)}) collective-permute-start(f32[256,256]{1,0:T(8,128)S(1)} %get-tuple-element.25.refs_4_), channel_id=1, source_target_pairs={{8,16},{16,8},{9,17},{17,9},{10,18},{18,10},{11,19},{19,11},{12,20... | collective-permute-start | bytes 786440 | tf_op jit(solution)/shard_map/ppermute | solution.py:346
  82.9 6.4 %collective-permute-start.15 = (f32[256,256]{1,0:T(8,128)S(1)}, f32[256,256]{1,0:T(8,128)S(1)}, u32[]{:S(2)}, u32[]{:S(2)}) collective-permute-start(f32[256,256]{1,0:T(8,128)S(1)} %get-tuple-element.28.refs_4_), channel_id=1, source_target_pairs={{8,16},{16,8},{9,17},{17,9},{10,18},{18,10},{11,19},{19,11},{12,20... | collective-permute-start | bytes 786440 | tf_op jit(solution)/shard_map/ppermute | solution.py:346
  94.5 4.0 %collective-permute-start.18 = (f32[256,256]{1,0:T(8,128)S(1)}, f32[256,256]{1,0:T(8,128)S(1)}, u32[]{:S(2)}, u32[]{:S(2)}) collective-permute-start(f32[256,256]{1,0:T(8,128)S(1)} %get-tuple-element.31), channel_id=1, source_target_pairs={{8,16},{16,8},{9,17},{17,9},{10,18},{18,10},{11,19},{19,11},{12,20... | collective-permute-start | bytes 786440 | tf_op jit(solution)/shard_map/ppermute | solution.py:346
  95.2 4.9 %collective-permute-start.16 = (f32[256,256]{1,0:T(8,128)S(1)}, f32[256,256]{1,0:T(8,128)S(1)}, u32[]{:S(2)}, u32[]{:S(2)}) collective-permute-start(f32[256,256]{1,0:T(8,128)S(1)} %get-tuple-element.30), channel_id=1, source_target_pairs={{8,16},{16,8},{9,17},{17,9},{10,18},{18,10},{11,19},{19,11},{12,20... | collective-permute-start | bytes 786440 | tf_op jit(solution)/shard_map/ppermute | solution.py:346
  95.8 20.8 %collective-permute-start.21 = (f32[256,256]{1,0:T(8,128)S(1)}, f32[256,256]{1,0:T(8,128)S(1)}, u32[]{:S(2)}, u32[]{:S(2)}) collective-permute-start(f32[256,256]{1,0:T(8,128)S(1)} %get-tuple-element.33.refs_5_), channel_id=1, source_target_pairs={{8,0},{16,24},{9,1},{17,25},{10,2},{18,26},{11,3},{19,27},{12,4},{... | collective-permute-start | bytes 786440 | tf_op jit(solution)/shard_map/ppermute | solution.py:354
  97.1 25.1 %collective-permute-start.20 = (f32[256,256]{1,0:T(8,128)S(1)}, f32[256,256]{1,0:T(8,128)S(1)}, u32[]{:S(2)}, u32[]{:S(2)}) collective-permute-start(f32[256,256]{1,0:T(8,128)S(1)} %get-tuple-element.32.refs_3_), channel_id=1, source_target_pairs={{8,0},{16,24},{9,1},{17,25},{10,2},{18,26},{11,3},{19,27},{12,4},{... | collective-permute-start | bytes 786440 | tf_op jit(solution)/shard_map/ppermute | solution.py:354
  98.5 29.0 %collective-permute-start.19 = (f32[256,256]{1,0:T(8,128)S(1)}, f32[256,256]{1,0:T(8,128)S(1)}, u32[]{:S(2)}, u32[]{:S(2)}) collective-permute-start(f32[256,256]{1,0:T(8,128)S(1)} %add.15.refs_5_), channel_id=1, source_target_pairs={{8,0},{16,24},{9,1},{17,25},{10,2},{18,26},{11,3},{19,27},{12,4},{... | collective-permute-start | bytes 786440 | tf_op jit(solution)/shard_map/ppermute | solution.py:354
  100.1 30.2 %collective-permute-start.17 = (f32[256,256]{1,0:T(8,128)S(1)}, f32[256,256]{1,0:T(8,128)S(1)}, u32[]{:S(2)}, u32[]{:S(2)}) collective-permute-start(f32[256,256]{1,0:T(8,128)S(1)} %add.14.refs_3_), channel_id=1, source_target_pairs={{8,0},{16,24},{9,1},{17,25},{10,2},{18,26},{11,3},{19,27},{12,4},{... | collective-permute-start | bytes 786440 | tf_op jit(solution)/shard_map/ppermute | solution.py:354

commit v2 on v1

--- a/solution.py
+++ b/solution.py
@@ -65,8 +65,8 @@
     )(children)
 
 
-def order_kernel(maps_ref, spread_ref, out_ref, sems):
-    owners, _, _, width = out_ref.shape
+def order_kernel(maps_ref, spread_ref, out_ref, mine_ref, sems, mine_sems):
+    owners, _, part, width = out_ref.shape
     per = width // PANEL
     copies = []
     for child in range(2):
@@ -74,25 +74,44 @@
             to = maps_ref[child, block]
             from_lane = (block % per) * PANEL
             to_lane = pl.multiple_of(lax.rem(to, per) * PANEL, PANEL)
+            source = spread_ref.at[block // per, child, :, pl.ds(from_lane, PANEL)]
             copies.append(
                 pltpu.make_async_copy(
-                    spread_ref.at[block // per, child, :, pl.ds(from_lane, PANEL)],
+                    source,
                     out_ref.at[lax.div(to, per), child, :, pl.ds(to_lane, PANEL)],
                     sems.at[child, block],
                 )
             )
+
+            @pl.when(to < 2)
+            def _():
+                pltpu.make_async_copy(
+                    source,
+                    mine_ref.at[pl.ds(child * part, part), pl.ds(to_lane, PANEL)],
+                    mine_sems.at[child, to],
+                ).start()
+
     run_copies(copies)
+    for child in range(2):
+        for panel in range(2):
+            piece = mine_ref.at[pl.ds(child * part, part), pl.ds(panel * PANEL, PANEL)]
+            pltpu.make_async_copy(piece, piece, mine_sems.at[child, panel]).wait()
 
 
 def order(spread, maps):
+    part, width = spread.shape[2:]
     return pl.pallas_call(
         order_kernel,
-        out_shape=shape(*spread.shape),
+        out_shape=(shape(*spread.shape), shape(2 * part, 2 * PANEL)),
         in_specs=[SMEM, ANY],
-        out_specs=ANY,
-        scratch_shapes=[pltpu.SemaphoreType.DMA(maps.shape)],
+        out_specs=(ANY, ANY),
+        scratch_shapes=[
+            pltpu.SemaphoreType.DMA(maps.shape),
+            pltpu.SemaphoreType.DMA((2, 2)),
+        ],
         compiler_params=KERNEL,
         cost_estimate=cost(0, 8 * spread.size),
+        name="order",
     )(maps, spread)
 
 
@@ -169,18 +188,19 @@
     return x, t
 
 
-def factor_inverse(block):
+def eliminate(index, a_ref, out_ref):
+    size = a_ref.shape[0]
+    lo = index // 2 * LANES
+    hi = lo + LANES
     steps = LANES // SUBS
-    lane = lax.broadcasted_iota(jnp.int32, (SUBS, LANES), 1)
-    sub = lax.broadcasted_iota(jnp.int32, (SUBS, LANES), 0)
-    a = [block[SUBS * i : SUBS * (i + 1), :] for i in range(steps)]
-    e = [jnp.where(lane == sub + SUBS * i, 1.0, 0.0).astype(F32) for i in range(steps)]
-    out = []
-    for s in range(steps):
+    first = index % 2 * (steps // 2)
+    a = {i: a_ref[lo + SUBS * i : lo + SUBS * (i + 1), lo:hi] for i in range(first, steps)}
+    e = {i: out_ref[lo + SUBS * i : lo + SUBS * (i + 1), lo:hi] for i in range(first, steps)}
+    for s in range(first, first + steps // 2):
         inv, t = small_inverse([column_of(a[s], SUBS * s + k) for k in range(SUBS)])
         rows_a = [row_of(a[s], k) for k in range(SUBS)]
         rows_e = [row_of(e[s], k) for k in range(SUBS)]
-        out.append(combined(t, rows_e))
+        out_ref[lo + SUBS * s : lo + SUBS * (s + 1), lo:hi] = combined(t, rows_e)
         if s + 1 < steps:
             scaled_a, scaled_e = combined(inv, rows_a), combined(inv, rows_e)
             scaled_a = [row_of(scaled_a, k) for k in range(SUBS)]
@@ -189,26 +209,26 @@
                 c = [column_of(a[i], SUBS * s + k) for k in range(SUBS)]
                 a[i] = a[i] - combined(c, scaled_a)
                 e[i] = e[i] - combined(c, scaled_e)
-    return jnp.concatenate(out, 0)
-
-
-def eliminate(lo, a_ref, out_ref):
-    size, hi = a_ref.shape[0], lo + LANES
-    inv = factor_inverse(a_ref[lo:hi, lo:hi])
+    if first == 0:
+        for i in range(steps // 2, steps):
+            a_ref[lo + SUBS * i : lo + SUBS * (i + 1), lo:hi] = a[i]
+            out_ref[lo + SUBS * i : lo + SUBS * (i + 1), lo:hi] = e[i]
+        return
+    inv = out_ref[lo:hi, lo:hi]
     if lo > 0:
         out_ref[lo:hi, :lo] = dot(inv, out_ref[lo:hi, :lo], ((1,), (0,)))
-    out_ref[lo:hi, lo:hi] = inv
     if hi < size:
         right = dot(inv, a_ref[lo:hi, hi:], ((1,), (0,)))
         a_ref[hi:, hi:] = a_ref[hi:, hi:] - dot(right, right, ((0,), (0,)))
         out_ref[hi:, :hi] = out_ref[hi:, :hi] - dot(right, out_ref[lo:hi, :hi], ((0,), (0,)))
 
 
-def stage_kernel(index, adds, *refs):
+def stage_kernel(index, adds, extras, *refs):
     taken = refs[: 2 + 2 * adds]
-    a_ref, out_ref = refs[2 + 2 * adds : 4 + 2 * adds]
-    sums = refs[4 + 2 * adds : 4 + 3 * adds]
-    landed, sems = refs[4 + 3 * adds :]
+    results = refs[2 + 2 * adds + extras :]
+    a_ref, out_ref = results[:2]
+    sums = results[2 : 2 + adds]
+    landed, sems = results[2 + adds :]
     copies = [
         pltpu.make_async_copy(taken[3 + 2 * i], landed.at[i], sems.at[i]) for i in range(adds)
     ]
@@ -218,27 +238,30 @@
         me = lax.axis_index("col")
         near_ref, far_ref = taken[:2]
         half, height, _ = near_ref.shape
-        groups = a_ref.shape[0] // height
+        size = a_ref.shape[0]
+        groups = size // height
         for i in range(half):
             for ref, k in ((near_ref, 2 * i), (far_ref, 2 * i + 1)):
                 at = lax.bitwise_xor(me, k)
                 row = pl.multiple_of(lax.rem(at, groups) * height, height)
                 lane = pl.multiple_of(lax.div(at, groups) * LANES, LANES)
                 a_ref[pl.ds(row, height), pl.ds(lane, LANES)] = ref[i]
-        out_ref[...] = jnp.zeros_like(out_ref)
-    eliminate(index * LANES, a_ref, out_ref)
+        down = lax.broadcasted_iota(jnp.int32, (size, size), 0)
+        along = lax.broadcasted_iota(jnp.int32, (size, size), 1)
+        out_ref[...] = jnp.where(down == along, 1.0, 0.0).astype(F32)
+    eliminate(index, a_ref, out_ref)
     for i, copy in enumerate(copies):
         copy.wait()
         sums[i][...] = taken[2 + 2 * i][...] + landed[i]
 
 
-def stage(index, size, state, adds):
+def stage(index, size, state, adds=(), extras=()):
     flat = [ref for pair in adds for ref in pair]
     chunk = (PANEL, PANEL)
     outs = pl.pallas_call(
-        lambda *refs: stage_kernel(index, len(adds), *refs),
+        lambda *refs: stage_kernel(index, len(adds), len(extras), *refs),
         out_shape=[shape(size, size)] * 2 + [shape(*chunk)] * len(adds),
-        in_specs=[VMEM, VMEM] + [VMEM, ANY] * len(adds),
+        in_specs=[VMEM, VMEM] + [VMEM, ANY] * len(adds) + [ANY] * len(extras),
         out_specs=[VMEM] * (2 + len(adds)),
         input_output_aliases={0: 0, 1: 1} if index > 0 else {},
         scratch_shapes=[
@@ -246,9 +269,9 @@
             pltpu.SemaphoreType.DMA((max(len(adds), 1),)),
         ],
         compiler_params=KERNEL,
-        cost_estimate=cost(6_000_000_000, 8 * size * size),
+        cost_estimate=cost(3_000_000_000, 4 * size * size),
         name="factor",
-    )(*state, *flat)
+    )(*state, *flat, *extras)
     return outs[:2], outs[2:]
 
 
@@ -366,9 +389,9 @@
     both = 2 * PANEL
 
     spread = lax.all_to_all(pack(children, cols), "col", 0, 0, tiled=True)
-    ordered = order(spread, block_maps)
+    ordered, mine = order(spread, block_maps)
     front = lax.all_to_all(ordered, "col", 0, 0, tiled=True)
-    near, far = gather_col(ordered[0].reshape(2 * part, both), cols)
+    near, far = gather_col(mine, cols)
     panels, tile = gram_tile(near, far)
     state = gather_col(sum_row_small(tile, rows), cols)
 
@@ -383,14 +406,18 @@
     one = across(one, rows)
     state, (two,) = stage(1, both, state, [sums[1]])
     two = across(two, rows)
-    state, (three, one) = stage(2, both, state, [sums[2], one])
+    state, _ = stage(2, both, state)
+    state, (three, one) = stage(3, both, state, [sums[2], one])
     one, three = outwards(one, rows), across(three, rows)
-    state, (four, two) = stage(3, both, state, [sums[3], two])
+    state, (four, two) = stage(4, both, state, [sums[3], two])
     two, four = outwards(two, rows), across(four, rows)
+    state, _ = stage(5, both, state)
+    state, (three,) = stage(6, both, state, [three], [one[1]])
+    three = outwards(three, rows)
+    state, (four,) = stage(7, both, state, [four], [two[1]])
+    four = outwards(four, rows)
     inv = state[1]
     basis = dot(panels, inv, ((1,), (1,)))
-    three = outwards(three[0] + three[1], rows)
-    four = outwards(four[0] + four[1], rows)
     outs = finish(0, inv, basis, front, (*one, *two), ())
     return finish(1, inv, basis, front, (*three, *four), outs)
 

time: 135 us -> 126 us (0.933)
  waiting for transfers between devices: 37.3 us -> 31.6 us
  Pallas kernels: 34.8 us -> 31.8 us
    ppermute x4, waiting for transfers between devices: 22.7 us -> 14.3 us  [outwards(): came = lax.ppermute(value, 'row', [(low, low - 1), (high, high + 1)])]
    pallas_call x5 -> x9, Pallas kernels: 24.7 us -> 21.7 us  [the longest x8 19.5 us: stage(): pl.pallas_call(lambda *refs: stage_kernel(index, len(adds), len(extras),...]
    ppermute x4, waiting for transfers between devices: 0.63 us -> 3.46 us  [inwards(): lax.ppermute(value, 'row', [(hop, hop + 1), (size - 1 - hop, size - 2 - h...]
  transfers between devices with their start and end apart: 23 -> 23, of which waited for: 12 -> 13; matrix products, arithmetic and copies ran while one was open for 4% -> 5% of each run, Pallas kernels for 17% -> 18%
where the time goes in v2:
time: 126 us; the launch traced here: 125 us
  starting transfers between devices  33.1 us (26%)
  Pallas kernels  31.8 us (25%)
  waiting for transfers between devices  31.6 us (25%)
  blocking collectives  20.3 us (16%)
  matrix products  5.87 us (5%)
    all_to_all x1, blocking collectives, per_device(): spread = lax.all_to_all(pack(children, cols), 'col', 0, 0, tiled=True)  20.3 us
    pallas_call x8, Pallas kernels, stage(): pl.pallas_call(lambda *refs: stage_kernel(index, len(adds), len(extras),...  19.5 us
    ppermute x4, waiting for transfers between devices, outwards(): came = lax.ppermute(value, 'row', [(low, low - 1), (high, high + 1)])  14.3 us
    ppermute x4, starting transfers between devices, inwards(): lax.ppermute(value, 'row', [(hop, hop + 1), (size - 1 - hop, size - 2 - h...  8.66 us
    pallas_call x2, Pallas kernels, finish(): pl.pallas_call(lambda *refs: finish_kernel(index, *refs), out_shape=outs,...  8.62 us
    ppermute x2, waiting for transfers between devices, sum_row_small(): value = value + lax.ppermute(value, 'row', pairs_xor(size, span - 1))  7.17 us
    ppermute x6, starting transfers between devices, gather_col(): lax.ppermute(piece, 'col', pairs_xor(size, k))  7.11 us
    dot_general x5, matrix products, dot(): lax.dot_general(left, right, (contract, ((), ())), precision=lax.Precisio...  5.87 us
  transfers between devices with their start and end apart: 23, of which 13 were waited for; matrix products, arithmetic and copies ran while one was open for 5% of the time, Pallas kernels for 18%

profile of v2, /device:TPU:0, one launch (start us, length us, event | category | flops | bytes accessed | tf_op | source)
XLA Modules:
  0.0 125.2 jit_solution(13606920570008656189)
XLA Ops:
  0.6 1.2 copy-done
  1.9 0.7 shard_map.41
  2.6 20.3 %all_to_all.10.spread_ref = f32[8,2,32,512]{3,2,1,0:T(8,128)S(1)} all-to-all(f32[8,2,32,512]{3,2,1,0:T(8,128)S(1)} %shard_map.41), channel_id=1, replica_groups=mesh['row'=4,'col'=8] {'col'}, dimensions={0} | all-to-all | bytes 2097152 | tf_op jit(solution)/shard_map/all_to_all | solution.py:391
  22.9 2.2 %order.1 = (f32[8,2,32,512]{3,2,1,0:T(8,128)}, f32[64,512]{1,0:T(8,128)S(1)}) custom-call(s32[2,16]{1,0:T(2,128)S(1)} %copy-done.1, f32[8,2,32,512]{3,2,1,0:T(8,128)S(1)} %all_to_all.10.spread_ref), custom_call_target="tpu_custom_call" | custom-call | bytes 2097152 | tf_op jit(solution)/shard_map/order/pallas_call | solution.py:103
  26.3 2.4 %collective-permute-start.2 = (f32[64,512]{1,0:T(8,128)S(1)}, f32[64,512]{1,0:T(8,128)S(1)}, u32[]{:S(2)}, u32[]{:S(2)}) collective-permute-start(f32[64,512]{1,0:T(8,128)S(1)} %get-tuple-element.31), channel_id=1, source_target_pairs={{0,6},{1,7},{2,4},{3,5},{4,2},{5,3},{6,0},{7,1},{8,14},{9,15},{10,... | collective-permute-start | bytes 393224 | tf_op jit(solution)/shard_map/ppermute | solution.py:346
  28.7 3.6 %all-to-all-start.1 = ((f32[8,2,32,512]{3,2,1,0:T(8,128)}), f32[8,2,32,512]{3,2,1,0:T(8,128)S(1)}, u32[]{:S(2)}, u32[]{:S(2)}) async-start(f32[8,2,32,512]{3,2,1,0:T(8,128)} %get-tuple-element.34), calls=%async_computation.1 | async-start | bytes 2097152 | tf_op jit(solution)/shard_map/all_to_all | solution.py:393
  32.3 1.4 %collective-permute-done.1 = f32[64,512]{1,0:T(8,128)S(1)} collective-permute-done((f32[64,512]{1,0:T(8,128)S(1)}, f32[64,512]{1,0:T(8,128)S(1)}, u32[]{:S(2)}, u32[]{:S(2)}) %collective-permute-start.1) | collective-permute-done | bytes 131104 | tf_op jit(solution)/shard_map/ppermute | solution.py:346
  33.7 1.9 %collective-permute-done.3.far_ref = f32[4,64,512]{2,1,0:T(8,128)S(1)} collective-permute-done((f32[4,64,512]{2,1,0:T(8,128)S(1)}, f32[4,64,512]{2,1,0:T(8,128)S(1)}, u32[]{:S(2)}, u32[]{:S(2)}) %collective-permute-start.3) | collective-permute-done | bytes 524320 | tf_op jit(solution)/shard_map/ppermute | solution.py:348
  35.6 0.8 shard_map.42
  36.4 1.6 %collective-permute-start.4 = (f32[256,128]{1,0:T(8,128)S(1)}, f32[256,128]{1,0:T(8,128)S(1)}, u32[]{:S(2)}, u32[]{:S(2)}) collective-permute-start(f32[256,128]{1,0:T(8,128)S(1)} %get-tuple-element.32), channel_id=1, source_target_pairs={{0,8},{8,0},{16,24},{24,16},{1,9},{9,1},{17,25},{25,17},{2,10},{10... | collective-permute-start | bytes 393224 | tf_op jit(solution)/shard_map/ppermute | solution.py:354
  38.1 4.0 %collective-permute-done.4 = f32[256,128]{1,0:T(8,128)S(1)} collective-permute-done((f32[256,128]{1,0:T(8,128)S(1)}, f32[256,128]{1,0:T(8,128)S(1)}, u32[]{:S(2)}, u32[]{:S(2)}) %collective-permute-start.4) | collective-permute-done | bytes 131104 | tf_op jit(solution)/shard_map/ppermute | solution.py:354
  42.1 3.7 %collective-permute-start.5 = (f32[256,128]{1,0:T(8,128)S(1)}, f32[256,128]{1,0:T(8,128)S(1)}, u32[]{:S(2)}, u32[]{:S(2)}) collective-permute-start(f32[256,128]{1,0:T(8,128)S(1)} %add.6), channel_id=1, source_target_pairs={{0,24},{8,16},{16,8},{24,0},{1,25},{9,17},{17,9},{25,1},{2,26},{10... | collective-permute-start | bytes 393224 | tf_op jit(solution)/shard_map/ppermute | solution.py:354
  45.7 3.2 %collective-permute-done.5 = f32[256,128]{1,0:T(8,128)S(1)} collective-permute-done((f32[256,128]{1,0:T(8,128)S(1)}, f32[256,128]{1,0:T(8,128)S(1)}, u32[]{:S(2)}, u32[]{:S(2)}) %collective-permute-start.5) | collective-permute-done | bytes 131104 | tf_op jit(solution)/shard_map/ppermute | solution.py:354
  49.0 1.0 collective-permute-start.6
  49.9 1.2 collective-permute-start.7
  51.1 1.4 %collective-permute-start.8 = (f32[256,128]{1,0:T(8,128)S(1)}, f32[256,128]{1,0:T(8,128)S(1)}, u32[]{:S(2)}, u32[]{:S(2)}) collective-permute-start(f32[256,128]{1,0:T(8,128)S(1)} %add.7), channel_id=1, source_target_pairs={{0,6},{1,7},{2,4},{3,5},{4,2},{5,3},{6,0},{7,1},{8,14},{9,15},{10,... | collective-permute-start | bytes 393224 | tf_op jit(solution)/shard_map/ppermute | solution.py:346
  52.5 1.0 fusion.6.refs_2_
  53.5 1.0 collective-permute-done.6
  54.5 1.0 collective-permute-done.7
  55.5 1.5 %collective-permute-done.8 = f32[256,128]{1,0:T(8,128)S(1)} collective-permute-done((f32[256,128]{1,0:T(8,128)S(1)}, f32[256,128]{1,0:T(8,128)S(1)}, u32[]{:S(2)}, u32[]{:S(2)}) %collective-permute-start.8) | collective-permute-done | bytes 131104 | tf_op jit(solution)/shard_map/ppermute | solution.py:346
  57.1 1.0 fusion.4.refs_2_
  58.1 4.7 %collective-permute-start.10 = (f32[256,256]{1,0:T(8,128)S(1)}, f32[256,256]{1,0:T(8,128)S(1)}, u32[]{:S(2)}, u32[]{:S(2)}) collective-permute-start(f32[256,256]{1,0:T(8,128)S(1)} %fusion.6.refs_2_), channel_id=1, source_target_pairs={{0,8},{24,16},{1,9},{25,17},{2,10},{26,18},{3,11},{27,19},{4,12},{... | collective-permute-start | bytes 786440 | tf_op jit(solution)/shard_map/ppermute | solution.py:361
  62.9 1.0 fusion.2.refs_2_
  63.9 1.3 %collective-permute-start.11 = (f32[256,256]{1,0:T(8,128)S(1)}, f32[256,256]{1,0:T(8,128)S(1)}, u32[]{:S(2)}, u32[]{:S(2)}) collective-permute-start(f32[256,256]{1,0:T(8,128)S(1)} %fusion.4.refs_2_), channel_id=1, source_target_pairs={{0,8},{24,16},{1,9},{25,17},{2,10},{26,18},{3,11},{27,19},{4,12},{... | collective-permute-start | bytes 786440 | tf_op jit(solution)/shard_map/ppermute | solution.py:361
  65.2 1.3 %collective-permute-start.12 = (f32[256,256]{1,0:T(8,128)S(1)}, f32[256,256]{1,0:T(8,128)S(1)}, u32[]{:S(2)}, u32[]{:S(2)}) collective-permute-start(f32[256,256]{1,0:T(8,128)S(1)} %fusion.2.refs_2_), channel_id=1, source_target_pairs={{0,8},{24,16},{1,9},{25,17},{2,10},{26,18},{3,11},{27,19},{4,12},{... | collective-permute-start | bytes 786440 | tf_op jit(solution)/shard_map/ppermute | solution.py:361
  66.5 1.0 fusion.refs_2_
  67.5 1.3 %collective-permute-start.14 = (f32[256,256]{1,0:T(8,128)S(1)}, f32[256,256]{1,0:T(8,128)S(1)}, u32[]{:S(2)}, u32[]{:S(2)}) collective-permute-start(f32[256,256]{1,0:T(8,128)S(1)} %fusion.refs_2_), channel_id=1, source_target_pairs={{0,8},{24,16},{1,9},{25,17},{2,10},{26,18},{3,11},{27,19},{4,12},{... | collective-permute-start | bytes 786440 | tf_op jit(solution)/shard_map/ppermute | solution.py:361
  69.5 2.1 %factor.8 = (f32[512,512]{1,0:T(8,128)S(1)}, f32[512,512]{1,0:T(8,128)S(1)}, f32[256,256]{1,0:T(8,128)S(1)}) custom-call(f32[4,256,128]{2,1,0:T(8,128)S(1)} %pad_maximum_fusion.1.refs_0_, f32[4,256,128]{2,1,0:T(8,128)S(1)} %collective-permute-done.9.refs_1_, f32[256,256]{1,0:T(8,128)S(1)} %fusion.6.refs_2_, f32[256,256]{1,0:T(8,128)S(1)} %collective-permute-done.10.refs_3_), custom_call_target="tpu_custom_call" | custom-call | flops 3000000000 | bytes 1048576 | tf_op jit(solution)/shard_map/factor/pallas_call | solution.py:261
  72.2 2.8 %collective-permute-done.11.refs_3_ = f32[256,256]{1,0:T(8,128)S(1)} collective-permute-done((f32[256,256]{1,0:T(8,128)S(1)}, f32[256,256]{1,0:T(8,128)S(1)}, u32[]{:S(2)}, u32[]{:S(2)}) %collective-permute-start.11) | collective-permute-done | bytes 262176 | tf_op jit(solution)/shard_map/ppermute | solution.py:361
  75.1 3.3 %factor.9 = (f32[512,512]{1,0:T(8,128)S(1)}, f32[512,512]{1,0:T(8,128)S(1)}, f32[256,256]{1,0:T(8,128)S(1)}) custom-call(f32[512,512]{1,0:T(8,128)S(1)} %get-tuple-element.35.refs_0_, f32[512,512]{1,0:T(8,128)S(1)} %get-tuple-element.36.refs_1_, f32[256,256]{1,0:T(8,128)S(1)} %fusion.4.refs_2_, ...), custom_call_target="tpu_custom_call", output_to_operand_aliasing={{0}: (0, {}), {1}: (1, {})} | custom-call | flops 3000000000 | bytes 1048576 | tf_op jit(solution)/shard_map/factor/pallas_call | solution.py:261
  78.4 0.9 collective-permute-start.15
  79.2 1.9 %factor.10 = (f32[512,512]{1,0:T(8,128)S(1)}, f32[512,512]{1,0:T(8,128)S(1)}) custom-call(f32[512,512]{1,0:T(8,128)S(1)} %get-tuple-element.37.refs_0_, f32[512,512]{1,0:T(8,128)S(1)} %get-tuple-element.38.refs_1_), custom_call_target="tpu_custom_call", output_to_operand_aliasing={{0}: (0, {}), {1}: (1, {})} | custom-call | flops 3000000000 | bytes 1048576 | tf_op jit(solution)/shard_map/factor/pallas_call | solution.py:261
  81.2 3.1 %factor.11 = (f32[512,512]{1,0:T(8,128)S(1)}, f32[512,512]{1,0:T(8,128)S(1)}, f32[256,256]{1,0:T(8,128)S(1)}, f32[256,256]{1,0:T(8,128)S(1)}) custom-call(f32[512,512]{1,0:T(8,128)S(1)} %get-tuple-element.39.refs_0_, f32[512,512]{1,0:T(8,128)S(1)} %get-tuple-element.40.refs_1_, ...), custom_call_target="tpu_custom_call", output_to_operand_aliasing={{0}: (0, {}), {1}: (1, {})} | custom-call | flops 3000000000 | bytes 1048576 | tf_op jit(solution)/shard_map/factor/pallas_call | solution.py:261
  85.0 1.3 %collective-permute-start.17 = (f32[256,256]{1,0:T(8,128)S(1)}, f32[256,256]{1,0:T(8,128)S(1)}, u32[]{:S(2)}, u32[]{:S(2)}) collective-permute-start(f32[256,256]{1,0:T(8,128)S(1)} %get-tuple-element.50.refs_3_), channel_id=1, source_target_pairs={{8,0},{16,24},{9,1},{17,25},{10,2},{18,26},{11,3},{19,27},{12,4},{... | collective-permute-start | bytes 786440 | tf_op jit(solution)/shard_map/ppermute | solution.py:377
  86.3 2.0 %factor.12 = (f32[512,512]{1,0:T(8,128)S(1)}, f32[512,512]{1,0:T(8,128)S(1)}, f32[256,256]{1,0:T(8,128)S(1)}, f32[256,256]{1,0:T(8,128)S(1)}) custom-call(f32[512,512]{1,0:T(8,128)S(1)} %get-tuple-element.42.refs_0_, f32[512,512]{1,0:T(8,128)S(1)} %get-tuple-element.43.refs_1_, ...), custom_call_target="tpu_custom_call", output_to_operand_aliasing={{0}: (0, {}), {1}: (1, {})} | custom-call | flops 3000000000 | bytes 1048576 | tf_op jit(solution)/shard_map/factor/pallas_call | solution.py:261
  89.0 1.3 %collective-permute-start.19 = (f32[256,256]{1,0:T(8,128)S(1)}, f32[256,256]{1,0:T(8,128)S(1)}, u32[]{:S(2)}, u32[]{:S(2)}) collective-permute-start(f32[256,256]{1,0:T(8,128)S(1)} %get-tuple-element.54.refs_5_), channel_id=1, source_target_pairs={{8,0},{16,24},{9,1},{17,25},{10,2},{18,26},{11,3},{19,27},{12,4},{... | collective-permute-start | bytes 786440 | tf_op jit(solution)/shard_map/ppermute | solution.py:377
  90.3 2.7 %factor.13 = (f32[512,512]{1,0:T(8,128)S(1)}, f32[512,512]{1,0:T(8,128)S(1)}) custom-call(f32[512,512]{1,0:T(8,128)S(1)} %get-tuple-element.45.refs_0_, f32[512,512]{1,0:T(8,128)S(1)} %get-tuple-element.46.refs_1_), custom_call_target="tpu_custom_call", output_to_operand_aliasing={{0}: (0, {}), {1}: (1, {})} | custom-call | flops 3000000000 | bytes 1048576 | tf_op jit(solution)/shard_map/factor/pallas_call | solution.py:261
  93.1 5.4 %collective-permute-done.17.refs_4_ = f32[256,256]{1,0:T(8,128)S(1)} collective-permute-done((f32[256,256]{1,0:T(8,128)S(1)}, f32[256,256]{1,0:T(8,128)S(1)}, u32[]{:S(2)}, u32[]{:S(2)}) %collective-permute-start.17) | collective-permute-done | bytes 262176 | tf_op jit(solution)/shard_map/ppermute | solution.py:377
  98.5 1.9 %factor.14 = (f32[512,512]{1,0:T(8,128)S(1)}, f32[512,512]{1,0:T(8,128)S(1)}, f32[256,256]{1,0:T(8,128)S(1)}) custom-call(f32[512,512]{1,0:T(8,128)S(1)} %get-tuple-element.47.refs_0_, f32[512,512]{1,0:T(8,128)S(1)} %get-tuple-element.48.refs_1_, f32[256,256]{1,0:T(8,128)S(1)} %get-tuple-element.49.refs_2_, ...), custom_call_target="tpu_custom_call", output_to_operand_aliasing={{0}: (0, {}), {1}: (1, {})} | custom-call | flops 3000000000 | bytes 1048576 | tf_op jit(solution)/shard_map/factor/pallas_call | solution.py:261
  100.4 4.3 %collective-permute-done.19.refs_4_.refs_6_ = f32[256,256]{1,0:T(8,128)S(1)} collective-permute-done((f32[256,256]{1,0:T(8,128)S(1)}, f32[256,256]{1,0:T(8,128)S(1)}, u32[]{:S(2)}, u32[]{:S(2)}) %collective-permute-start.19) | collective-permute-done | bytes 262176 | tf_op jit(solution)/shard_map/ppermute | solution.py:377
  104.7 2.4 %factor.15 = (f32[512,512]{1,0:T(8,128)S(1)}, f32[512,512]{1,0:T(8,128)S(1)}, f32[256,256]{1,0:T(8,128)S(1)}) custom-call(f32[512,512]{1,0:T(8,128)S(1)} %get-tuple-element.51.refs_0_, f32[512,512]{1,0:T(8,128)S(1)} %get-tuple-element.52.refs_1_, f32[256,256]{1,0:T(8,128)S(1)} %get-tuple-element.53.refs_2_, ...), custom_call_target="tpu_custom_call", output_to_operand_aliasing={{0}: (0, {}), {1}: (1, {})} | custom-call | flops 3000000000 | bytes 1048576 | tf_op jit(solution)/shard_map/factor/pallas_call | solution.py:261
  107.1 1.3 %collective-permute-start.21 = (f32[256,256]{1,0:T(8,128)S(1)}, f32[256,256]{1,0:T(8,128)S(1)}, u32[]{:S(2)}, u32[]{:S(2)}) collective-permute-start(f32[256,256]{1,0:T(8,128)S(1)} %get-tuple-element.57.refs_5_), channel_id=1, source_target_pairs={{8,0},{16,24},{9,1},{17,25},{10,2},{18,26},{11,3},{19,27},{12,4},{... | collective-permute-start | bytes 786440 | tf_op jit(solution)/shard_map/ppermute | solution.py:377
  108.4 1.5 %collective-permute-start.20 = (f32[256,256]{1,0:T(8,128)S(1)}, f32[256,256]{1,0:T(8,128)S(1)}, u32[]{:S(2)}, u32[]{:S(2)}) collective-permute-start(f32[256,256]{1,0:T(8,128)S(1)} %get-tuple-element.56.refs_3_), channel_id=1, source_target_pairs={{8,0},{16,24},{9,1},{17,25},{10,2},{18,26},{11,3},{19,27},{12,4},{... | collective-permute-start | bytes 786440 | tf_op jit(solution)/shard_map/ppermute | solution.py:377
  110.0 1.9 %fusion.12.refs_1_ = f32[512,512]{1,0:T(8,128)S(1)} fusion(f32[512,512]{1,0:T(8,128)S(1)} %get-tuple-element.33, f32[512,512]{1,0:T(8,128)S(1)} %get-tuple-element.55.refs_0_), kind=kOutput, calls=%fused_computation.14 | convolution fusion | flops 1610612736 | bytes 3145728 | tf_op jit(solution)/shard_map/dot_general | solution.py:19
  111.8 4.3 %finish.2 = (f32[512,512]{1,0:T(8,128)}, f32[2,256,512]{2,1,0:T(8,128)}) custom-call(f32[512,512]{1,0:T(8,128)S(1)} %get-tuple-element.55.refs_0_, f32[512,512]{1,0:T(8,128)S(1)} %fusion.12.refs_1_, f32[8,2,32,512]{3,2,1,0:T(8,128)S(1)} %all-to-all-done.1.refs_2_, f32[256,256]{1,0:T(8,128)S(1)} %get-tuple-element.50.refs_3_, ...), custom_call_target="tpu_custom_call" | custom-call | flops 1610612736 | bytes 3145728 | tf_op jit(solution)/shard_map/finish/pallas_call | solution.py:323
  116.2 1.7 %collective-permute-done.21.refs_6_ = f32[256,256]{1,0:T(8,128)S(1)} collective-permute-done((f32[256,256]{1,0:T(8,128)S(1)}, f32[256,256]{1,0:T(8,128)S(1)}, u32[]{:S(2)}, u32[]{:S(2)}) %collective-permute-start.21) | collective-permute-done | bytes 262176 | tf_op jit(solution)/shard_map/ppermute | solution.py:377
  117.9 2.8 %collective-permute-done.20.refs_4_ = f32[256,256]{1,0:T(8,128)S(1)} collective-permute-done((f32[256,256]{1,0:T(8,128)S(1)}, f32[256,256]{1,0:T(8,128)S(1)}, u32[]{:S(2)}, u32[]{:S(2)}) %collective-permute-start.20) | collective-permute-done | bytes 262176 | tf_op jit(solution)/shard_map/ppermute | solution.py:377
  120.7 4.3 %finish.3 = (f32[512,512]{1,0:T(8,128)}, f32[2,256,512]{2,1,0:T(8,128)}) custom-call(f32[512,512]{1,0:T(8,128)S(1)} %get-tuple-element.55.refs_0_, f32[512,512]{1,0:T(8,128)S(1)} %fusion.12.refs_1_, f32[8,2,32,512]{3,2,1,0:T(8,128)S(1)} %all-to-all-done.1.refs_2_, ...), custom_call_target="tpu_custom_call", output_to_operand_aliasing={{0}: (7, {}), {1}: (8, {})} | custom-call | flops 1610612736 | bytes 3145728 | tf_op jit(solution)/shard_map/finish/pallas_call | solution.py:323
  (25 shorter events, 4.1 us)
Async XLA Ops:
  0.6 1.2 copy-start
  2.6 20.3 %copy-start.1 = (s32[2,16]{1,0:T(2,128)S(1)}, s32[2,16]{1,0:T(2,128)}, u32[]{:S(2)}) copy-start(s32[2,16]{1,0:T(2,128)} %maps_ref.1) | copy-start | bytes 388
  25.1 7.1 %collective-permute-start = (f32[64,512]{1,0:T(8,128)S(1)}, f32[64,512]{1,0:T(8,128)S(1)}, u32[]{:S(2)}, u32[]{:S(2)}) collective-permute-start(f32[64,512]{1,0:T(8,128)S(1)} %get-tuple-element.31), channel_id=1, source_target_pairs={{0,2},{1,3},{2,0},{3,1},{4,6},{5,7},{6,4},{7,5},{8,10},{9,11},{10,... | collective-permute-start | bytes 393224 | tf_op jit(solution)/shard_map/ppermute | solution.py:346
  25.8 7.9 %collective-permute-start.1 = (f32[64,512]{1,0:T(8,128)S(1)}, f32[64,512]{1,0:T(8,128)S(1)}, u32[]{:S(2)}, u32[]{:S(2)}) collective-permute-start(f32[64,512]{1,0:T(8,128)S(1)} %get-tuple-element.31), channel_id=1, source_target_pairs={{0,4},{1,5},{2,6},{3,7},{4,0},{5,1},{6,2},{7,3},{8,12},{9,13},{10,... | collective-permute-start | bytes 393224 | tf_op jit(solution)/shard_map/ppermute | solution.py:346
  26.3 7.3 %collective-permute-start.2 = (f32[64,512]{1,0:T(8,128)S(1)}, f32[64,512]{1,0:T(8,128)S(1)}, u32[]{:S(2)}, u32[]{:S(2)}) collective-permute-start(f32[64,512]{1,0:T(8,128)S(1)} %get-tuple-element.31), channel_id=1, source_target_pairs={{0,6},{1,7},{2,4},{3,5},{4,2},{5,3},{6,0},{7,1},{8,14},{9,15},{10,... | collective-permute-start | bytes 393224 | tf_op jit(solution)/shard_map/ppermute | solution.py:346
  28.7 23.8 %all-to-all-start.1 = ((f32[8,2,32,512]{3,2,1,0:T(8,128)}), f32[8,2,32,512]{3,2,1,0:T(8,128)S(1)}, u32[]{:S(2)}, u32[]{:S(2)}) async-start(f32[8,2,32,512]{3,2,1,0:T(8,128)} %get-tuple-element.34), calls=%async_computation.1 | async-start | bytes 2097152 | tf_op jit(solution)/shard_map/all_to_all | solution.py:393
  33.7 2.0 %collective-permute-start.3 = (f32[4,64,512]{2,1,0:T(8,128)S(1)}, f32[4,64,512]{2,1,0:T(8,128)S(1)}, u32[]{:S(2)}, u32[]{:S(2)}) collective-permute-start(f32[4,64,512]{2,1,0:T(8,128)S(1)} %pad_maximum_fusion.near_ref), channel_id=1, source_target_pairs={{0,1},{1,0},{2,3},{3,2},{4,5},{5,4},{6,7},{7,6},{8,9},{9,8},{10,11... | collective-permute-start | bytes 1572872 | tf_op jit(solution)/shard_map/ppermute | solution.py:348
  36.4 5.6 %collective-permute-start.4 = (f32[256,128]{1,0:T(8,128)S(1)}, f32[256,128]{1,0:T(8,128)S(1)}, u32[]{:S(2)}, u32[]{:S(2)}) collective-permute-start(f32[256,128]{1,0:T(8,128)S(1)} %get-tuple-element.32), channel_id=1, source_target_pairs={{0,8},{8,0},{16,24},{24,16},{1,9},{9,1},{17,25},{25,17},{2,10},{10... | collective-permute-start | bytes 393224 | tf_op jit(solution)/shard_map/ppermute | solution.py:354
  42.1 6.9 %collective-permute-start.5 = (f32[256,128]{1,0:T(8,128)S(1)}, f32[256,128]{1,0:T(8,128)S(1)}, u32[]{:S(2)}, u32[]{:S(2)}) collective-permute-start(f32[256,128]{1,0:T(8,128)S(1)} %add.6), channel_id=1, source_target_pairs={{0,24},{8,16},{16,8},{24,0},{1,25},{9,17},{17,9},{25,1},{2,26},{10... | collective-permute-start | bytes 393224 | tf_op jit(solution)/shard_map/ppermute | solution.py:354
  49.0 5.5 %collective-permute-start.6 = (f32[256,128]{1,0:T(8,128)S(1)}, f32[256,128]{1,0:T(8,128)S(1)}, u32[]{:S(2)}, u32[]{:S(2)}) collective-permute-start(f32[256,128]{1,0:T(8,128)S(1)} %add.7), channel_id=1, source_target_pairs={{0,2},{1,3},{2,0},{3,1},{4,6},{5,7},{6,4},{7,5},{8,10},{9,11},{10,... | collective-permute-start | bytes 393224 | tf_op jit(solution)/shard_map/ppermute | solution.py:346
  49.9 5.6 %collective-permute-start.7 = (f32[256,128]{1,0:T(8,128)S(1)}, f32[256,128]{1,0:T(8,128)S(1)}, u32[]{:S(2)}, u32[]{:S(2)}) collective-permute-start(f32[256,128]{1,0:T(8,128)S(1)} %add.7), channel_id=1, source_target_pairs={{0,4},{1,5},{2,6},{3,7},{4,0},{5,1},{6,2},{7,3},{8,12},{9,13},{10,... | collective-permute-start | bytes 393224 | tf_op jit(solution)/shard_map/ppermute | solution.py:346
  51.1 5.9 %collective-permute-start.8 = (f32[256,128]{1,0:T(8,128)S(1)}, f32[256,128]{1,0:T(8,128)S(1)}, u32[]{:S(2)}, u32[]{:S(2)}) collective-permute-start(f32[256,128]{1,0:T(8,128)S(1)} %add.7), channel_id=1, source_target_pairs={{0,6},{1,7},{2,4},{3,5},{4,2},{5,3},{6,0},{7,1},{8,14},{9,15},{10,... | collective-permute-start | bytes 393224 | tf_op jit(solution)/shard_map/ppermute | solution.py:346
  57.0 12.4 %collective-permute-start.9 = (f32[4,256,128]{2,1,0:T(8,128)S(1)}, f32[4,256,128]{2,1,0:T(8,128)S(1)}, u32[]{:S(2)}, u32[]{:S(2)}) collective-permute-start(f32[4,256,128]{2,1,0:T(8,128)S(1)} %pad_maximum_fusion.1.refs_0_), channel_id=1, source_target_pairs={{0,1},{1,0},{2,3},{3,2},{4,5},{5,4},{6,7},{7,6},{8,9},{9,8},{10,11... | collective-permute-start | bytes 1572872 | tf_op jit(solution)/shard_map/ppermute | solution.py:348
  58.1 11.3 %collective-permute-start.10 = (f32[256,256]{1,0:T(8,128)S(1)}, f32[256,256]{1,0:T(8,128)S(1)}, u32[]{:S(2)}, u32[]{:S(2)}) collective-permute-start(f32[256,256]{1,0:T(8,128)S(1)} %fusion.6.refs_2_), channel_id=1, source_target_pairs={{0,8},{24,16},{1,9},{25,17},{2,10},{26,18},{3,11},{27,19},{4,12},{... | collective-permute-start | bytes 786440 | tf_op jit(solution)/shard_map/ppermute | solution.py:361
  63.9 11.2 %collective-permute-start.11 = (f32[256,256]{1,0:T(8,128)S(1)}, f32[256,256]{1,0:T(8,128)S(1)}, u32[]{:S(2)}, u32[]{:S(2)}) collective-permute-start(f32[256,256]{1,0:T(8,128)S(1)} %fusion.4.refs_2_), channel_id=1, source_target_pairs={{0,8},{24,16},{1,9},{25,17},{2,10},{26,18},{3,11},{27,19},{4,12},{... | collective-permute-start | bytes 786440 | tf_op jit(solution)/shard_map/ppermute | solution.py:361
  65.2 16.0 %collective-permute-start.12 = (f32[256,256]{1,0:T(8,128)S(1)}, f32[256,256]{1,0:T(8,128)S(1)}, u32[]{:S(2)}, u32[]{:S(2)}) collective-permute-start(f32[256,256]{1,0:T(8,128)S(1)} %fusion.2.refs_2_), channel_id=1, source_target_pairs={{0,8},{24,16},{1,9},{25,17},{2,10},{26,18},{3,11},{27,19},{4,12},{... | collective-permute-start | bytes 786440 | tf_op jit(solution)/shard_map/ppermute | solution.py:361
  67.5 18.8 %collective-permute-start.14 = (f32[256,256]{1,0:T(8,128)S(1)}, f32[256,256]{1,0:T(8,128)S(1)}, u32[]{:S(2)}, u32[]{:S(2)}) collective-permute-start(f32[256,256]{1,0:T(8,128)S(1)} %fusion.refs_2_), channel_id=1, source_target_pairs={{0,8},{24,16},{1,9},{25,17},{2,10},{26,18},{3,11},{27,19},{4,12},{... | collective-permute-start | bytes 786440 | tf_op jit(solution)/shard_map/ppermute | solution.py:361
  71.6 9.6 %collective-permute-start.13 = (f32[256,256]{1,0:T(8,128)S(1)}, f32[256,256]{1,0:T(8,128)S(1)}, u32[]{:S(2)}, u32[]{:S(2)}) collective-permute-start(f32[256,256]{1,0:T(8,128)S(1)} %get-tuple-element.41.refs_4_), channel_id=1, source_target_pairs={{8,16},{16,8},{9,17},{17,9},{10,18},{18,10},{11,19},{19,11},{12,20... | collective-permute-start | bytes 786440 | tf_op jit(solution)/shard_map/ppermute | solution.py:369
  78.4 7.9 %collective-permute-start.15 = (f32[256,256]{1,0:T(8,128)S(1)}, f32[256,256]{1,0:T(8,128)S(1)}, u32[]{:S(2)}, u32[]{:S(2)}) collective-permute-start(f32[256,256]{1,0:T(8,128)S(1)} %get-tuple-element.44.refs_4_), channel_id=1, source_target_pairs={{8,16},{16,8},{9,17},{17,9},{10,18},{18,10},{11,19},{19,11},{12,20... | collective-permute-start | bytes 786440 | tf_op jit(solution)/shard_map/ppermute | solution.py:369
  84.3 8.7 %collective-permute-start.16 = (f32[256,256]{1,0:T(8,128)S(1)}, f32[256,256]{1,0:T(8,128)S(1)}, u32[]{:S(2)}, u32[]{:S(2)}) collective-permute-start(f32[256,256]{1,0:T(8,128)S(1)} %get-tuple-element.49.refs_2_), channel_id=1, source_target_pairs={{8,16},{16,8},{9,17},{17,9},{10,18},{18,10},{11,19},{19,11},{12,20... | collective-permute-start | bytes 786440 | tf_op jit(solution)/shard_map/ppermute | solution.py:369
  85.0 13.5 %collective-permute-start.17 = (f32[256,256]{1,0:T(8,128)S(1)}, f32[256,256]{1,0:T(8,128)S(1)}, u32[]{:S(2)}, u32[]{:S(2)}) collective-permute-start(f32[256,256]{1,0:T(8,128)S(1)} %get-tuple-element.50.refs_3_), channel_id=1, source_target_pairs={{8,0},{16,24},{9,1},{17,25},{10,2},{18,26},{11,3},{19,27},{12,4},{... | collective-permute-start | bytes 786440 | tf_op jit(solution)/shard_map/ppermute | solution.py:377
  88.3 12.1 %collective-permute-start.18 = (f32[256,256]{1,0:T(8,128)S(1)}, f32[256,256]{1,0:T(8,128)S(1)}, u32[]{:S(2)}, u32[]{:S(2)}) collective-permute-start(f32[256,256]{1,0:T(8,128)S(1)} %get-tuple-element.53.refs_2_), channel_id=1, source_target_pairs={{8,16},{16,8},{9,17},{17,9},{10,18},{18,10},{11,19},{19,11},{12,20... | collective-permute-start | bytes 786440 | tf_op jit(solution)/shard_map/ppermute | solution.py:369
  89.0 15.7 %collective-permute-start.19 = (f32[256,256]{1,0:T(8,128)S(1)}, f32[256,256]{1,0:T(8,128)S(1)}, u32[]{:S(2)}, u32[]{:S(2)}) collective-permute-start(f32[256,256]{1,0:T(8,128)S(1)} %get-tuple-element.54.refs_5_), channel_id=1, source_target_pairs={{8,0},{16,24},{9,1},{17,25},{10,2},{18,26},{11,3},{19,27},{12,4},{... | collective-permute-start | bytes 786440 | tf_op jit(solution)/shard_map/ppermute | solution.py:377
  107.1 10.7 %collective-permute-start.21 = (f32[256,256]{1,0:T(8,128)S(1)}, f32[256,256]{1,0:T(8,128)S(1)}, u32[]{:S(2)}, u32[]{:S(2)}) collective-permute-start(f32[256,256]{1,0:T(8,128)S(1)} %get-tuple-element.57.refs_5_), channel_id=1, source_target_pairs={{8,0},{16,24},{9,1},{17,25},{10,2},{18,26},{11,3},{19,27},{12,4},{... | collective-permute-start | bytes 786440 | tf_op jit(solution)/shard_map/ppermute | solution.py:377
  108.4 12.3 %collective-permute-start.20 = (f32[256,256]{1,0:T(8,128)S(1)}, f32[256,256]{1,0:T(8,128)S(1)}, u32[]{:S(2)}, u32[]{:S(2)}) collective-permute-start(f32[256,256]{1,0:T(8,128)S(1)} %get-tuple-element.56.refs_3_), channel_id=1, source_target_pairs={{8,0},{16,24},{9,1},{17,25},{10,2},{18,26},{11,3},{19,27},{12,4},{... | collective-permute-start | bytes 786440 | tf_op jit(solution)/shard_map/ppermute | solution.py:377

commit v3 on v2

v3 whole, which is shorter than its diff:
```python
import jax
import jax.numpy as jnp
from jax import lax
from jax.experimental import pallas as pl
from jax.experimental.pallas import tpu as pltpu
from jax.sharding import PartitionSpec as P

PANEL = 256
LANES = 128
SUBS = 8
ANY = pl.BlockSpec(memory_space=pl.ANY)
VMEM = pl.BlockSpec(memory_space=pltpu.VMEM)
SMEM = pl.BlockSpec(memory_space=pltpu.SMEM)
KERNEL = pltpu.CompilerParams(vmem_limit_bytes=24 << 20)
F32 = jnp.float32


def dot(left, right, contract):
    return lax.dot_general(
        left,
        right,
        (contract, ((), ())),
        precision=lax.Precision.HIGHEST,
        preferred_element_type=F32,
    )


def shape(*dims):
    return jax.ShapeDtypeStruct(dims, F32)


def cost(flops, size):
    return pl.CostEstimate(flops=flops, bytes_accessed=size, transcendentals=0)


def run_copies(copies):
    for copy in copies:
        copy.start()
    for copy in copies:
        copy.wait()


def pack_kernel(children_ref, out_ref, sems):
    parts, _, part, _ = out_ref.shape
    run_copies(
        [
            pltpu.make_async_copy(
                children_ref.at[:, pl.ds(part * d, part), :], out_ref.at[d], sems.at[d]
            )
            for d in range(parts)
        ]
    )


def pack(children, parts):
    two, rows_dev, width = children.shape
    return pl.pallas_call(
        pack_kernel,
        out_shape=shape(parts, two, rows_dev // parts, width),
        in_specs=[ANY],
        out_specs=ANY,
        scratch_shapes=[pltpu.SemaphoreType.DMA((parts,))],
        compiler_params=KERNEL,
        cost_estimate=cost(1000, 1000),
    )(children)


def order_kernel(maps_ref, spread_ref, out_ref, mine_ref, sems, mine_sems):
    owners, _, part, width = out_ref.shape
    per = width // PANEL
    copies = []
    for child in range(2):
        for block in range(owners * per):
            to = maps_ref[child, block]
            from_lane = (block % per) * PANEL
            to_lane = pl.multiple_of(lax.rem(to, per) * PANEL, PANEL)
            source = spread_ref.at[block // per, child, :, pl.ds(from_lane, PANEL)]
            copies.append(
                pltpu.make_async_copy(
                    source,
                    out_ref.at[lax.div(to, per), child, :, pl.ds(to_lane, PANEL)],
                    sems.at[child, block],
                )
            )

            @pl.when(to < 2)
            def _():
                pltpu.make_async_copy(
                    source,
                    mine_ref.at[pl.ds(child * part, part), pl.ds(to_lane, PANEL)],
                    mine_sems.at[child, to],
                ).start()

    run_copies(copies)
    for child in range(2):
        for panel in range(2):
            piece = mine_ref.at[pl.ds(child * part, part), pl.ds(panel * PANEL, PANEL)]
            pltpu.make_async_copy(piece, piece, mine_sems.at[child, panel]).wait()


def order(spread, maps):
    part, width = spread.shape[2:]
    return pl.pallas_call(
        order_kernel,
        out_shape=(shape(*spread.shape), shape(2 * part, 2 * PANEL)),
        in_specs=[SMEM, ANY],
        out_specs=(ANY, ANY),
        scratch_shapes=[
            pltpu.SemaphoreType.DMA(maps.shape),
            pltpu.SemaphoreType.DMA((2, 2)),
        ],
        compiler_params=KERNEL,
        cost_estimate=cost(1000, 1000),
        name="order",
    )(maps, spread)


def tile_kernel(near_ref, far_ref, panels_ref, tile_ref):
    me = lax.axis_index("col")
    half, part, both = near_ref.shape
    height = tile_ref.shape[0]
    groups = both // height
    for i in range(half):
        for ref, k in ((near_ref, 2 * i), (far_ref, 2 * i + 1)):
            at = pl.multiple_of(lax.bitwise_xor(me, k) * part, part)
            panels_ref[pl.ds(at, part), :] = ref[i]
    if height % LANES == 0:
        left = panels_ref[:, pl.ds(pl.multiple_of(lax.rem(me, groups) * height, height), height)]
    else:
        per = LANES // height
        group = lax.rem(me, groups)
        wide = panels_ref[:, pl.ds(pl.multiple_of(lax.div(group, per) * LANES, LANES), LANES)]
        left = wide[:, :height]
        for step in range(1, per):
            piece = wide[:, step * height : (step + 1) * height]
            left = jnp.where(lax.rem(group, per) == step, piece, left)
    right = panels_ref[:, pl.ds(pl.multiple_of(lax.div(me, groups) * LANES, LANES), LANES)]
    tile_ref[...] = dot(left, right, ((0,), (0,)))


def gram_tile(near, far):
    half, part, both = near.shape
    height = both * both // (2 * half * LANES)
    rows_dev = 2 * half * part
    return pl.pallas_call(
        tile_kernel,
        out_shape=(shape(rows_dev, both), shape(height, LANES)),
        in_specs=[VMEM, VMEM],
        out_specs=(VMEM, VMEM),
        compiler_params=KERNEL,
        cost_estimate=cost(1000, 1000),
    )(near, far)


def row_of(x, i):
    return jnp.broadcast_to(x[i : i + 1, :], (SUBS, LANES))


def column_of(x, j):
    return jnp.broadcast_to(x[:, j : j + 1], (SUBS, LANES))


def combined(weights, rows):
    p = [w * r for w, r in zip(weights, rows)]
    return ((p[0] + p[1]) + (p[2] + p[3])) + ((p[4] + p[5]) + (p[6] + p[7]))


def small_inverse(cols):
    sub = lax.broadcasted_iota(jnp.int32, (SUBS, LANES), 0)
    x = list(cols)
    t = [jnp.zeros((SUBS, LANES), F32) for _ in range(SUBS)]
    for j in range(SUBS):
        pivot = row_of(x[j], j)
        reciprocal = 1.0 / pivot
        root = lax.rsqrt(pivot)
        here = sub == j
        xj = x[j]
        for k in range(SUBS):
            if k == j:
                continue
            b = row_of(x[k], j)
            if k < j:
                t[k] = jnp.where(here, root * b, t[k])
            b = b * reciprocal
            x[k] = jnp.where(here, b, x[k] - xj * b)
        t[j] = jnp.where(here, root, t[j])
        x[j] = jnp.where(here, reciprocal, -xj * reciprocal)
    return x, t


def factor_inverse(lo, a_ref, out_ref):
    hi = lo + LANES
    steps = LANES // SUBS
    lane = lax.broadcasted_iota(jnp.int32, (SUBS, LANES), 1)
    sub = lax.broadcasted_iota(jnp.int32, (SUBS, LANES), 0)
    z = [a_ref[lo + SUBS * i : lo + SUBS * (i + 1), lo:hi] for i in range(steps)]
    for s in range(steps):
        inv, t = small_inverse([column_of(z[s], SUBS * s + k) for k in range(SUBS)])
        here = (lane >= SUBS * s) & (lane < SUBS * (s + 1))
        own = jnp.where(here, jnp.where(lane == sub + SUBS * s, 1.0, 0.0), z[s])
        rows = [row_of(own, k) for k in range(SUBS)]
        out_ref[lo + SUBS * s : lo + SUBS * (s + 1), lo:hi] = jnp.where(
            lane < SUBS * (s + 1), combined(t, rows), 0.0
        )
        if s + 1 < steps:
            scaled = combined(inv, rows)
            scaled = [row_of(scaled, k) for k in range(SUBS)]
            for i in range(s + 1, steps):
                c = [column_of(z[i], SUBS * s + k) for k in range(SUBS)]
                z[i] = jnp.where(here, 0.0, z[i]) - combined(c, scaled)


def stage_kernel(lo, *refs):
    a_ref, out_ref = refs[-2:]
    size, hi = a_ref.shape[0], lo + LANES
    if lo == 0:
        me = lax.axis_index("col")
        near_ref, far_ref = refs[:2]
        half, height, _ = near_ref.shape
        groups = size // height
        for i in range(half):
            for ref, k in ((near_ref, 2 * i), (far_ref, 2 * i + 1)):
                at = lax.bitwise_xor(me, k)
                row = pl.multiple_of(lax.rem(at, groups) * height, height)
                lane = pl.multiple_of(lax.div(at, groups) * LANES, LANES)
                a_ref[pl.ds(row, height), pl.ds(lane, LANES)] = ref[i]
        out_ref[...] = jnp.zeros_like(out_ref)
    factor_inverse(lo, a_ref, out_ref)
    inv = out_ref[lo:hi, lo:hi]
    if lo > 0:
        out_ref[lo:hi, :lo] = dot(inv, out_ref[lo:hi, :lo], ((1,), (0,)))
    if hi < size:
        right = dot(inv, a_ref[lo:hi, hi:], ((1,), (0,)))
        a_ref[hi:, hi:] = a_ref[hi:, hi:] - dot(right, right, ((0,), (0,)))
        out_ref[hi:, :hi] = out_ref[hi:, :hi] - dot(right, out_ref[lo:hi, :hi], ((0,), (0,)))


def stage(lo, state, after=()):
    size = 2 * PANEL
    return pl.pallas_call(
        lambda *refs: stage_kernel(lo, *refs),
        out_shape=(shape(size, size), shape(size, size)),
        in_specs=[VMEM, VMEM] + [ANY] * len(after),
        out_specs=(VMEM, VMEM),
        input_output_aliases={0: 0, 1: 1} if lo > 0 else {},
        compiler_params=KERNEL,
        cost_estimate=cost(1000, 1000),
        name="stage",
    )(*state, *after)


def stack_kernel(count, *refs):
    for i in range(count):
        refs[-1][i] = refs[i][...]


def stack_after(pieces, after):
    return pl.pallas_call(
        lambda *refs: stack_kernel(len(pieces), *refs),
        out_shape=shape(len(pieces), *pieces[0].shape),
        in_specs=[VMEM] * len(pieces) + [ANY] * len(after),
        out_specs=VMEM,
        compiler_params=KERNEL,
        cost_estimate=cost(1000, 1000),
        name="stack",
    )(*pieces, *after)


def multiply_kernel(panels_ref, front_ref, *refs):
    out_ref, held_ref, sems = refs[-3:]
    count, _, width = out_ref.shape
    step = max(width, PANEL)
    copies = []
    for lane in range(0, count * width, step):
        product = dot(panels_ref[...], front_ref[:, lane : lane + step], ((0,), (0,)))
        for at in range(0, step, width):
            n = (lane + at) // width
            held_ref[n] = product[:, at : at + width]
            copies.append(pltpu.make_async_copy(held_ref.at[n], out_ref.at[n], sems.at[n]))
            copies[-1].start()
    for copy in copies:
        copy.wait()


def multiply(panels, front, count, after):
    both = panels.shape[1]
    part = (count, both, front.shape[1] // count)
    return pl.pallas_call(
        multiply_kernel,
        out_shape=shape(*part),
        in_specs=[VMEM, VMEM] + [ANY] * len(after),
        out_specs=ANY,
        scratch_shapes=[pltpu.VMEM(part, F32), pltpu.SemaphoreType.DMA((count,))],
        compiler_params=KERNEL,
        cost_estimate=cost(1000, 1000),
        name="multiply",
    )(panels, front, *after)


def hold(array, after):
    return pl.pallas_call(
        lambda *refs: None,
        out_shape=shape(*array.shape),
        in_specs=[ANY] * (1 + len(after)),
        out_specs=ANY,
        input_output_aliases={0: 0},
        compiler_params=KERNEL,
        cost_estimate=cost(1000, 1000),
        name="hold",
    )(array, *after)


def total_kernel(parts_ref, out_ref):
    total = parts_ref[0]
    for i in range(1, parts_ref.shape[0]):
        total = total + parts_ref[i]
    out_ref[...] = total


def total_of(parts):
    return pl.pallas_call(
        total_kernel,
        out_shape=shape(*parts.shape[1:]),
        in_specs=[VMEM],
        out_specs=VMEM,
        compiler_params=KERNEL,
        cost_estimate=cost(1000, 1000),
        name="total",
    )(parts)


def finish_kernel(masks, inv_ref, basis_ref, front_ref, *refs):
    upper_ref, trail_ref, m_ref, w_ref, f_ref, sems = refs[-6:]
    owners, two, part, total = front_ref.shape
    width = refs[0].shape[1]
    for n in range(len(masks)):
        m_ref[:, n * width : (n + 1) * width] = refs[n][...]
    w_ref[...] = dot(inv_ref[...], m_ref[...], ((1,), (0,)))
    copies = []
    columns = []
    for n, mask in enumerate(masks):
        if width == total:
            columns.append(pl.ds(0, width))
        else:
            at = lax.bitwise_xor(lax.axis_index("row"), mask) * width
            columns.append(pl.ds(pl.multiple_of(at, LANES), width))
        held = w_ref.at[:, pl.ds(n * width, width)]
        copies.append(pltpu.make_async_copy(held, upper_ref.at[:, columns[n]], sems.at[0, n]))
        copies[-1].start()
    product = dot(basis_ref[...], w_ref[...], ((1,), (0,)))
    for n, mask in enumerate(masks):
        for owner in range(owners):
            for child in range(two):
                row = (owner * two + child) * part
                f_ref[n, child, owner * part : (owner + 1) * part, :] = (
                    front_ref[owner, child, :, columns[n]]
                    - product[row : row + part, n * width : (n + 1) * width]
                )
        copies.append(
            pltpu.make_async_copy(f_ref.at[n], trail_ref.at[:, :, columns[n]], sems.at[1, n])
        )
        copies[-1].start()
    for copy in copies:
        copy.wait()


def finish(pieces, inv, basis, front, given):
    owners, two, part, total = front.shape
    masks = [mask for mask, _ in pieces]
    arrays = [array for _, array in pieces]
    count = len(pieces)
    both, width = arrays[0].shape
    return pl.pallas_call(
        lambda *refs: finish_kernel(masks, *refs),
        out_shape=(shape(both, total), shape(two, owners * part, total)),
        in_specs=[VMEM] * (3 + count) + [ANY] * len(given),
        out_specs=(ANY, ANY),
        input_output_aliases={3 + count: 0, 4 + count: 1} if given else {},
        scratch_shapes=[
            pltpu.VMEM((both, count * width), F32),
            pltpu.VMEM((both, count * width), F32),
            pltpu.VMEM((count, two, owners * part, width), F32),
            pltpu.SemaphoreType.DMA((2, count)),
        ],
        compiler_params=KERNEL,
        cost_estimate=cost(1000, 1000),
        name="finish",
    )(inv, basis, front, *arrays, *given)


def pairs_xor(size, mask):
    return [(i, i ^ mask) for i in range(size)]


def even_pieces(piece, size):
    return [piece] + [lax.ppermute(piece, "col", pairs_xor(size, k)) for k in range(2, size, 2)]


def gather_col(piece, size):
    near = jnp.stack(even_pieces(piece, size))
    return near, lax.ppermute(near, "col", pairs_xor(size, 1))


def sum_row_small(value, size):
    span = 2
    while span <= size:
        value = value + lax.ppermute(value, "row", pairs_xor(size, span - 1))
        span *= 2
    return value


def per_device(children, block_maps):
    cols = lax.axis_size("col")
    rows = lax.axis_size("row")
    rows_dev, width = children.shape[1], children.shape[2]
    blocks_dev = width // PANEL
    part = rows_dev // cols
    both = 2 * PANEL

    spread = lax.all_to_all(pack(children, cols), "col", 0, 0, tiled=True)
    ordered, mine = order(spread, block_maps)
    pieces = even_pieces(mine, cols)
    front = lax.all_to_all(hold(ordered, pieces[1:2]), "col", 0, 0, tiled=True)
    near = stack_after(pieces, [])
    panels, tile = gram_tile(near, lax.ppermute(near, "col", pairs_xor(cols, 1)))
    tile = sum_row_small(tile, rows)
    tiles = even_pieces(tile, cols)

    flat = front.reshape(cols * 2 * part, width)
    products = multiply(panels, flat, rows, [tile])
    parts = lax.all_to_all(products, "row", 0, 0, tiled=True)
    near = stack_after(tiles, [products])
    state = near, lax.ppermute(near, "col", pairs_xor(cols, 1))
    for lo in range(0, both - LANES, LANES):
        state = stage(lo, state)
    mine = total_of(parts)
    _, inv = stage(both - LANES, state, [mine])
    basis = dot(panels, inv, ((1,), (1,)))
    masks = sorted(range(1, rows), key=lambda k: (k.bit_length(), -k))
    pieces = [(0, mine)]
    pieces += [(k, lax.ppermute(mine, "row", pairs_xor(rows, k))) for k in masks]
    if mine.shape[1] % LANES:
        place = lax.axis_index("row")
        ordered = jnp.stack([piece for _, piece in sorted(pieces, key=lambda p: p[0])])
        ordered = jnp.take(ordered, jnp.arange(rows, dtype=jnp.int32) ^ place, axis=0)
        pieces = [(0, ordered.transpose(1, 0, 2).reshape(both, width))]
    outs = ()
    for n in range(0, len(pieces), 2):
        outs = finish(pieces[n : n + 2], inv, basis, front, outs)
    return outs


def solution(mesh):
    placed = (P(None, "row", "col"), P())
    return jax.shard_map(
        per_device,
        mesh=mesh,
        in_specs=placed,
        out_specs=(P(None, "col"), P(None, "row", "col")),
        check_vma=False,
    )
```

time: 126 us -> 118 us (0.937)
  the two profiles are of different devices: /device:TPU:0 before, /device:TPU:10 now
where the time goes in v3:
time: 118 us; the launch traced here: 117 us
  Pallas kernels  39.1 us (33%)
  waiting for transfers between devices  34 us (29%)
  starting transfers between devices  22.2 us (19%)
  blocking collectives  18 us (15%)
  matrix products  1.86 us (2%)
  local copies, waits for them, and re-layouts  1.23 us (1%)
    pallas_call x4, Pallas kernels, stage(): pl.pallas_call(lambda *refs: stage_kernel(lo, *refs), out_shape=(shape(si...  22.5 us
    all_to_all x1, blocking collectives, per_device(): spread = lax.all_to_all(pack(children, cols), 'col', 0, 0, tiled=True)  18 us
    ppermute x3, waiting for transfers between devices, per_device(): lax.ppermute(mine, 'row', pairs_xor(rows, k))  11.7 us
    ppermute x2, waiting for transfers between devices, sum_row_small(): value = value + lax.ppermute(value, 'row', pairs_xor(size, span - 1))  11 us
    pallas_call x2, Pallas kernels, finish(): pl.pallas_call(lambda *refs: finish_kernel(masks, *refs), out_shape=(shap...  8.55 us
    ppermute x6, waiting for transfers between devices, even_pieces(): lax.ppermute(piece, 'col', pairs_xor(size, k))  7.59 us
    ppermute x6, starting transfers between devices, even_pieces(): lax.ppermute(piece, 'col', pairs_xor(size, k))  7.04 us
    all_to_all x1, starting transfers between devices, per_device(): parts = lax.all_to_all(products, 'row', 0, 0, tiled=True)  4.63 us
  transfers between devices with their start and end apart: 15, of which 11 were waited for; matrix products, arithmetic and copies ran while one was open for 2% of the time, Pallas kernels for 24%

profile of v3, /device:TPU:10, one launch (start us, length us, event | category | flops | bytes accessed | tf_op | source)
XLA Modules:
  0.0 117.4 jit_solution(17043935537851460369)
XLA Ops:
  0.6 0.0 copy-start.2
  0.6 1.2 %copy-done.2 = f32[2,256,512]{2,1,0:T(8,128)S(1)} copy-done((f32[2,256,512]{2,1,0:T(8,128)S(1)}, f32[2,256,512]{2,1,0:T(8,128)}, u32[]{:S(2)}) %copy-start.2) | copy-done | bytes 1048600
  1.9 0.7 shard_map.41
  2.6 0.0 copy-start.3
  2.6 18.0 %all_to_all.15.spread_ref = f32[8,2,32,512]{3,2,1,0:T(8,128)S(1)} all-to-all(f32[8,2,32,512]{3,2,1,0:T(8,128)S(1)} %shard_map.41), channel_id=1, replica_groups=mesh['row'=4,'col'=8] {'col'}, dimensions={0} | all-to-all | bytes 2097152 | tf_op jit(solution)/shard_map/all_to_all | solution.py:420
  20.6 2.2 %order.1 = (f32[8,2,32,512]{3,2,1,0:T(8,128)}, f32[64,512]{1,0:T(8,128)S(1)}) custom-call(s32[2,16]{1,0:T(2,128)S(1)} %copy-done.3, f32[8,2,32,512]{3,2,1,0:T(8,128)S(1)} %all_to_all.15.spread_ref), custom_call_target="tpu_custom_call" | custom-call | flops 1000 | bytes 1000 | tf_op jit(solution)/shard_map/order/pallas_call | solution.py:103
  22.8 1.5 %collective-permute-start = (f32[64,512]{1,0:T(8,128)S(1)}, f32[64,512]{1,0:T(8,128)S(1)}, u32[]{:S(2)}, u32[]{:S(2)}) collective-permute-start(f32[64,512]{1,0:T(8,128)S(1)} %get-tuple-element.15.refs_0_), channel_id=1, source_target_pairs={{0,2},{1,3},{2,0},{3,1},{4,6},{5,7},{6,4},{7,5},{8,10},{9,11},{10,... | collective-permute-start | bytes 393224 | tf_op jit(solution)/shard_map/ppermute | solution.py:396
  24.3 0.6 collective-permute-start.2
  24.8 1.5 %collective-permute-start.1 = (f32[64,512]{1,0:T(8,128)S(1)}, f32[64,512]{1,0:T(8,128)S(1)}, u32[]{:S(2)}, u32[]{:S(2)}) collective-permute-start(f32[64,512]{1,0:T(8,128)S(1)} %get-tuple-element.15.refs_0_), channel_id=1, source_target_pairs={{0,4},{1,5},{2,6},{3,7},{4,0},{5,1},{6,2},{7,3},{8,12},{9,13},{10,... | collective-permute-start | bytes 393224 | tf_op jit(solution)/shard_map/ppermute | solution.py:396
  26.3 2.9 %collective-permute-done.refs_1_ = f32[64,512]{1,0:T(8,128)S(1)} collective-permute-done((f32[64,512]{1,0:T(8,128)S(1)}, f32[64,512]{1,0:T(8,128)S(1)}, u32[]{:S(2)}, u32[]{:S(2)}) %collective-permute-start) | collective-permute-done | bytes 131104 | tf_op jit(solution)/shard_map/ppermute | solution.py:396
  29.2 4.5 %all-to-all-start.1 = ((f32[8,2,32,512]{3,2,1,0:T(8,128)}), f32[8,2,32,512]{3,2,1,0:T(8,128)S(1)}, u32[]{:S(2)}, u32[]{:S(2)}) async-start(f32[8,2,32,512]{3,2,1,0:T(8,128)} %hold.1), calls=%async_computation.1 | async-start | bytes 2097152 | tf_op jit(solution)/shard_map/all_to_all | solution.py:423
  33.7 0.0 collective-permute-done.2.refs_3_
  33.7 0.0 collective-permute-done.1.refs_2_
  33.8 0.2 collective-permute-start.3
  34.0 1.8 %collective-permute-done.3.far_ref = f32[4,64,512]{2,1,0:T(8,128)S(1)} collective-permute-done((f32[4,64,512]{2,1,0:T(8,128)S(1)}, f32[4,64,512]{2,1,0:T(8,128)S(1)}, u32[]{:S(2)}, u32[]{:S(2)}) %collective-permute-start.3) | collective-permute-done | bytes 524320 | tf_op jit(solution)/shard_map/ppermute | solution.py:425
  35.8 0.8 shard_map.42
  36.6 0.0 copy-start
  36.6 0.5 collective-permute-start.4
  37.1 5.1 %collective-permute-done.4 = f32[256,128]{1,0:T(8,128)S(1)} collective-permute-done((f32[256,128]{1,0:T(8,128)S(1)}, f32[256,128]{1,0:T(8,128)S(1)}, u32[]{:S(2)}, u32[]{:S(2)}) %collective-permute-start.4) | collective-permute-done | bytes 131104 | tf_op jit(solution)/shard_map/ppermute | solution.py:407
  42.2 1.6 %collective-permute-start.5 = (f32[256,128]{1,0:T(8,128)S(1)}, f32[256,128]{1,0:T(8,128)S(1)}, u32[]{:S(2)}, u32[]{:S(2)}) collective-permute-start(f32[256,128]{1,0:T(8,128)S(1)} %add.6), channel_id=1, source_target_pairs={{0,24},{8,16},{16,8},{24,0},{1,25},{9,17},{17,9},{25,1},{2,26},{10... | collective-permute-start | bytes 393224 | tf_op jit(solution)/shard_map/ppermute | solution.py:407
  43.9 5.9 %collective-permute-done.5 = f32[256,128]{1,0:T(8,128)S(1)} collective-permute-done((f32[256,128]{1,0:T(8,128)S(1)}, f32[256,128]{1,0:T(8,128)S(1)}, u32[]{:S(2)}, u32[]{:S(2)}) %collective-permute-start.5) | collective-permute-done | bytes 131104 | tf_op jit(solution)/shard_map/ppermute | solution.py:407
  49.8 0.0 all-to-all-done.1.refs_2_
  49.8 3.0 %multiply.1.refs_4_ = f32[4,512,128]{2,1,0:T(8,128)} custom-call(f32[512,512]{1,0:T(8,128)S(1)} %get-tuple-element.17.panels_ref, f32[512,512]{1,0:T(8,128)S(1)} %bitcast.3, f32[256,128]{1,0:T(8,128)S(1)} %add.7.refs_0_), custom_call_target="tpu_custom_call" | custom-call | flops 1000 | bytes 1000 | tf_op jit(solution)/shard_map/multiply/pallas_call | solution.py:288
  52.8 0.0 copy-done
  52.9 4.6 %all-to-all-start.2 = ((f32[4,512,128]{2,1,0:T(8,128)}), f32[4,512,128]{2,1,0:T(8,128)}, u32[]{:S(2)}, u32[]{:S(2)}) async-start(f32[4,512,128]{2,1,0:T(8,128)} %multiply.1.refs_4_), calls=%async_computation.2 | async-start | bytes 2097152 | tf_op jit(solution)/shard_map/all_to_all | solution.py:431
  57.5 1.5 %collective-permute-start.8 = (f32[256,128]{1,0:T(8,128)S(1)}, f32[256,128]{1,0:T(8,128)S(1)}, u32[]{:S(2)}, u32[]{:S(2)}) collective-permute-start(f32[256,128]{1,0:T(8,128)S(1)} %add.7.refs_0_), channel_id=1, source_target_pairs={{0,6},{1,7},{2,4},{3,5},{4,2},{5,3},{6,0},{7,1},{8,14},{9,15},{10,... | collective-permute-start | bytes 393224 | tf_op jit(solution)/shard_map/ppermute | solution.py:396
  59.0 0.4 collective-permute-start.7
  59.4 1.6 %collective-permute-start.6 = (f32[256,128]{1,0:T(8,128)S(1)}, f32[256,128]{1,0:T(8,128)S(1)}, u32[]{:S(2)}, u32[]{:S(2)}) collective-permute-start(f32[256,128]{1,0:T(8,128)S(1)} %add.7.refs_0_), channel_id=1, source_target_pairs={{0,2},{1,3},{2,0},{3,1},{4,6},{5,7},{6,4},{7,5},{8,10},{9,11},{10,... | collective-permute-start | bytes 393224 | tf_op jit(solution)/shard_map/ppermute | solution.py:396
  61.0 3.3 %collective-permute-done.8.refs_3_ = f32[256,128]{1,0:T(8,128)S(1)} collective-permute-done((f32[256,128]{1,0:T(8,128)S(1)}, f32[256,128]{1,0:T(8,128)S(1)}, u32[]{:S(2)}, u32[]{:S(2)}) %collective-permute-start.8) | collective-permute-done | bytes 131104 | tf_op jit(solution)/shard_map/ppermute | solution.py:396
  64.3 1.3 %collective-permute-done.7.refs_2_ = f32[256,128]{1,0:T(8,128)S(1)} collective-permute-done((f32[256,128]{1,0:T(8,128)S(1)}, f32[256,128]{1,0:T(8,128)S(1)}, u32[]{:S(2)}, u32[]{:S(2)}) %collective-permute-start.7) | collective-permute-done | bytes 131104 | tf_op jit(solution)/shard_map/ppermute | solution.py:396
  65.6 0.1 collective-permute-done.6.refs_1_
  65.7 0.1 collective-permute-start.9
  65.8 1.9 %collective-permute-done.9.refs_1_ = f32[4,256,128]{2,1,0:T(8,128)S(1)} collective-permute-done((f32[4,256,128]{2,1,0:T(8,128)S(1)}, f32[4,256,128]{2,1,0:T(8,128)S(1)}, u32[]{:S(2)}, u32[]{:S(2)}) %collective-permute-start.9) | collective-permute-done | bytes 524320 | tf_op jit(solution)/shard_map/ppermute | solution.py:433
  67.7 6.1 %stage.4 = (f32[512,512]{1,0:T(8,128)S(1)}, f32[512,512]{1,0:T(8,128)S(1)}) custom-call(f32[4,256,128]{2,1,0:T(8,128)S(1)} %stack.3.refs_0_, f32[4,256,128]{2,1,0:T(8,128)S(1)} %collective-permute-done.9.refs_1_), custom_call_target="tpu_custom_call" | custom-call | flops 1000 | bytes 1000 | tf_op jit(solution)/shard_map/stage/pallas_call | solution.py:240
  73.8 5.8 %stage.5 = (f32[512,512]{1,0:T(8,128)S(1)}, f32[512,512]{1,0:T(8,128)S(1)}) custom-call(f32[512,512]{1,0:T(8,128)S(1)} %get-tuple-element.19.refs_0_, f32[512,512]{1,0:T(8,128)S(1)} %get-tuple-element.20.refs_1_), custom_call_target="tpu_custom_call", output_to_operand_aliasing={{0}: (0, {}), {1}: (1, {})} | custom-call | flops 1000 | bytes 1000 | tf_op jit(solution)/shard_map/stage/pallas_call | solution.py:240
  79.6 5.5 %stage.6 = (f32[512,512]{1,0:T(8,128)S(1)}, f32[512,512]{1,0:T(8,128)S(1)}) custom-call(f32[512,512]{1,0:T(8,128)S(1)} %get-tuple-element.21.refs_0_, f32[512,512]{1,0:T(8,128)S(1)} %get-tuple-element.22.refs_1_), custom_call_target="tpu_custom_call", output_to_operand_aliasing={{0}: (0, {}), {1}: (1, {})} | custom-call | flops 1000 | bytes 1000 | tf_op jit(solution)/shard_map/stage/pallas_call | solution.py:240
  85.1 0.0 all-to-all-done.2.parts_ref
  85.1 1.3 %total.1.refs_2_.refs_3_ = f32[512,128]{1,0:T(8,128)S(1)} custom-call(f32[4,512,128]{2,1,0:T(8,128)} %all-to-all-done.2.parts_ref), custom_call_target="tpu_custom_call" | custom-call | flops 1000 | bytes 1000 | tf_op jit(solution)/shard_map/total/pallas_call | solution.py:321
  86.4 0.1 collective-permute-start.12
  86.5 2.3 %collective-permute-start.11 = (f32[512,128]{1,0:T(8,128)S(1)}, f32[512,128]{1,0:T(8,128)S(1)}, u32[]{:S(2)}, u32[]{:S(2)}) collective-permute-start(f32[512,128]{1,0:T(8,128)S(1)} %total.1.refs_2_.refs_3_), channel_id=1, source_target_pairs={{0,16},{8,24},{16,0},{24,8},{1,17},{9,25},{17,1},{25,9},{2,18},{10... | collective-permute-start | bytes 786440 | tf_op jit(solution)/shard_map/ppermute | solution.py:441
  88.8 1.2 collective-permute-start.10
  90.0 5.1 %stage.7 = (f32[512,512]{1,0:T(8,128)S(1)}, f32[512,512]{1,0:T(8,128)S(1)}) custom-call(f32[512,512]{1,0:T(8,128)S(1)} %get-tuple-element.23.refs_0_, f32[512,512]{1,0:T(8,128)S(1)} %get-tuple-element.24.refs_1_, f32[512,128]{1,0:T(8,128)S(1)} %total.1.refs_2_.refs_3_), custom_call_target="tpu_custom_call", output_to_operand_aliasing={{0}: (0, {}), {1}: (1, {})} | custom-call | flops 1000 | bytes 1000 | tf_op jit(solution)/shard_map/stage/pallas_call | solution.py:240
  95.1 1.9 %fusion.refs_1_ = f32[512,512]{1,0:T(8,128)S(1)} fusion(f32[512,512]{1,0:T(8,128)S(1)} %copy-done.1, f32[512,512]{1,0:T(8,128)S(1)} %get-tuple-element.25.refs_0_), kind=kOutput, calls=%fused_computation | convolution fusion | flops 1610612736 | bytes 3145728 | tf_op jit(solution)/shard_map/dot_general | solution.py:19
  96.9 0.4 collective-permute-done.12.refs_4_
  97.3 4.3 %finish.2 = (f32[512,512]{1,0:T(8,128)}, f32[2,256,512]{2,1,0:T(8,128)}) custom-call(f32[512,512]{1,0:T(8,128)S(1)} %get-tuple-element.25.refs_0_, f32[512,512]{1,0:T(8,128)S(1)} %fusion.refs_1_, f32[8,2,32,512]{3,2,1,0:T(8,128)S(1)} %all-to-all-done.1.refs_2_, f32[512,128]{1,0:T(8,128)S(1)} %total.1.refs_2_.refs_3_, ...), custom_call_target="tpu_custom_call" | custom-call | flops 1000 | bytes 1000 | tf_op jit(solution)/shard_map/finish/pallas_call | solution.py:373
  101.6 5.2 %collective-permute-done.11.refs_4_ = f32[512,128]{1,0:T(8,128)S(1)} collective-permute-done((f32[512,128]{1,0:T(8,128)S(1)}, f32[512,128]{1,0:T(8,128)S(1)}, u32[]{:S(2)}, u32[]{:S(2)}) %collective-permute-start.11) | collective-permute-done | bytes 262176 | tf_op jit(solution)/shard_map/ppermute | solution.py:441
  106.7 6.2 %collective-permute-done.10.refs_3_ = f32[512,128]{1,0:T(8,128)S(1)} collective-permute-done((f32[512,128]{1,0:T(8,128)S(1)}, f32[512,128]{1,0:T(8,128)S(1)}, u32[]{:S(2)}, u32[]{:S(2)}) %collective-permute-start.10) | collective-permute-done | bytes 262176 | tf_op jit(solution)/shard_map/ppermute | solution.py:441
  112.9 4.3 %finish.3 = (f32[512,512]{1,0:T(8,128)}, f32[2,256,512]{2,1,0:T(8,128)}) custom-call(f32[512,512]{1,0:T(8,128)S(1)} %get-tuple-element.25.refs_0_, f32[512,512]{1,0:T(8,128)S(1)} %fusion.refs_1_, f32[8,2,32,512]{3,2,1,0:T(8,128)S(1)} %all-to-all-done.1.refs_2_, ...), custom_call_target="tpu_custom_call", output_to_operand_aliasing={{0}: (5, {}), {1}: (6, {})} | custom-call | flops 1000 | bytes 1000 | tf_op jit(solution)/shard_map/finish/pallas_call | solution.py:373
  (8 shorter events, 0.1 us)
Async XLA Ops:
  0.6 1.2 %copy-start.2 = (f32[2,256,512]{2,1,0:T(8,128)S(1)}, f32[2,256,512]{2,1,0:T(8,128)}, u32[]{:S(2)}) copy-start(f32[2,256,512]{2,1,0:T(8,128)} %children_ref.1) | copy-start | bytes 3145732
  2.6 18.0 %copy-start.3 = (s32[2,16]{1,0:T(2,128)S(1)}, s32[2,16]{1,0:T(2,128)}, u32[]{:S(2)}) copy-start(s32[2,16]{1,0:T(2,128)} %maps_ref.1) | copy-start | bytes 388
  22.8 6.4 %collective-permute-start = (f32[64,512]{1,0:T(8,128)S(1)}, f32[64,512]{1,0:T(8,128)S(1)}, u32[]{:S(2)}, u32[]{:S(2)}) collective-permute-start(f32[64,512]{1,0:T(8,128)S(1)} %get-tuple-element.15.refs_0_), channel_id=1, source_target_pairs={{0,2},{1,3},{2,0},{3,1},{4,6},{5,7},{6,4},{7,5},{8,10},{9,11},{10,... | collective-permute-start | bytes 393224 | tf_op jit(solution)/shard_map/ppermute | solution.py:396
  24.3 9.5 %collective-permute-start.2 = (f32[64,512]{1,0:T(8,128)S(1)}, f32[64,512]{1,0:T(8,128)S(1)}, u32[]{:S(2)}, u32[]{:S(2)}) collective-permute-start(f32[64,512]{1,0:T(8,128)S(1)} %get-tuple-element.15.refs_0_), channel_id=1, source_target_pairs={{0,6},{1,7},{2,4},{3,5},{4,2},{5,3},{6,0},{7,1},{8,14},{9,15},{10,... | collective-permute-start | bytes 393224 | tf_op jit(solution)/shard_map/ppermute | solution.py:396
  24.8 8.9 %collective-permute-start.1 = (f32[64,512]{1,0:T(8,128)S(1)}, f32[64,512]{1,0:T(8,128)S(1)}, u32[]{:S(2)}, u32[]{:S(2)}) collective-permute-start(f32[64,512]{1,0:T(8,128)S(1)} %get-tuple-element.15.refs_0_), channel_id=1, source_target_pairs={{0,4},{1,5},{2,6},{3,7},{4,0},{5,1},{6,2},{7,3},{8,12},{9,13},{10,... | collective-permute-start | bytes 393224 | tf_op jit(solution)/shard_map/ppermute | solution.py:396
  29.2 20.6 %all-to-all-start.1 = ((f32[8,2,32,512]{3,2,1,0:T(8,128)}), f32[8,2,32,512]{3,2,1,0:T(8,128)S(1)}, u32[]{:S(2)}, u32[]{:S(2)}) async-start(f32[8,2,32,512]{3,2,1,0:T(8,128)} %hold.1), calls=%async_computation.1 | async-start | bytes 2097152 | tf_op jit(solution)/shard_map/all_to_all | solution.py:423
  33.8 2.0 %collective-permute-start.3 = (f32[4,64,512]{2,1,0:T(8,128)S(1)}, f32[4,64,512]{2,1,0:T(8,128)S(1)}, u32[]{:S(2)}, u32[]{:S(2)}) collective-permute-start(f32[4,64,512]{2,1,0:T(8,128)S(1)} %stack.2.near_ref), channel_id=1, source_target_pairs={{0,1},{1,0},{2,3},{3,2},{4,5},{5,4},{6,7},{7,6},{8,9},{9,8},{10,11... | collective-permute-start | bytes 1572872 | tf_op jit(solution)/shard_map/ppermute | solution.py:425
  36.6 16.3 %copy-start = (f32[512,512]{1,0:T(8,128)}, f32[512,512]{1,0:T(8,128)S(1)}, u32[]{:S(2)}) copy-start(f32[512,512]{1,0:T(8,128)S(1)} %get-tuple-element.17.panels_ref) | copy-start | bytes 3145732
  36.6 5.6 %collective-permute-start.4 = (f32[256,128]{1,0:T(8,128)S(1)}, f32[256,128]{1,0:T(8,128)S(1)}, u32[]{:S(2)}, u32[]{:S(2)}) collective-permute-start(f32[256,128]{1,0:T(8,128)S(1)} %get-tuple-element.16), channel_id=1, source_target_pairs={{0,8},{8,0},{16,24},{24,16},{1,9},{9,1},{17,25},{25,17},{2,10},{10... | collective-permute-start | bytes 393224 | tf_op jit(solution)/shard_map/ppermute | solution.py:407
  42.2 7.6 %collective-permute-start.5 = (f32[256,128]{1,0:T(8,128)S(1)}, f32[256,128]{1,0:T(8,128)S(1)}, u32[]{:S(2)}, u32[]{:S(2)}) collective-permute-start(f32[256,128]{1,0:T(8,128)S(1)} %add.6), channel_id=1, source_target_pairs={{0,24},{8,16},{16,8},{24,0},{1,25},{9,17},{17,9},{25,1},{2,26},{10... | collective-permute-start | bytes 393224 | tf_op jit(solution)/shard_map/ppermute | solution.py:407
  52.9 32.3 %all-to-all-start.2 = ((f32[4,512,128]{2,1,0:T(8,128)}), f32[4,512,128]{2,1,0:T(8,128)}, u32[]{:S(2)}, u32[]{:S(2)}) async-start(f32[4,512,128]{2,1,0:T(8,128)} %multiply.1.refs_4_), calls=%async_computation.2 | async-start | bytes 2097152 | tf_op jit(solution)/shard_map/all_to_all | solution.py:431
  57.5 6.8 %collective-permute-start.8 = (f32[256,128]{1,0:T(8,128)S(1)}, f32[256,128]{1,0:T(8,128)S(1)}, u32[]{:S(2)}, u32[]{:S(2)}) collective-permute-start(f32[256,128]{1,0:T(8,128)S(1)} %add.7.refs_0_), channel_id=1, source_target_pairs={{0,6},{1,7},{2,4},{3,5},{4,2},{5,3},{6,0},{7,1},{8,14},{9,15},{10,... | collective-permute-start | bytes 393224 | tf_op jit(solution)/shard_map/ppermute | solution.py:396
  59.0 6.6 %collective-permute-start.7 = (f32[256,128]{1,0:T(8,128)S(1)}, f32[256,128]{1,0:T(8,128)S(1)}, u32[]{:S(2)}, u32[]{:S(2)}) collective-permute-start(f32[256,128]{1,0:T(8,128)S(1)} %add.7.refs_0_), channel_id=1, source_target_pairs={{0,4},{1,5},{2,6},{3,7},{4,0},{5,1},{6,2},{7,3},{8,12},{9,13},{10,... | collective-permute-start | bytes 393224 | tf_op jit(solution)/shard_map/ppermute | solution.py:396
  59.4 6.3 %collective-permute-start.6 = (f32[256,128]{1,0:T(8,128)S(1)}, f32[256,128]{1,0:T(8,128)S(1)}, u32[]{:S(2)}, u32[]{:S(2)}) collective-permute-start(f32[256,128]{1,0:T(8,128)S(1)} %add.7.refs_0_), channel_id=1, source_target_pairs={{0,2},{1,3},{2,0},{3,1},{4,6},{5,7},{6,4},{7,5},{8,10},{9,11},{10,... | collective-permute-start | bytes 393224 | tf_op jit(solution)/shard_map/ppermute | solution.py:396
  65.7 2.0 %collective-permute-start.9 = (f32[4,256,128]{2,1,0:T(8,128)S(1)}, f32[4,256,128]{2,1,0:T(8,128)S(1)}, u32[]{:S(2)}, u32[]{:S(2)}) collective-permute-start(f32[4,256,128]{2,1,0:T(8,128)S(1)} %stack.3.refs_0_), channel_id=1, source_target_pairs={{0,1},{1,0},{2,3},{3,2},{4,5},{5,4},{6,7},{7,6},{8,9},{9,8},{10,11... | collective-permute-start | bytes 1572872 | tf_op jit(solution)/shard_map/ppermute | solution.py:433
  86.4 10.9 %collective-permute-start.12 = (f32[512,128]{1,0:T(8,128)S(1)}, f32[512,128]{1,0:T(8,128)S(1)}, u32[]{:S(2)}, u32[]{:S(2)}) collective-permute-start(f32[512,128]{1,0:T(8,128)S(1)} %total.1.refs_2_.refs_3_), channel_id=1, source_target_pairs={{0,8},{8,0},{16,24},{24,16},{1,9},{9,1},{17,25},{25,17},{2,10},{10... | collective-permute-start | bytes 786440 | tf_op jit(solution)/shard_map/ppermute | solution.py:441
  86.5 20.2 %collective-permute-start.11 = (f32[512,128]{1,0:T(8,128)S(1)}, f32[512,128]{1,0:T(8,128)S(1)}, u32[]{:S(2)}, u32[]{:S(2)}) collective-permute-start(f32[512,128]{1,0:T(8,128)S(1)} %total.1.refs_2_.refs_3_), channel_id=1, source_target_pairs={{0,16},{8,24},{16,0},{24,8},{1,17},{9,25},{17,1},{25,9},{2,18},{10... | collective-permute-start | bytes 786440 | tf_op jit(solution)/shard_map/ppermute | solution.py:441
  88.8 24.1 %collective-permute-start.10 = (f32[512,128]{1,0:T(8,128)S(1)}, f32[512,128]{1,0:T(8,128)S(1)}, u32[]{:S(2)}, u32[]{:S(2)}) collective-permute-start(f32[512,128]{1,0:T(8,128)S(1)} %total.1.refs_2_.refs_3_), channel_id=1, source_target_pairs={{0,24},{8,16},{16,8},{24,0},{1,25},{9,17},{17,9},{25,1},{2,26},{10... | collective-permute-start | bytes 786440 | tf_op jit(solution)/shard_map/ppermute | solution.py:441
  90.0 5.1 %copy-start.1 = (f32[512,512]{1,0:T(8,128)S(1)}, f32[512,512]{1,0:T(8,128)}, u32[]{:S(2)}) copy-start(f32[512,512]{1,0:T(8,128)} %copy-done) | copy-start | bytes 3145732

commit v4 on v3

--- a/solution.py
+++ b/solution.py
@@ -165,29 +165,6 @@
     return ((p[0] + p[1]) + (p[2] + p[3])) + ((p[4] + p[5]) + (p[6] + p[7]))
 
 
-def small_inverse(cols):
-    sub = lax.broadcasted_iota(jnp.int32, (SUBS, LANES), 0)
-    x = list(cols)
-    t = [jnp.zeros((SUBS, LANES), F32) for _ in range(SUBS)]
-    for j in range(SUBS):
-        pivot = row_of(x[j], j)
-        reciprocal = 1.0 / pivot
-        root = lax.rsqrt(pivot)
-        here = sub == j
-        xj = x[j]
-        for k in range(SUBS):
-            if k == j:
-                continue
-            b = row_of(x[k], j)
-            if k < j:
-                t[k] = jnp.where(here, root * b, t[k])
-            b = b * reciprocal
-            x[k] = jnp.where(here, b, x[k] - xj * b)
-        t[j] = jnp.where(here, root, t[j])
-        x[j] = jnp.where(here, reciprocal, -xj * reciprocal)
-    return x, t
-
-
 def factor_inverse(lo, a_ref, out_ref):
     hi = lo + LANES
     steps = LANES // SUBS
@@ -195,19 +172,36 @@
     sub = lax.broadcasted_iota(jnp.int32, (SUBS, LANES), 0)
     z = [a_ref[lo + SUBS * i : lo + SUBS * (i + 1), lo:hi] for i in range(steps)]
     for s in range(steps):
-        inv, t = small_inverse([column_of(z[s], SUBS * s + k) for k in range(SUBS)])
-        here = (lane >= SUBS * s) & (lane < SUBS * (s + 1))
-        own = jnp.where(here, jnp.where(lane == sub + SUBS * s, 1.0, 0.0), z[s])
-        rows = [row_of(own, k) for k in range(SUBS)]
+        x = [column_of(z[s], SUBS * s + k) for k in range(SUBS)]
+        block = (lane >= SUBS * s) & (lane < SUBS * (s + 1))
+        slab = jnp.where(block, jnp.where(lane == sub + SUBS * s, 1.0, 0.0), z[s])
+        out = jnp.zeros((SUBS, LANES), F32)
+        for j in range(SUBS):
+            here = sub == j
+            pivot = row_of(x[j], j)
+            reciprocal = 1.0 / pivot
+            for k in range(j + 1, SUBS):
+                b = row_of(x[k], j) * reciprocal
+                x[k] = jnp.where(here, b, x[k] - x[j] * b)
+            row = row_of(slab, j)
+            out = jnp.where(here, lax.rsqrt(pivot) * row, out)
+            row = row * reciprocal
+            slab = jnp.where(here, row, slab - x[j] * row)
         out_ref[lo + SUBS * s : lo + SUBS * (s + 1), lo:hi] = jnp.where(
-            lane < SUBS * (s + 1), combined(t, rows), 0.0
+            lane < SUBS * (s + 1), out, 0.0
         )
         if s + 1 < steps:
-            scaled = combined(inv, rows)
-            scaled = [row_of(scaled, k) for k in range(SUBS)]
-            for i in range(s + 1, steps):
-                c = [column_of(z[i], SUBS * s + k) for k in range(SUBS)]
-                z[i] = jnp.where(here, 0.0, z[i]) - combined(c, scaled)
+            c = [column_of(z[s + 1], SUBS * s + k) for k in range(SUBS)]
+            change = combined(c, [row_of(slab, k) for k in range(SUBS)])
+            z[s + 1] = jnp.where(block, 0.0, z[s + 1]) - change
+        if s + 2 < steps:
+            below = jnp.concatenate(z[s + 2 :], axis=0)
+            around = [jnp.zeros((SUBS, LANES), F32)] * steps
+            around[s] = slab
+            change = dot(below, jnp.concatenate(around, axis=0), ((1,), (0,)))
+            for i in range(s + 2, steps):
+                at = SUBS * (i - s - 2)
+                z[i] = jnp.where(block, 0.0, z[i]) - change[at : at + SUBS, :]
 
 
 def stage_kernel(lo, *refs):
@@ -332,34 +326,43 @@
 def finish_kernel(masks, inv_ref, basis_ref, front_ref, *refs):
     upper_ref, trail_ref, m_ref, w_ref, f_ref, sems = refs[-6:]
     owners, two, part, total = front_ref.shape
+    both = inv_ref.shape[0]
     width = refs[0].shape[1]
-    for n in range(len(masks)):
-        m_ref[:, n * width : (n + 1) * width] = refs[n][...]
-    w_ref[...] = dot(inv_ref[...], m_ref[...], ((1,), (0,)))
-    copies = []
     columns = []
     for n, mask in enumerate(masks):
+        m_ref[:, n * width : (n + 1) * width] = refs[n][...]
         if width == total:
             columns.append(pl.ds(0, width))
         else:
             at = lax.bitwise_xor(lax.axis_index("row"), mask) * width
             columns.append(pl.ds(pl.multiple_of(at, LANES), width))
-        held = w_ref.at[:, pl.ds(n * width, width)]
-        copies.append(pltpu.make_async_copy(held, upper_ref.at[:, columns[n]], sems.at[0, n]))
-        copies[-1].start()
-    product = dot(basis_ref[...], w_ref[...], ((1,), (0,)))
-    for n, mask in enumerate(masks):
-        for owner in range(owners):
-            for child in range(two):
-                row = (owner * two + child) * part
-                f_ref[n, child, owner * part : (owner + 1) * part, :] = (
-                    front_ref[owner, child, :, columns[n]]
-                    - product[row : row + part, n * width : (n + 1) * width]
-                )
-        copies.append(
-            pltpu.make_async_copy(f_ref.at[n], trail_ref.at[:, :, columns[n]], sems.at[1, n])
-        )
-        copies[-1].start()
+    copies = []
+    for step in range(both // LANES):
+        lo, hi = step * LANES, (step + 1) * LANES
+        w_ref[lo:hi, :] = dot(inv_ref[lo:hi, :hi], m_ref[:hi, :], ((1,), (0,)))
+        for n in range(len(masks)):
+            held = w_ref.at[lo:hi, pl.ds(n * width, width)]
+            goal = upper_ref.at[lo:hi, columns[n]]
+            copies.append(pltpu.make_async_copy(held, goal, sems.at[0, n, step]))
+            copies[-1].start()
+    rows = LANES // two
+    held_owners = rows // part
+    for step in range(owners // held_owners):
+        lo = step * LANES
+        product = dot(basis_ref[lo : lo + LANES, :], w_ref[...], ((1,), (0,)))
+        for n in range(len(masks)):
+            for owner in range(held_owners):
+                for child in range(two):
+                    row = (owner * two + child) * part
+                    at = step * rows + owner * part
+                    f_ref[n, child, at : at + part, :] = (
+                        front_ref[step * held_owners + owner, child, :, columns[n]]
+                        - product[row : row + part, n * width : (n + 1) * width]
+                    )
+            held = f_ref.at[n, :, pl.ds(step * rows, rows), :]
+            goal = trail_ref.at[:, pl.ds(step * rows, rows), columns[n]]
+            copies.append(pltpu.make_async_copy(held, goal, sems.at[1, n, step]))
+            copies[-1].start()
     for copy in copies:
         copy.wait()
 
@@ -380,7 +383,7 @@
             pltpu.VMEM((both, count * width), F32),
             pltpu.VMEM((both, count * width), F32),
             pltpu.VMEM((count, two, owners * part, width), F32),
-            pltpu.SemaphoreType.DMA((2, count)),
+            pltpu.SemaphoreType.DMA((2, count, both // LANES)),
         ],
         compiler_params=KERNEL,
         cost_estimate=cost(1000, 1000),

time: 118 us -> 114 us (0.966)
  Pallas kernels: 39.1 us -> 33.8 us
  waiting for transfers between devices: 34 us -> 35.3 us
    pallas_call x4, Pallas kernels: 22.5 us -> 18.3 us  [stage(): pl.pallas_call(lambda *refs: stage_kernel(lo, *refs), out_shape=(shape(si...]
    ppermute x3, waiting for transfers between devices: 11.7 us -> 13 us  [per_device(): lax.ppermute(mine, 'row', pairs_xor(rows, k))]
  transfers between devices with their start and end apart: 15 -> 15, of which waited for: 11 -> 11; matrix products, arithmetic and copies ran while one was open for 2% -> 2% of each run, Pallas kernels for 24% -> 20%
where the time goes in v4:
time: 114 us
  waiting for transfers between devices  35.3 us (31%)
  Pallas kernels  33.8 us (30%)
  starting transfers between devices  22.2 us (19%)
  blocking collectives  18 us (16%)
  matrix products  2.08 us (2%)
  local copies, waits for them, and re-layouts  1.23 us (1%)
    pallas_call x4, Pallas kernels, stage(): pl.pallas_call(lambda *refs: stage_kernel(lo, *refs), out_shape=(shape(si...  18.3 us
    all_to_all x1, blocking collectives, per_device(): spread = lax.all_to_all(pack(children, cols), 'col', 0, 0, tiled=True)  18 us
    ppermute x3, waiting for transfers between devices, per_device(): lax.ppermute(mine, 'row', pairs_xor(rows, k))  13 us
    ppermute x2, waiting for transfers between devices, sum_row_small(): value = value + lax.ppermute(value, 'row', pairs_xor(size, span - 1))  11 us
    ppermute x6, waiting for transfers between devices, even_pieces(): lax.ppermute(piece, 'col', pairs_xor(size, k))  7.54 us
    pallas_call x2, Pallas kernels, finish(): pl.pallas_call(lambda *refs: finish_kernel(masks, *refs), out_shape=(shap...  7.43 us
    ppermute x6, starting transfers between devices, even_pieces(): lax.ppermute(piece, 'col', pairs_xor(size, k))  7.04 us
    all_to_all x1, starting transfers between devices, per_device(): parts = lax.all_to_all(products, 'row', 0, 0, tiled=True)  4.63 us
  transfers between devices with their start and end apart: 15, of which 11 were waited for; matrix products, arithmetic and copies ran while one was open for 2% of the time, Pallas kernels for 20%

profile of v4, /device:TPU:10, one launch (start us, length us, event | category | flops | bytes accessed | tf_op | source)
XLA Modules:
  0.0 113.5 jit_solution(1277225926802944843)
XLA Ops:
  0.6 0.0 copy-start.2
  0.6 1.2 %copy-done.2 = f32[2,256,512]{2,1,0:T(8,128)S(1)} copy-done((f32[2,256,512]{2,1,0:T(8,128)S(1)}, f32[2,256,512]{2,1,0:T(8,128)}, u32[]{:S(2)}) %copy-start.2) | copy-done | bytes 1048600
  1.9 0.7 shard_map.41
  2.6 0.0 copy-start.3
  2.6 18.0 %all_to_all.15.spread_ref = f32[8,2,32,512]{3,2,1,0:T(8,128)S(1)} all-to-all(f32[8,2,32,512]{3,2,1,0:T(8,128)S(1)} %shard_map.41), channel_id=1, replica_groups=mesh['row'=4,'col'=8] {'col'}, dimensions={0} | all-to-all | bytes 2097152 | tf_op jit(solution)/shard_map/all_to_all | solution.py:423
  20.6 0.0 copy-done.3
  20.6 2.2 %order.1 = (f32[8,2,32,512]{3,2,1,0:T(8,128)}, f32[64,512]{1,0:T(8,128)S(1)}) custom-call(s32[2,16]{1,0:T(2,128)S(1)} %copy-done.3, f32[8,2,32,512]{3,2,1,0:T(8,128)S(1)} %all_to_all.15.spread_ref), custom_call_target="tpu_custom_call" | custom-call | flops 1000 | bytes 1000 | tf_op jit(solution)/shard_map/order/pallas_call | solution.py:103
  22.8 1.5 %collective-permute-start = (f32[64,512]{1,0:T(8,128)S(1)}, f32[64,512]{1,0:T(8,128)S(1)}, u32[]{:S(2)}, u32[]{:S(2)}) collective-permute-start(f32[64,512]{1,0:T(8,128)S(1)} %get-tuple-element.15.refs_0_), channel_id=1, source_target_pairs={{0,2},{1,3},{2,0},{3,1},{4,6},{5,7},{6,4},{7,5},{8,10},{9,11},{10,... | collective-permute-start | bytes 393224 | tf_op jit(solution)/shard_map/ppermute | solution.py:399
  24.3 0.6 collective-permute-start.2
  24.8 1.5 %collective-permute-start.1 = (f32[64,512]{1,0:T(8,128)S(1)}, f32[64,512]{1,0:T(8,128)S(1)}, u32[]{:S(2)}, u32[]{:S(2)}) collective-permute-start(f32[64,512]{1,0:T(8,128)S(1)} %get-tuple-element.15.refs_0_), channel_id=1, source_target_pairs={{0,4},{1,5},{2,6},{3,7},{4,0},{5,1},{6,2},{7,3},{8,12},{9,13},{10,... | collective-permute-start | bytes 393224 | tf_op jit(solution)/shard_map/ppermute | solution.py:399
  26.3 2.9 %collective-permute-done.refs_1_ = f32[64,512]{1,0:T(8,128)S(1)} collective-permute-done((f32[64,512]{1,0:T(8,128)S(1)}, f32[64,512]{1,0:T(8,128)S(1)}, u32[]{:S(2)}, u32[]{:S(2)}) %collective-permute-start) | collective-permute-done | bytes 131104 | tf_op jit(solution)/shard_map/ppermute | solution.py:399
  29.2 4.5 %all-to-all-start.1 = ((f32[8,2,32,512]{3,2,1,0:T(8,128)}), f32[8,2,32,512]{3,2,1,0:T(8,128)S(1)}, u32[]{:S(2)}, u32[]{:S(2)}) async-start(f32[8,2,32,512]{3,2,1,0:T(8,128)} %hold.1), calls=%async_computation.1 | async-start | bytes 2097152 | tf_op jit(solution)/shard_map/all_to_all | solution.py:426
  33.7 0.0 collective-permute-done.2.refs_3_
  33.7 0.0 collective-permute-done.1.refs_2_
  33.8 0.2 collective-permute-start.3
  34.0 1.8 %collective-permute-done.3.far_ref = f32[4,64,512]{2,1,0:T(8,128)S(1)} collective-permute-done((f32[4,64,512]{2,1,0:T(8,128)S(1)}, f32[4,64,512]{2,1,0:T(8,128)S(1)}, u32[]{:S(2)}, u32[]{:S(2)}) %collective-permute-start.3) | collective-permute-done | bytes 524320 | tf_op jit(solution)/shard_map/ppermute | solution.py:428
  35.8 0.8 shard_map.42
  36.6 0.0 copy-start
  36.6 0.5 collective-permute-start.4
  37.1 5.1 %collective-permute-done.4 = f32[256,128]{1,0:T(8,128)S(1)} collective-permute-done((f32[256,128]{1,0:T(8,128)S(1)}, f32[256,128]{1,0:T(8,128)S(1)}, u32[]{:S(2)}, u32[]{:S(2)}) %collective-permute-start.4) | collective-permute-done | bytes 131104 | tf_op jit(solution)/shard_map/ppermute | solution.py:410
  42.2 1.7 %collective-permute-start.5 = (f32[256,128]{1,0:T(8,128)S(1)}, f32[256,128]{1,0:T(8,128)S(1)}, u32[]{:S(2)}, u32[]{:S(2)}) collective-permute-start(f32[256,128]{1,0:T(8,128)S(1)} %add.6), channel_id=1, source_target_pairs={{0,24},{8,16},{16,8},{24,0},{1,25},{9,17},{17,9},{25,1},{2,26},{10... | collective-permute-start | bytes 393224 | tf_op jit(solution)/shard_map/ppermute | solution.py:410
  43.9 5.9 %collective-permute-done.5 = f32[256,128]{1,0:T(8,128)S(1)} collective-permute-done((f32[256,128]{1,0:T(8,128)S(1)}, f32[256,128]{1,0:T(8,128)S(1)}, u32[]{:S(2)}, u32[]{:S(2)}) %collective-permute-start.5) | collective-permute-done | bytes 131104 | tf_op jit(solution)/shard_map/ppermute | solution.py:410
  49.8 0.0 all-to-all-done.1.refs_2_
  49.8 3.0 %multiply.1.refs_4_ = f32[4,512,128]{2,1,0:T(8,128)} custom-call(f32[512,512]{1,0:T(8,128)S(1)} %get-tuple-element.17.panels_ref, f32[512,512]{1,0:T(8,128)S(1)} %bitcast.3, f32[256,128]{1,0:T(8,128)S(1)} %add.7.refs_0_), custom_call_target="tpu_custom_call" | custom-call | flops 1000 | bytes 1000 | tf_op jit(solution)/shard_map/multiply/pallas_call | solution.py:282
  52.9 4.6 %all-to-all-start.2 = ((f32[4,512,128]{2,1,0:T(8,128)}), f32[4,512,128]{2,1,0:T(8,128)}, u32[]{:S(2)}, u32[]{:S(2)}) async-start(f32[4,512,128]{2,1,0:T(8,128)} %multiply.1.refs_4_), calls=%async_computation.2 | async-start | bytes 2097152 | tf_op jit(solution)/shard_map/all_to_all | solution.py:434
  57.5 1.5 %collective-permute-start.8 = (f32[256,128]{1,0:T(8,128)S(1)}, f32[256,128]{1,0:T(8,128)S(1)}, u32[]{:S(2)}, u32[]{:S(2)}) collective-permute-start(f32[256,128]{1,0:T(8,128)S(1)} %add.7.refs_0_), channel_id=1, source_target_pairs={{0,6},{1,7},{2,4},{3,5},{4,2},{5,3},{6,0},{7,1},{8,14},{9,15},{10,... | collective-permute-start | bytes 393224 | tf_op jit(solution)/shard_map/ppermute | solution.py:399
  59.0 0.4 collective-permute-start.7
  59.4 1.6 %collective-permute-start.6 = (f32[256,128]{1,0:T(8,128)S(1)}, f32[256,128]{1,0:T(8,128)S(1)}, u32[]{:S(2)}, u32[]{:S(2)}) collective-permute-start(f32[256,128]{1,0:T(8,128)S(1)} %add.7.refs_0_), channel_id=1, source_target_pairs={{0,2},{1,3},{2,0},{3,1},{4,6},{5,7},{6,4},{7,5},{8,10},{9,11},{10,... | collective-permute-start | bytes 393224 | tf_op jit(solution)/shard_map/ppermute | solution.py:399
  61.0 3.3 %collective-permute-done.8.refs_3_ = f32[256,128]{1,0:T(8,128)S(1)} collective-permute-done((f32[256,128]{1,0:T(8,128)S(1)}, f32[256,128]{1,0:T(8,128)S(1)}, u32[]{:S(2)}, u32[]{:S(2)}) %collective-permute-start.8) | collective-permute-done | bytes 131104 | tf_op jit(solution)/shard_map/ppermute | solution.py:399
  64.3 1.3 %collective-permute-done.7.refs_2_ = f32[256,128]{1,0:T(8,128)S(1)} collective-permute-done((f32[256,128]{1,0:T(8,128)S(1)}, f32[256,128]{1,0:T(8,128)S(1)}, u32[]{:S(2)}, u32[]{:S(2)}) %collective-permute-start.7) | collective-permute-done | bytes 131104 | tf_op jit(solution)/shard_map/ppermute | solution.py:399
  65.6 0.1 collective-permute-done.6.refs_1_
  65.7 0.1 collective-permute-start.9
  65.7 1.9 %collective-permute-done.9.refs_1_ = f32[4,256,128]{2,1,0:T(8,128)S(1)} collective-permute-done((f32[4,256,128]{2,1,0:T(8,128)S(1)}, f32[4,256,128]{2,1,0:T(8,128)S(1)}, u32[]{:S(2)}, u32[]{:S(2)}) %collective-permute-start.9) | collective-permute-done | bytes 524320 | tf_op jit(solution)/shard_map/ppermute | solution.py:436
  67.6 5.0 %stage.4 = (f32[512,512]{1,0:T(8,128)S(1)}, f32[512,512]{1,0:T(8,128)S(1)}) custom-call(f32[4,256,128]{2,1,0:T(8,128)S(1)} %stack.3.refs_0_, f32[4,256,128]{2,1,0:T(8,128)S(1)} %collective-permute-done.9.refs_1_), custom_call_target="tpu_custom_call" | custom-call | flops 1000 | bytes 1000 | tf_op jit(solution)/shard_map/stage/pallas_call | solution.py:234
  72.7 4.7 %stage.5 = (f32[512,512]{1,0:T(8,128)S(1)}, f32[512,512]{1,0:T(8,128)S(1)}) custom-call(f32[512,512]{1,0:T(8,128)S(1)} %get-tuple-element.19.refs_0_, f32[512,512]{1,0:T(8,128)S(1)} %get-tuple-element.20.refs_1_), custom_call_target="tpu_custom_call", output_to_operand_aliasing={{0}: (0, {}), {1}: (1, {})} | custom-call | flops 1000 | bytes 1000 | tf_op jit(solution)/shard_map/stage/pallas_call | solution.py:234
  77.4 4.4 %stage.6 = (f32[512,512]{1,0:T(8,128)S(1)}, f32[512,512]{1,0:T(8,128)S(1)}) custom-call(f32[512,512]{1,0:T(8,128)S(1)} %get-tuple-element.21.refs_0_, f32[512,512]{1,0:T(8,128)S(1)} %get-tuple-element.22.refs_1_), custom_call_target="tpu_custom_call", output_to_operand_aliasing={{0}: (0, {}), {1}: (1, {})} | custom-call | flops 1000 | bytes 1000 | tf_op jit(solution)/shard_map/stage/pallas_call | solution.py:234
  81.9 0.0 all-to-all-done.2.parts_ref
  81.9 1.3 %total.1.refs_2_.refs_3_ = f32[512,128]{1,0:T(8,128)S(1)} custom-call(f32[4,512,128]{2,1,0:T(8,128)} %all-to-all-done.2.parts_ref), custom_call_target="tpu_custom_call" | custom-call | flops 1000 | bytes 1000 | tf_op jit(solution)/shard_map/total/pallas_call | solution.py:315
  83.2 0.2 collective-permute-start.12
  83.4 2.2 %collective-permute-start.11 = (f32[512,128]{1,0:T(8,128)S(1)}, f32[512,128]{1,0:T(8,128)S(1)}, u32[]{:S(2)}, u32[]{:S(2)}) collective-permute-start(f32[512,128]{1,0:T(8,128)S(1)} %total.1.refs_2_.refs_3_), channel_id=1, source_target_pairs={{0,16},{8,24},{16,0},{24,8},{1,17},{9,25},{17,1},{25,9},{2,18},{10... | collective-permute-start | bytes 786440 | tf_op jit(solution)/shard_map/ppermute | solution.py:444
  85.6 1.1 collective-permute-start.10
  86.7 4.1 %stage.7 = (f32[512,512]{1,0:T(8,128)S(1)}, f32[512,512]{1,0:T(8,128)S(1)}) custom-call(f32[512,512]{1,0:T(8,128)S(1)} %get-tuple-element.23.refs_0_, f32[512,512]{1,0:T(8,128)S(1)} %get-tuple-element.24.refs_1_, f32[512,128]{1,0:T(8,128)S(1)} %total.1.refs_2_.refs_3_), custom_call_target="tpu_custom_call", output_to_operand_aliasing={{0}: (0, {}), {1}: (1, {})} | custom-call | flops 1000 | bytes 1000 | tf_op jit(solution)/shard_map/stage/pallas_call | solution.py:234
  90.8 2.1 %fusion.refs_1_ = f32[512,512]{1,0:T(8,128)S(1)} fusion(f32[512,512]{1,0:T(8,128)S(1)} %copy-done.1, f32[512,512]{1,0:T(8,128)S(1)} %get-tuple-element.25.refs_0_), kind=kOutput, calls=%fused_computation | convolution fusion | flops 1610612736 | bytes 3145728 | tf_op jit(solution)/shard_map/dot_general | solution.py:19
  92.9 1.2 %collective-permute-done.12.refs_4_ = f32[512,128]{1,0:T(8,128)S(1)} collective-permute-done((f32[512,128]{1,0:T(8,128)S(1)}, f32[512,128]{1,0:T(8,128)S(1)}, u32[]{:S(2)}, u32[]{:S(2)}) %collective-permute-start.12) | collective-permute-done | bytes 262176 | tf_op jit(solution)/shard_map/ppermute | solution.py:444
  94.1 3.7 %finish.2 = (f32[512,512]{1,0:T(8,128)}, f32[2,256,512]{2,1,0:T(8,128)}) custom-call(f32[512,512]{1,0:T(8,128)S(1)} %get-tuple-element.25.refs_0_, f32[512,512]{1,0:T(8,128)S(1)} %fusion.refs_1_, f32[8,2,32,512]{3,2,1,0:T(8,128)S(1)} %all-to-all-done.1.refs_2_, f32[512,128]{1,0:T(8,128)S(1)} %total.1.refs_2_.refs_3_, ...), custom_call_target="tpu_custom_call" | custom-call | flops 1000 | bytes 1000 | tf_op jit(solution)/shard_map/finish/pallas_call | solution.py:376
  97.8 5.7 %collective-permute-done.11.refs_4_ = f32[512,128]{1,0:T(8,128)S(1)} collective-permute-done((f32[512,128]{1,0:T(8,128)S(1)}, f32[512,128]{1,0:T(8,128)S(1)}, u32[]{:S(2)}, u32[]{:S(2)}) %collective-permute-start.11) | collective-permute-done | bytes 262176 | tf_op jit(solution)/shard_map/ppermute | solution.py:444
  103.5 6.1 %collective-permute-done.10.refs_3_ = f32[512,128]{1,0:T(8,128)S(1)} collective-permute-done((f32[512,128]{1,0:T(8,128)S(1)}, f32[512,128]{1,0:T(8,128)S(1)}, u32[]{:S(2)}, u32[]{:S(2)}) %collective-permute-start.10) | collective-permute-done | bytes 262176 | tf_op jit(solution)/shard_map/ppermute | solution.py:444
  109.7 3.7 %finish.3 = (f32[512,512]{1,0:T(8,128)}, f32[2,256,512]{2,1,0:T(8,128)}) custom-call(f32[512,512]{1,0:T(8,128)S(1)} %get-tuple-element.25.refs_0_, f32[512,512]{1,0:T(8,128)S(1)} %fusion.refs_1_, f32[8,2,32,512]{3,2,1,0:T(8,128)S(1)} %all-to-all-done.1.refs_2_, ...), custom_call_target="tpu_custom_call", output_to_operand_aliasing={{0}: (5, {}), {1}: (6, {})} | custom-call | flops 1000 | bytes 1000 | tf_op jit(solution)/shard_map/finish/pallas_call | solution.py:376
  (8 shorter events, 0.1 us)
Async XLA Ops:
  0.6 1.2 %copy-start.2 = (f32[2,256,512]{2,1,0:T(8,128)S(1)}, f32[2,256,512]{2,1,0:T(8,128)}, u32[]{:S(2)}) copy-start(f32[2,256,512]{2,1,0:T(8,128)} %children_ref.1) | copy-start | bytes 3145732
  2.6 18.0 %copy-start.3 = (s32[2,16]{1,0:T(2,128)S(1)}, s32[2,16]{1,0:T(2,128)}, u32[]{:S(2)}) copy-start(s32[2,16]{1,0:T(2,128)} %maps_ref.1) | copy-start | bytes 388
  22.8 6.4 %collective-permute-start = (f32[64,512]{1,0:T(8,128)S(1)}, f32[64,512]{1,0:T(8,128)S(1)}, u32[]{:S(2)}, u32[]{:S(2)}) collective-permute-start(f32[64,512]{1,0:T(8,128)S(1)} %get-tuple-element.15.refs_0_), channel_id=1, source_target_pairs={{0,2},{1,3},{2,0},{3,1},{4,6},{5,7},{6,4},{7,5},{8,10},{9,11},{10,... | collective-permute-start | bytes 393224 | tf_op jit(solution)/shard_map/ppermute | solution.py:399
  24.3 9.5 %collective-permute-start.2 = (f32[64,512]{1,0:T(8,128)S(1)}, f32[64,512]{1,0:T(8,128)S(1)}, u32[]{:S(2)}, u32[]{:S(2)}) collective-permute-start(f32[64,512]{1,0:T(8,128)S(1)} %get-tuple-element.15.refs_0_), channel_id=1, source_target_pairs={{0,6},{1,7},{2,4},{3,5},{4,2},{5,3},{6,0},{7,1},{8,14},{9,15},{10,... | collective-permute-start | bytes 393224 | tf_op jit(solution)/shard_map/ppermute | solution.py:399
  24.8 8.9 %collective-permute-start.1 = (f32[64,512]{1,0:T(8,128)S(1)}, f32[64,512]{1,0:T(8,128)S(1)}, u32[]{:S(2)}, u32[]{:S(2)}) collective-permute-start(f32[64,512]{1,0:T(8,128)S(1)} %get-tuple-element.15.refs_0_), channel_id=1, source_target_pairs={{0,4},{1,5},{2,6},{3,7},{4,0},{5,1},{6,2},{7,3},{8,12},{9,13},{10,... | collective-permute-start | bytes 393224 | tf_op jit(solution)/shard_map/ppermute | solution.py:399
  29.2 20.6 %all-to-all-start.1 = ((f32[8,2,32,512]{3,2,1,0:T(8,128)}), f32[8,2,32,512]{3,2,1,0:T(8,128)S(1)}, u32[]{:S(2)}, u32[]{:S(2)}) async-start(f32[8,2,32,512]{3,2,1,0:T(8,128)} %hold.1), calls=%async_computation.1 | async-start | bytes 2097152 | tf_op jit(solution)/shard_map/all_to_all | solution.py:426
  33.8 2.0 %collective-permute-start.3 = (f32[4,64,512]{2,1,0:T(8,128)S(1)}, f32[4,64,512]{2,1,0:T(8,128)S(1)}, u32[]{:S(2)}, u32[]{:S(2)}) collective-permute-start(f32[4,64,512]{2,1,0:T(8,128)S(1)} %stack.2.near_ref), channel_id=1, source_target_pairs={{0,1},{1,0},{2,3},{3,2},{4,5},{5,4},{6,7},{7,6},{8,9},{9,8},{10,11... | collective-permute-start | bytes 1572872 | tf_op jit(solution)/shard_map/ppermute | solution.py:428
  36.6 16.3 %copy-start = (f32[512,512]{1,0:T(8,128)}, f32[512,512]{1,0:T(8,128)S(1)}, u32[]{:S(2)}) copy-start(f32[512,512]{1,0:T(8,128)S(1)} %get-tuple-element.17.panels_ref) | copy-start | bytes 3145732
  36.6 5.6 %collective-permute-start.4 = (f32[256,128]{1,0:T(8,128)S(1)}, f32[256,128]{1,0:T(8,128)S(1)}, u32[]{:S(2)}, u32[]{:S(2)}) collective-permute-start(f32[256,128]{1,0:T(8,128)S(1)} %get-tuple-element.16), channel_id=1, source_target_pairs={{0,8},{8,0},{16,24},{24,16},{1,9},{9,1},{17,25},{25,17},{2,10},{10... | collective-permute-start | bytes 393224 | tf_op jit(solution)/shard_map/ppermute | solution.py:410
  42.2 7.6 %collective-permute-start.5 = (f32[256,128]{1,0:T(8,128)S(1)}, f32[256,128]{1,0:T(8,128)S(1)}, u32[]{:S(2)}, u32[]{:S(2)}) collective-permute-start(f32[256,128]{1,0:T(8,128)S(1)} %add.6), channel_id=1, source_target_pairs={{0,24},{8,16},{16,8},{24,0},{1,25},{9,17},{17,9},{25,1},{2,26},{10... | collective-permute-start | bytes 393224 | tf_op jit(solution)/shard_map/ppermute | solution.py:410
  52.9 29.0 %all-to-all-start.2 = ((f32[4,512,128]{2,1,0:T(8,128)}), f32[4,512,128]{2,1,0:T(8,128)}, u32[]{:S(2)}, u32[]{:S(2)}) async-start(f32[4,512,128]{2,1,0:T(8,128)} %multiply.1.refs_4_), calls=%async_computation.2 | async-start | bytes 2097152 | tf_op jit(solution)/shard_map/all_to_all | solution.py:434
  57.5 6.8 %collective-permute-start.8 = (f32[256,128]{1,0:T(8,128)S(1)}, f32[256,128]{1,0:T(8,128)S(1)}, u32[]{:S(2)}, u32[]{:S(2)}) collective-permute-start(f32[256,128]{1,0:T(8,128)S(1)} %add.7.refs_0_), channel_id=1, source_target_pairs={{0,6},{1,7},{2,4},{3,5},{4,2},{5,3},{6,0},{7,1},{8,14},{9,15},{10,... | collective-permute-start | bytes 393224 | tf_op jit(solution)/shard_map/ppermute | solution.py:399
  59.0 6.6 %collective-permute-start.7 = (f32[256,128]{1,0:T(8,128)S(1)}, f32[256,128]{1,0:T(8,128)S(1)}, u32[]{:S(2)}, u32[]{:S(2)}) collective-permute-start(f32[256,128]{1,0:T(8,128)S(1)} %add.7.refs_0_), channel_id=1, source_target_pairs={{0,4},{1,5},{2,6},{3,7},{4,0},{5,1},{6,2},{7,3},{8,12},{9,13},{10,... | collective-permute-start | bytes 393224 | tf_op jit(solution)/shard_map/ppermute | solution.py:399
  59.4 6.2 %collective-permute-start.6 = (f32[256,128]{1,0:T(8,128)S(1)}, f32[256,128]{1,0:T(8,128)S(1)}, u32[]{:S(2)}, u32[]{:S(2)}) collective-permute-start(f32[256,128]{1,0:T(8,128)S(1)} %add.7.refs_0_), channel_id=1, source_target_pairs={{0,2},{1,3},{2,0},{3,1},{4,6},{5,7},{6,4},{7,5},{8,10},{9,11},{10,... | collective-permute-start | bytes 393224 | tf_op jit(solution)/shard_map/ppermute | solution.py:399
  65.7 2.0 %collective-permute-start.9 = (f32[4,256,128]{2,1,0:T(8,128)S(1)}, f32[4,256,128]{2,1,0:T(8,128)S(1)}, u32[]{:S(2)}, u32[]{:S(2)}) collective-permute-start(f32[4,256,128]{2,1,0:T(8,128)S(1)} %stack.3.refs_0_), channel_id=1, source_target_pairs={{0,1},{1,0},{2,3},{3,2},{4,5},{5,4},{6,7},{7,6},{8,9},{9,8},{10,11... | collective-permute-start | bytes 1572872 | tf_op jit(solution)/shard_map/ppermute | solution.py:436
  83.2 10.9 %collective-permute-start.12 = (f32[512,128]{1,0:T(8,128)S(1)}, f32[512,128]{1,0:T(8,128)S(1)}, u32[]{:S(2)}, u32[]{:S(2)}) collective-permute-start(f32[512,128]{1,0:T(8,128)S(1)} %total.1.refs_2_.refs_3_), channel_id=1, source_target_pairs={{0,8},{8,0},{16,24},{24,16},{1,9},{9,1},{17,25},{25,17},{2,10},{10... | collective-permute-start | bytes 786440 | tf_op jit(solution)/shard_map/ppermute | solution.py:444
  83.4 20.1 %collective-permute-start.11 = (f32[512,128]{1,0:T(8,128)S(1)}, f32[512,128]{1,0:T(8,128)S(1)}, u32[]{:S(2)}, u32[]{:S(2)}) collective-permute-start(f32[512,128]{1,0:T(8,128)S(1)} %total.1.refs_2_.refs_3_), channel_id=1, source_target_pairs={{0,16},{8,24},{16,0},{24,8},{1,17},{9,25},{17,1},{25,9},{2,18},{10... | collective-permute-start | bytes 786440 | tf_op jit(solution)/shard_map/ppermute | solution.py:444
  85.6 24.1 %collective-permute-start.10 = (f32[512,128]{1,0:T(8,128)S(1)}, f32[512,128]{1,0:T(8,128)S(1)}, u32[]{:S(2)}, u32[]{:S(2)}) collective-permute-start(f32[512,128]{1,0:T(8,128)S(1)} %total.1.refs_2_.refs_3_), channel_id=1, source_target_pairs={{0,24},{8,16},{16,8},{24,0},{1,25},{9,17},{17,9},{25,1},{2,26},{10... | collective-permute-start | bytes 786440 | tf_op jit(solution)/shard_map/ppermute | solution.py:444
  86.7 4.1 %copy-start.1 = (f32[512,512]{1,0:T(8,128)S(1)}, f32[512,512]{1,0:T(8,128)}, u32[]{:S(2)}) copy-start(f32[512,512]{1,0:T(8,128)} %copy-done) | copy-start | bytes 3145732

commit v5 on v4

--- a/solution.py
+++ b/solution.py
@@ -115,40 +115,46 @@
     )(maps, spread)
 
 
-def tile_kernel(near_ref, far_ref, panels_ref, tile_ref):
+def lower_blocks(size):
+    return [(i, j) for i in range(size // LANES) for j in range(i + 1)]
+
+
+def tile_kernel(near_ref, far_ref, panels_ref, tile_ref, blocks_ref):
     me = lax.axis_index("col")
     half, part, both = near_ref.shape
     height = tile_ref.shape[0]
-    groups = both // height
     for i in range(half):
         for ref, k in ((near_ref, 2 * i), (far_ref, 2 * i + 1)):
             at = pl.multiple_of(lax.bitwise_xor(me, k) * part, part)
             panels_ref[pl.ds(at, part), :] = ref[i]
-    if height % LANES == 0:
-        left = panels_ref[:, pl.ds(pl.multiple_of(lax.rem(me, groups) * height, height), height)]
-    else:
-        per = LANES // height
-        group = lax.rem(me, groups)
-        wide = panels_ref[:, pl.ds(pl.multiple_of(lax.div(group, per) * LANES, LANES), LANES)]
-        left = wide[:, :height]
-        for step in range(1, per):
-            piece = wide[:, step * height : (step + 1) * height]
-            left = jnp.where(lax.rem(group, per) == step, piece, left)
-    right = panels_ref[:, pl.ds(pl.multiple_of(lax.div(me, groups) * LANES, LANES), LANES)]
-    tile_ref[...] = dot(left, right, ((0,), (0,)))
+    last = len(lower_blocks(both)) - 1
+    start = me * height
+    first = lax.div(start, LANES)
+    for n in range(2):
+        block = lax.min(first + n, last)
+        row = jnp.int32(0)
+        for i in range(1, both // LANES):
+            row = row + (block >= i * (i + 1) // 2).astype(jnp.int32)
+        lane = block - lax.div(row * (row + 1), 2)
+        left = panels_ref[:, pl.ds(pl.multiple_of(row * LANES, LANES), LANES)]
+        right = panels_ref[:, pl.ds(pl.multiple_of(lane * LANES, LANES), LANES)]
+        blocks_ref[n * LANES : (n + 1) * LANES, :] = dot(left, right, ((0,), (0,)))
+    offset = pl.multiple_of(start - first * LANES, SUBS)
+    tile_ref[...] = blocks_ref[pl.ds(offset, height), :]
 
 
 def gram_tile(near, far):
     half, part, both = near.shape
-    height = both * both // (2 * half * LANES)
-    rows_dev = 2 * half * part
+    height = len(lower_blocks(both)) * LANES // (2 * half)
     return pl.pallas_call(
         tile_kernel,
-        out_shape=(shape(rows_dev, both), shape(height, LANES)),
+        out_shape=(shape(2 * half * part, both), shape(height, LANES)),
         in_specs=[VMEM, VMEM],
         out_specs=(VMEM, VMEM),
-        compiler_params=KERNEL,
-        cost_estimate=cost(1000, 1000),
+        scratch_shapes=[pltpu.VMEM((2 * LANES, LANES), F32)],
+        compiler_params=KERNEL,
+        cost_estimate=cost(2_200_000_000, 1000),
+        name="tile",
     )(near, far)
 
 
@@ -205,38 +211,45 @@
 
 
 def stage_kernel(lo, *refs):
-    a_ref, out_ref = refs[-2:]
-    size, hi = a_ref.shape[0], lo + LANES
     if lo == 0:
+        near_ref, far_ref, a_ref, out_ref, packed_ref = refs
+        size = a_ref.shape[0]
         me = lax.axis_index("col")
-        near_ref, far_ref = refs[:2]
         half, height, _ = near_ref.shape
-        groups = size // height
         for i in range(half):
             for ref, k in ((near_ref, 2 * i), (far_ref, 2 * i + 1)):
-                at = lax.bitwise_xor(me, k)
-                row = pl.multiple_of(lax.rem(at, groups) * height, height)
-                lane = pl.multiple_of(lax.div(at, groups) * LANES, LANES)
-                a_ref[pl.ds(row, height), pl.ds(lane, LANES)] = ref[i]
+                at = pl.multiple_of(lax.bitwise_xor(me, k) * height, SUBS)
+                packed_ref[pl.ds(at, height), :] = ref[i]
+        a_ref[...] = jnp.zeros_like(a_ref)
         out_ref[...] = jnp.zeros_like(out_ref)
+        for n, (i, j) in enumerate(lower_blocks(size)):
+            a_ref[i * LANES : (i + 1) * LANES, j * LANES : (j + 1) * LANES] = packed_ref[
+                n * LANES : (n + 1) * LANES, :
+            ]
+    else:
+        a_ref, out_ref = refs[-2:]
+        size = a_ref.shape[0]
+    hi = lo + LANES
     factor_inverse(lo, a_ref, out_ref)
     inv = out_ref[lo:hi, lo:hi]
     if lo > 0:
         out_ref[lo:hi, :lo] = dot(inv, out_ref[lo:hi, :lo], ((1,), (0,)))
     if hi < size:
-        right = dot(inv, a_ref[lo:hi, hi:], ((1,), (0,)))
-        a_ref[hi:, hi:] = a_ref[hi:, hi:] - dot(right, right, ((0,), (0,)))
-        out_ref[hi:, :hi] = out_ref[hi:, :hi] - dot(right, out_ref[lo:hi, :hi], ((0,), (0,)))
+        below = dot(a_ref[hi:, lo:hi], inv, ((1,), (1,)))
+        a_ref[hi:, hi:] = a_ref[hi:, hi:] - dot(below, below, ((1,), (1,)))
+        out_ref[hi:, :hi] = out_ref[hi:, :hi] - dot(below, out_ref[lo:hi, :hi], ((1,), (0,)))
 
 
 def stage(lo, state, after=()):
     size = 2 * PANEL
+    rows = len(lower_blocks(size)) * LANES
     return pl.pallas_call(
         lambda *refs: stage_kernel(lo, *refs),
         out_shape=(shape(size, size), shape(size, size)),
         in_specs=[VMEM, VMEM] + [ANY] * len(after),
         out_specs=(VMEM, VMEM),
         input_output_aliases={0: 0, 1: 1} if lo > 0 else {},
+        scratch_shapes=[pltpu.VMEM((rows, LANES), F32)] if lo == 0 else [],
         compiler_params=KERNEL,
         cost_estimate=cost(1000, 1000),
         name="stage",
@@ -423,7 +436,7 @@
     spread = lax.all_to_all(pack(children, cols), "col", 0, 0, tiled=True)
     ordered, mine = order(spread, block_maps)
     pieces = even_pieces(mine, cols)
-    front = lax.all_to_all(hold(ordered, pieces[1:2]), "col", 0, 0, tiled=True)
+    front = lax.all_to_all(ordered, "col", 0, 0, tiled=True)
     near = stack_after(pieces, [])
     panels, tile = gram_tile(near, lax.ppermute(near, "col", pairs_xor(cols, 1)))
     tile = sum_row_small(tile, rows)

time: 114 us -> 109 us (0.956)
  waiting for transfers between devices: 35.3 us -> 28.7 us
  starting transfers between devices: 22.2 us -> 23.9 us
    ppermute x6, waiting for transfers between devices: 7.54 us -> 4.09 us  [even_pieces(): lax.ppermute(piece, 'col', pairs_xor(size, k))]
    ppermute x2, waiting for transfers between devices: 11 us -> 7.87 us  [sum_row_small(): value = value + lax.ppermute(value, 'row', pairs_xor(size, span - 1))]
  transfers between devices with their start and end apart: 15 -> 15, of which waited for: 11 -> 12; matrix products, arithmetic and copies ran while one was open for 2% -> 2% of each run, Pallas kernels for 20% -> 21%
where the time goes in v5:
time: 109 us
  Pallas kernels  33.9 us (31%)
  waiting for transfers between devices  28.7 us (26%)
  starting transfers between devices  23.9 us (22%)
  blocking collectives  18 us (17%)
  matrix products  1.86 us (2%)
  local copies, waits for them, and re-layouts  1.23 us (1%)
    pallas_call x4, Pallas kernels, stage(): pl.pallas_call(lambda *refs: stage_kernel(lo, *refs), out_shape=(shape(si...  18.5 us
    all_to_all x1, blocking collectives, per_device(): spread = lax.all_to_all(pack(children, cols), 'col', 0, 0, tiled=True)  18 us
    ppermute x3, waiting for transfers between devices, per_device(): lax.ppermute(mine, 'row', pairs_xor(rows, k))  12.3 us
    ppermute x2, waiting for transfers between devices, sum_row_small(): value = value + lax.ppermute(value, 'row', pairs_xor(size, span - 1))  7.87 us
    pallas_call x2, Pallas kernels, finish(): pl.pallas_call(lambda *refs: finish_kernel(masks, *refs), out_shape=(shap...  7.43 us
    ppermute x6, starting transfers between devices, even_pieces(): lax.ppermute(piece, 'col', pairs_xor(size, k))  7.04 us
    all_to_all x1, starting transfers between devices, per_device(): parts = lax.all_to_all(products, 'row', 0, 0, tiled=True)  5.33 us
    all_to_all x1, starting transfers between devices, per_device(): front = lax.all_to_all(ordered, 'col', 0, 0, tiled=True)  4.93 us
  transfers between devices with their start and end apart: 15, of which 12 were waited for; matrix products, arithmetic and copies ran while one was open for 2% of the time, Pallas kernels for 21%

profile of v5, /device:TPU:10, one launch (start us, length us, event | category | flops | bytes accessed | tf_op | source)
XLA Modules:
  0.0 108.5 jit_solution(4428368270279158532)
XLA Ops:
  0.6 0.0 copy-start.2
  0.6 1.2 %copy-done.2 = f32[2,256,512]{2,1,0:T(8,128)S(1)} copy-done((f32[2,256,512]{2,1,0:T(8,128)S(1)}, f32[2,256,512]{2,1,0:T(8,128)}, u32[]{:S(2)}) %copy-start.2) | copy-done | bytes 1048600
  1.9 0.7 shard_map.41
  2.6 0.0 copy-start.3
  2.6 18.0 %all_to_all.15.spread_ref = f32[8,2,32,512]{3,2,1,0:T(8,128)S(1)} all-to-all(f32[8,2,32,512]{3,2,1,0:T(8,128)S(1)} %shard_map.41), channel_id=1, replica_groups=mesh['row'=4,'col'=8] {'col'}, dimensions={0} | all-to-all | bytes 2097152 | tf_op jit(solution)/shard_map/all_to_all | solution.py:436
  20.6 0.0 copy-done.3
  20.6 2.2 %order.1 = (f32[8,2,32,512]{3,2,1,0:T(8,128)}, f32[64,512]{1,0:T(8,128)S(1)}) custom-call(s32[2,16]{1,0:T(2,128)S(1)} %copy-done.3, f32[8,2,32,512]{3,2,1,0:T(8,128)S(1)} %all_to_all.15.spread_ref), custom_call_target="tpu_custom_call" | custom-call | flops 1000 | bytes 1000 | tf_op jit(solution)/shard_map/order/pallas_call | solution.py:103
  22.8 1.5 %collective-permute-start.2 = (f32[64,512]{1,0:T(8,128)S(1)}, f32[64,512]{1,0:T(8,128)S(1)}, u32[]{:S(2)}, u32[]{:S(2)}) collective-permute-start(f32[64,512]{1,0:T(8,128)S(1)} %get-tuple-element.15.refs_0_), channel_id=1, source_target_pairs={{0,6},{1,7},{2,4},{3,5},{4,2},{5,3},{6,0},{7,1},{8,14},{9,15},{10,... | collective-permute-start | bytes 393224 | tf_op jit(solution)/shard_map/ppermute | solution.py:412
  24.3 1.5 %collective-permute-start.1 = (f32[64,512]{1,0:T(8,128)S(1)}, f32[64,512]{1,0:T(8,128)S(1)}, u32[]{:S(2)}, u32[]{:S(2)}) collective-permute-start(f32[64,512]{1,0:T(8,128)S(1)} %get-tuple-element.15.refs_0_), channel_id=1, source_target_pairs={{0,4},{1,5},{2,6},{3,7},{4,0},{5,1},{6,2},{7,3},{8,12},{9,13},{10,... | collective-permute-start | bytes 393224 | tf_op jit(solution)/shard_map/ppermute | solution.py:412
  25.7 0.6 collective-permute-start
  26.3 4.9 %all-to-all-start.1 = ((f32[8,2,32,512]{3,2,1,0:T(8,128)}), f32[8,2,32,512]{3,2,1,0:T(8,128)S(1)}, u32[]{:S(2)}, u32[]{:S(2)}) async-start(f32[8,2,32,512]{3,2,1,0:T(8,128)} %get-tuple-element.18), calls=%async_computation.1 | async-start | bytes 2097152 | tf_op jit(solution)/shard_map/all_to_all | solution.py:439
  31.2 0.0 collective-permute-done.2.refs_3_
  31.2 0.2 collective-permute-done.1.refs_2_
  31.4 0.0 collective-permute-done.refs_1_
  31.4 0.1 collective-permute-start.3
  31.5 1.9 %collective-permute-done.3.far_ref = f32[4,64,512]{2,1,0:T(8,128)S(1)} collective-permute-done((f32[4,64,512]{2,1,0:T(8,128)S(1)}, f32[4,64,512]{2,1,0:T(8,128)S(1)}, u32[]{:S(2)}, u32[]{:S(2)}) %collective-permute-start.3) | collective-permute-done | bytes 524320 | tf_op jit(solution)/shard_map/ppermute | solution.py:441
  33.4 0.7 tile.1
  34.1 0.0 copy-start
  34.2 0.5 collective-permute-start.4
  34.7 4.0 %collective-permute-done.4 = f32[160,128]{1,0:T(8,128)S(1)} collective-permute-done((f32[160,128]{1,0:T(8,128)S(1)}, f32[160,128]{1,0:T(8,128)S(1)}, u32[]{:S(2)}, u32[]{:S(2)}) %collective-permute-start.4) | collective-permute-done | bytes 81952 | tf_op jit(solution)/shard_map/ppermute | solution.py:423
  38.7 1.6 %collective-permute-start.5 = (f32[160,128]{1,0:T(8,128)S(1)}, f32[160,128]{1,0:T(8,128)S(1)}, u32[]{:S(2)}, u32[]{:S(2)}) collective-permute-start(f32[160,128]{1,0:T(8,128)S(1)} %add.6), channel_id=1, source_target_pairs={{0,24},{8,16},{16,8},{24,0},{1,25},{9,17},{17,9},{25,1},{2,26},{10... | collective-permute-start | bytes 245768 | tf_op jit(solution)/shard_map/ppermute | solution.py:423
  40.4 3.8 %collective-permute-done.5 = f32[160,128]{1,0:T(8,128)S(1)} collective-permute-done((f32[160,128]{1,0:T(8,128)S(1)}, f32[160,128]{1,0:T(8,128)S(1)}, u32[]{:S(2)}, u32[]{:S(2)}) %collective-permute-start.5) | collective-permute-done | bytes 81952 | tf_op jit(solution)/shard_map/ppermute | solution.py:423
  44.2 0.9 all-to-all-done.1.refs_2_
  45.2 3.0 %multiply.1.refs_4_ = f32[4,512,128]{2,1,0:T(8,128)} custom-call(f32[512,512]{1,0:T(8,128)S(1)} %get-tuple-element.17.panels_ref, f32[512,512]{1,0:T(8,128)S(1)} %bitcast.3, f32[160,128]{1,0:T(8,128)S(1)} %add.7.refs_0_), custom_call_target="tpu_custom_call" | custom-call | flops 1000 | bytes 1000 | tf_op jit(solution)/shard_map/multiply/pallas_call | solution.py:295
  48.2 5.3 %all-to-all-start.2 = ((f32[4,512,128]{2,1,0:T(8,128)}), f32[4,512,128]{2,1,0:T(8,128)}, u32[]{:S(2)}, u32[]{:S(2)}) async-start(f32[4,512,128]{2,1,0:T(8,128)} %multiply.1.refs_4_), calls=%async_computation.2 | async-start | bytes 2097152 | tf_op jit(solution)/shard_map/all_to_all | solution.py:447
  53.5 1.5 %collective-permute-start.8 = (f32[160,128]{1,0:T(8,128)S(1)}, f32[160,128]{1,0:T(8,128)S(1)}, u32[]{:S(2)}, u32[]{:S(2)}) collective-permute-start(f32[160,128]{1,0:T(8,128)S(1)} %add.7.refs_0_), channel_id=1, source_target_pairs={{0,6},{1,7},{2,4},{3,5},{4,2},{5,3},{6,0},{7,1},{8,14},{9,15},{10,... | collective-permute-start | bytes 245768 | tf_op jit(solution)/shard_map/ppermute | solution.py:412
  55.0 1.5 %collective-permute-start.7 = (f32[160,128]{1,0:T(8,128)S(1)}, f32[160,128]{1,0:T(8,128)S(1)}, u32[]{:S(2)}, u32[]{:S(2)}) collective-permute-start(f32[160,128]{1,0:T(8,128)S(1)} %add.7.refs_0_), channel_id=1, source_target_pairs={{0,4},{1,5},{2,6},{3,7},{4,0},{5,1},{6,2},{7,3},{8,12},{9,13},{10,... | collective-permute-start | bytes 245768 | tf_op jit(solution)/shard_map/ppermute | solution.py:412
  56.5 0.5 collective-permute-start.6
  57.0 2.2 %collective-permute-done.8.refs_3_ = f32[160,128]{1,0:T(8,128)S(1)} collective-permute-done((f32[160,128]{1,0:T(8,128)S(1)}, f32[160,128]{1,0:T(8,128)S(1)}, u32[]{:S(2)}, u32[]{:S(2)}) %collective-permute-start.8) | collective-permute-done | bytes 81952 | tf_op jit(solution)/shard_map/ppermute | solution.py:412
  59.2 0.8 collective-permute-done.7.refs_2_
  60.0 0.9 collective-permute-done.6.refs_1_
  60.9 0.1 collective-permute-start.9
  61.0 1.6 %collective-permute-done.9.refs_1_ = f32[4,160,128]{2,1,0:T(8,128)S(1)} collective-permute-done((f32[4,160,128]{2,1,0:T(8,128)S(1)}, f32[4,160,128]{2,1,0:T(8,128)S(1)}, u32[]{:S(2)}, u32[]{:S(2)}) %collective-permute-start.9) | collective-permute-done | bytes 327712 | tf_op jit(solution)/shard_map/ppermute | solution.py:449
  62.6 4.9 %stage.4 = (f32[512,512]{1,0:T(8,128)S(1)}, f32[512,512]{1,0:T(8,128)S(1)}) custom-call(f32[4,160,128]{2,1,0:T(8,128)S(1)} %stack.3.refs_0_, f32[4,160,128]{2,1,0:T(8,128)S(1)} %collective-permute-done.9.refs_1_), custom_call_target="tpu_custom_call" | custom-call | flops 1000 | bytes 1000 | tf_op jit(solution)/shard_map/stage/pallas_call | solution.py:246
  67.6 4.7 %stage.5 = (f32[512,512]{1,0:T(8,128)S(1)}, f32[512,512]{1,0:T(8,128)S(1)}) custom-call(f32[512,512]{1,0:T(8,128)S(1)} %get-tuple-element.19.refs_0_, f32[512,512]{1,0:T(8,128)S(1)} %get-tuple-element.20.refs_1_), custom_call_target="tpu_custom_call", output_to_operand_aliasing={{0}: (0, {}), {1}: (1, {})} | custom-call | flops 1000 | bytes 1000 | tf_op jit(solution)/shard_map/stage/pallas_call | solution.py:246
  72.3 4.5 %stage.6 = (f32[512,512]{1,0:T(8,128)S(1)}, f32[512,512]{1,0:T(8,128)S(1)}) custom-call(f32[512,512]{1,0:T(8,128)S(1)} %get-tuple-element.21.refs_0_, f32[512,512]{1,0:T(8,128)S(1)} %get-tuple-element.22.refs_1_), custom_call_target="tpu_custom_call", output_to_operand_aliasing={{0}: (0, {}), {1}: (1, {})} | custom-call | flops 1000 | bytes 1000 | tf_op jit(solution)/shard_map/stage/pallas_call | solution.py:246
  76.9 0.0 all-to-all-done.2.parts_ref
  76.9 1.3 %total.1.refs_2_.refs_3_ = f32[512,128]{1,0:T(8,128)S(1)} custom-call(f32[4,512,128]{2,1,0:T(8,128)} %all-to-all-done.2.parts_ref), custom_call_target="tpu_custom_call" | custom-call | flops 1000 | bytes 1000 | tf_op jit(solution)/shard_map/total/pallas_call | solution.py:328
  78.2 2.7 %collective-permute-start.12 = (f32[512,128]{1,0:T(8,128)S(1)}, f32[512,128]{1,0:T(8,128)S(1)}, u32[]{:S(2)}, u32[]{:S(2)}) collective-permute-start(f32[512,128]{1,0:T(8,128)S(1)} %total.1.refs_2_.refs_3_), channel_id=1, source_target_pairs={{0,8},{8,0},{16,24},{24,16},{1,9},{9,1},{17,25},{25,17},{2,10},{10... | collective-permute-start | bytes 786440 | tf_op jit(solution)/shard_map/ppermute | solution.py:457
  80.9 0.2 collective-permute-start.11
  81.1 1.3 %collective-permute-start.10 = (f32[512,128]{1,0:T(8,128)S(1)}, f32[512,128]{1,0:T(8,128)S(1)}, u32[]{:S(2)}, u32[]{:S(2)}) collective-permute-start(f32[512,128]{1,0:T(8,128)S(1)} %total.1.refs_2_.refs_3_), channel_id=1, source_target_pairs={{0,24},{8,16},{16,8},{24,0},{1,25},{9,17},{17,9},{25,1},{2,26},{10... | collective-permute-start | bytes 786440 | tf_op jit(solution)/shard_map/ppermute | solution.py:457
  82.4 4.3 %stage.7 = (f32[512,512]{1,0:T(8,128)S(1)}, f32[512,512]{1,0:T(8,128)S(1)}) custom-call(f32[512,512]{1,0:T(8,128)S(1)} %get-tuple-element.23.refs_0_, f32[512,512]{1,0:T(8,128)S(1)} %get-tuple-element.24.refs_1_, f32[512,128]{1,0:T(8,128)S(1)} %total.1.refs_2_.refs_3_), custom_call_target="tpu_custom_call", output_to_operand_aliasing={{0}: (0, {}), {1}: (1, {})} | custom-call | flops 1000 | bytes 1000 | tf_op jit(solution)/shard_map/stage/pallas_call | solution.py:246
  86.8 1.9 %fusion.refs_1_ = f32[512,512]{1,0:T(8,128)S(1)} fusion(f32[512,512]{1,0:T(8,128)S(1)} %copy-done.1, f32[512,512]{1,0:T(8,128)S(1)} %get-tuple-element.25.refs_0_), kind=kOutput, calls=%fused_computation | convolution fusion | flops 1610612736 | bytes 3145728 | tf_op jit(solution)/shard_map/dot_general | solution.py:19
  88.6 1.7 %collective-permute-done.12.refs_4_ = f32[512,128]{1,0:T(8,128)S(1)} collective-permute-done((f32[512,128]{1,0:T(8,128)S(1)}, f32[512,128]{1,0:T(8,128)S(1)}, u32[]{:S(2)}, u32[]{:S(2)}) %collective-permute-start.12) | collective-permute-done | bytes 262176 | tf_op jit(solution)/shard_map/ppermute | solution.py:457
  90.3 3.7 %finish.2 = (f32[512,512]{1,0:T(8,128)}, f32[2,256,512]{2,1,0:T(8,128)}) custom-call(f32[512,512]{1,0:T(8,128)S(1)} %get-tuple-element.25.refs_0_, f32[512,512]{1,0:T(8,128)S(1)} %fusion.refs_1_, f32[8,2,32,512]{3,2,1,0:T(8,128)S(1)} %all-to-all-done.1.refs_2_, f32[512,128]{1,0:T(8,128)S(1)} %total.1.refs_2_.refs_3_, ...), custom_call_target="tpu_custom_call" | custom-call | flops 1000 | bytes 1000 | tf_op jit(solution)/shard_map/finish/pallas_call | solution.py:389
  94.0 5.1 %collective-permute-done.11.refs_4_ = f32[512,128]{1,0:T(8,128)S(1)} collective-permute-done((f32[512,128]{1,0:T(8,128)S(1)}, f32[512,128]{1,0:T(8,128)S(1)}, u32[]{:S(2)}, u32[]{:S(2)}) %collective-permute-start.11) | collective-permute-done | bytes 262176 | tf_op jit(solution)/shard_map/ppermute | solution.py:457
  99.1 5.6 %collective-permute-done.10.refs_3_ = f32[512,128]{1,0:T(8,128)S(1)} collective-permute-done((f32[512,128]{1,0:T(8,128)S(1)}, f32[512,128]{1,0:T(8,128)S(1)}, u32[]{:S(2)}, u32[]{:S(2)}) %collective-permute-start.10) | collective-permute-done | bytes 262176 | tf_op jit(solution)/shard_map/ppermute | solution.py:457
  104.6 3.7 %finish.3 = (f32[512,512]{1,0:T(8,128)}, f32[2,256,512]{2,1,0:T(8,128)}) custom-call(f32[512,512]{1,0:T(8,128)S(1)} %get-tuple-element.25.refs_0_, f32[512,512]{1,0:T(8,128)S(1)} %fusion.refs_1_, f32[8,2,32,512]{3,2,1,0:T(8,128)S(1)} %all-to-all-done.1.refs_2_, ...), custom_call_target="tpu_custom_call", output_to_operand_aliasing={{0}: (5, {}), {1}: (6, {})} | custom-call | flops 1000 | bytes 1000 | tf_op jit(solution)/shard_map/finish/pallas_call | solution.py:389
  (7 shorter events, 0.1 us)
Async XLA Ops:
  0.6 1.2 %copy-start.2 = (f32[2,256,512]{2,1,0:T(8,128)S(1)}, f32[2,256,512]{2,1,0:T(8,128)}, u32[]{:S(2)}) copy-start(f32[2,256,512]{2,1,0:T(8,128)} %children_ref.1) | copy-start | bytes 3145732
  2.6 18.0 %copy-start.3 = (s32[2,16]{1,0:T(2,128)S(1)}, s32[2,16]{1,0:T(2,128)}, u32[]{:S(2)}) copy-start(s32[2,16]{1,0:T(2,128)} %maps_ref.1) | copy-start | bytes 388
  22.8 8.5 %collective-permute-start.2 = (f32[64,512]{1,0:T(8,128)S(1)}, f32[64,512]{1,0:T(8,128)S(1)}, u32[]{:S(2)}, u32[]{:S(2)}) collective-permute-start(f32[64,512]{1,0:T(8,128)S(1)} %get-tuple-element.15.refs_0_), channel_id=1, source_target_pairs={{0,6},{1,7},{2,4},{3,5},{4,2},{5,3},{6,0},{7,1},{8,14},{9,15},{10,... | collective-permute-start | bytes 393224 | tf_op jit(solution)/shard_map/ppermute | solution.py:412
  24.3 7.1 %collective-permute-start.1 = (f32[64,512]{1,0:T(8,128)S(1)}, f32[64,512]{1,0:T(8,128)S(1)}, u32[]{:S(2)}, u32[]{:S(2)}) collective-permute-start(f32[64,512]{1,0:T(8,128)S(1)} %get-tuple-element.15.refs_0_), channel_id=1, source_target_pairs={{0,4},{1,5},{2,6},{3,7},{4,0},{5,1},{6,2},{7,3},{8,12},{9,13},{10,... | collective-permute-start | bytes 393224 | tf_op jit(solution)/shard_map/ppermute | solution.py:412
  25.7 5.7 %collective-permute-start = (f32[64,512]{1,0:T(8,128)S(1)}, f32[64,512]{1,0:T(8,128)S(1)}, u32[]{:S(2)}, u32[]{:S(2)}) collective-permute-start(f32[64,512]{1,0:T(8,128)S(1)} %get-tuple-element.15.refs_0_), channel_id=1, source_target_pairs={{0,2},{1,3},{2,0},{3,1},{4,6},{5,7},{6,4},{7,5},{8,10},{9,11},{10,... | collective-permute-start | bytes 393224 | tf_op jit(solution)/shard_map/ppermute | solution.py:412
  26.3 18.8 %all-to-all-start.1 = ((f32[8,2,32,512]{3,2,1,0:T(8,128)}), f32[8,2,32,512]{3,2,1,0:T(8,128)S(1)}, u32[]{:S(2)}, u32[]{:S(2)}) async-start(f32[8,2,32,512]{3,2,1,0:T(8,128)} %get-tuple-element.18), calls=%async_computation.1 | async-start | bytes 2097152 | tf_op jit(solution)/shard_map/all_to_all | solution.py:439
  31.4 2.0 %collective-permute-start.3 = (f32[4,64,512]{2,1,0:T(8,128)S(1)}, f32[4,64,512]{2,1,0:T(8,128)S(1)}, u32[]{:S(2)}, u32[]{:S(2)}) collective-permute-start(f32[4,64,512]{2,1,0:T(8,128)S(1)} %stack.2.near_ref), channel_id=1, source_target_pairs={{0,1},{1,0},{2,3},{3,2},{4,5},{5,4},{6,7},{7,6},{8,9},{9,8},{10,11... | collective-permute-start | bytes 1572872 | tf_op jit(solution)/shard_map/ppermute | solution.py:441
  34.1 14.0 %copy-start = (f32[512,512]{1,0:T(8,128)}, f32[512,512]{1,0:T(8,128)S(1)}, u32[]{:S(2)}) copy-start(f32[512,512]{1,0:T(8,128)S(1)} %get-tuple-element.17.panels_ref) | copy-start | bytes 3145732
  34.2 4.6 %collective-permute-start.4 = (f32[160,128]{1,0:T(8,128)S(1)}, f32[160,128]{1,0:T(8,128)S(1)}, u32[]{:S(2)}, u32[]{:S(2)}) collective-permute-start(f32[160,128]{1,0:T(8,128)S(1)} %get-tuple-element.16), channel_id=1, source_target_pairs={{0,8},{8,0},{16,24},{24,16},{1,9},{9,1},{17,25},{25,17},{2,10},{10... | collective-permute-start | bytes 245768 | tf_op jit(solution)/shard_map/ppermute | solution.py:423
  38.7 5.5 %collective-permute-start.5 = (f32[160,128]{1,0:T(8,128)S(1)}, f32[160,128]{1,0:T(8,128)S(1)}, u32[]{:S(2)}, u32[]{:S(2)}) collective-permute-start(f32[160,128]{1,0:T(8,128)S(1)} %add.6), channel_id=1, source_target_pairs={{0,24},{8,16},{16,8},{24,0},{1,25},{9,17},{17,9},{25,1},{2,26},{10... | collective-permute-start | bytes 245768 | tf_op jit(solution)/shard_map/ppermute | solution.py:423
  48.2 28.7 %all-to-all-start.2 = ((f32[4,512,128]{2,1,0:T(8,128)}), f32[4,512,128]{2,1,0:T(8,128)}, u32[]{:S(2)}, u32[]{:S(2)}) async-start(f32[4,512,128]{2,1,0:T(8,128)} %multiply.1.refs_4_), calls=%async_computation.2 | async-start | bytes 2097152 | tf_op jit(solution)/shard_map/all_to_all | solution.py:447
  53.5 5.7 %collective-permute-start.8 = (f32[160,128]{1,0:T(8,128)S(1)}, f32[160,128]{1,0:T(8,128)S(1)}, u32[]{:S(2)}, u32[]{:S(2)}) collective-permute-start(f32[160,128]{1,0:T(8,128)S(1)} %add.7.refs_0_), channel_id=1, source_target_pairs={{0,6},{1,7},{2,4},{3,5},{4,2},{5,3},{6,0},{7,1},{8,14},{9,15},{10,... | collective-permute-start | bytes 245768 | tf_op jit(solution)/shard_map/ppermute | solution.py:412
  55.0 5.0 %collective-permute-start.7 = (f32[160,128]{1,0:T(8,128)S(1)}, f32[160,128]{1,0:T(8,128)S(1)}, u32[]{:S(2)}, u32[]{:S(2)}) collective-permute-start(f32[160,128]{1,0:T(8,128)S(1)} %add.7.refs_0_), channel_id=1, source_target_pairs={{0,4},{1,5},{2,6},{3,7},{4,0},{5,1},{6,2},{7,3},{8,12},{9,13},{10,... | collective-permute-start | bytes 245768 | tf_op jit(solution)/shard_map/ppermute | solution.py:412
  56.5 4.4 %collective-permute-start.6 = (f32[160,128]{1,0:T(8,128)S(1)}, f32[160,128]{1,0:T(8,128)S(1)}, u32[]{:S(2)}, u32[]{:S(2)}) collective-permute-start(f32[160,128]{1,0:T(8,128)S(1)} %add.7.refs_0_), channel_id=1, source_target_pairs={{0,2},{1,3},{2,0},{3,1},{4,6},{5,7},{6,4},{7,5},{8,10},{9,11},{10,... | collective-permute-start | bytes 245768 | tf_op jit(solution)/shard_map/ppermute | solution.py:412
  60.9 1.7 %collective-permute-start.9 = (f32[4,160,128]{2,1,0:T(8,128)S(1)}, f32[4,160,128]{2,1,0:T(8,128)S(1)}, u32[]{:S(2)}, u32[]{:S(2)}) collective-permute-start(f32[4,160,128]{2,1,0:T(8,128)S(1)} %stack.3.refs_0_), channel_id=1, source_target_pairs={{0,1},{1,0},{2,3},{3,2},{4,5},{5,4},{6,7},{7,6},{8,9},{9,8},{10,11... | collective-permute-start | bytes 983048 | tf_op jit(solution)/shard_map/ppermute | solution.py:449
  78.2 12.1 %collective-permute-start.12 = (f32[512,128]{1,0:T(8,128)S(1)}, f32[512,128]{1,0:T(8,128)S(1)}, u32[]{:S(2)}, u32[]{:S(2)}) collective-permute-start(f32[512,128]{1,0:T(8,128)S(1)} %total.1.refs_2_.refs_3_), channel_id=1, source_target_pairs={{0,8},{8,0},{16,24},{24,16},{1,9},{9,1},{17,25},{25,17},{2,10},{10... | collective-permute-start | bytes 786440 | tf_op jit(solution)/shard_map/ppermute | solution.py:457
  80.9 18.2 %collective-permute-start.11 = (f32[512,128]{1,0:T(8,128)S(1)}, f32[512,128]{1,0:T(8,128)S(1)}, u32[]{:S(2)}, u32[]{:S(2)}) collective-permute-start(f32[512,128]{1,0:T(8,128)S(1)} %total.1.refs_2_.refs_3_), channel_id=1, source_target_pairs={{0,16},{8,24},{16,0},{24,8},{1,17},{9,25},{17,1},{25,9},{2,18},{10... | collective-permute-start | bytes 786440 | tf_op jit(solution)/shard_map/ppermute | solution.py:457
  81.1 23.5 %collective-permute-start.10 = (f32[512,128]{1,0:T(8,128)S(1)}, f32[512,128]{1,0:T(8,128)S(1)}, u32[]{:S(2)}, u32[]{:S(2)}) collective-permute-start(f32[512,128]{1,0:T(8,128)S(1)} %total.1.refs_2_.refs_3_), channel_id=1, source_target_pairs={{0,24},{8,16},{16,8},{24,0},{1,25},{9,17},{17,9},{25,1},{2,26},{10... | collective-permute-start | bytes 786440 | tf_op jit(solution)/shard_map/ppermute | solution.py:457
  82.4 4.3 %copy-start.1 = (f32[512,512]{1,0:T(8,128)S(1)}, f32[512,512]{1,0:T(8,128)}, u32[]{:S(2)}) copy-start(f32[512,512]{1,0:T(8,128)} %copy-done) | copy-start | bytes 3145732

commit v6 on v5

--- a/solution.py
+++ b/solution.py
@@ -65,50 +65,27 @@
     )(children)
 
 
-def order_kernel(maps_ref, spread_ref, out_ref, mine_ref, sems, mine_sems):
+def order_kernel(maps_ref, spread_ref, out_ref, mine_ref):
     owners, _, part, width = out_ref.shape
     per = width // PANEL
-    copies = []
     for child in range(2):
         for block in range(owners * per):
             to = maps_ref[child, block]
-            from_lane = (block % per) * PANEL
-            to_lane = pl.multiple_of(lax.rem(to, per) * PANEL, PANEL)
-            source = spread_ref.at[block // per, child, :, pl.ds(from_lane, PANEL)]
-            copies.append(
-                pltpu.make_async_copy(
-                    source,
-                    out_ref.at[lax.div(to, per), child, :, pl.ds(to_lane, PANEL)],
-                    sems.at[child, block],
-                )
-            )
-
-            @pl.when(to < 2)
-            def _():
-                pltpu.make_async_copy(
-                    source,
-                    mine_ref.at[pl.ds(child * part, part), pl.ds(to_lane, PANEL)],
-                    mine_sems.at[child, to],
-                ).start()
-
-    run_copies(copies)
-    for child in range(2):
-        for panel in range(2):
-            piece = mine_ref.at[pl.ds(child * part, part), pl.ds(panel * PANEL, PANEL)]
-            pltpu.make_async_copy(piece, piece, mine_sems.at[child, panel]).wait()
+            lane = pl.multiple_of(lax.rem(to, per) * PANEL, PANEL)
+            from_lane = block % per * PANEL
+            out_ref[lax.div(to, per), child, :, pl.ds(lane, PANEL)] = spread_ref[
+                block // per, child, :, from_lane : from_lane + PANEL
+            ]
+        mine_ref[child * part : (child + 1) * part, :] = out_ref[0, child]
 
 
 def order(spread, maps):
     part, width = spread.shape[2:]
     return pl.pallas_call(
         order_kernel,
-        out_shape=(shape(*spread.shape), shape(2 * part, 2 * PANEL)),
-        in_specs=[SMEM, ANY],
-        out_specs=(ANY, ANY),
-        scratch_shapes=[
-            pltpu.SemaphoreType.DMA(maps.shape),
-            pltpu.SemaphoreType.DMA((2, 2)),
-        ],
+        out_shape=(shape(*spread.shape), shape(2 * part, width)),
+        in_specs=[SMEM, VMEM],
+        out_specs=(VMEM, VMEM),
         compiler_params=KERNEL,
         cost_estimate=cost(1000, 1000),
         name="order",
@@ -273,13 +250,45 @@
     )(*pieces, *after)
 
 
-def multiply_kernel(panels_ref, front_ref, *refs):
+def turn_kernel(panels_ref, out_ref):
+    out_ref[...] = panels_ref[...].T
+
+
+def turned(panels):
+    return pl.pallas_call(
+        turn_kernel,
+        out_shape=shape(*panels.shape[::-1]),
+        in_specs=[VMEM],
+        out_specs=VMEM,
+        compiler_params=KERNEL,
+        cost_estimate=cost(1000, 1000),
+        name="turn",
+    )(panels)
+
+
+def add_kernel(left_ref, right_ref, *refs):
+    refs[-1][...] = left_ref[...] + right_ref[...]
+
+
+def add_after(left, right, after):
+    return pl.pallas_call(
+        add_kernel,
+        out_shape=shape(*left.shape),
+        in_specs=[VMEM, VMEM] + [ANY] * len(after),
+        out_specs=VMEM,
+        compiler_params=KERNEL,
+        cost_estimate=cost(1000, 1000),
+        name="add",
+    )(left, right, *after)
+
+
+def multiply_kernel(turned_ref, front_ref, *refs):
     out_ref, held_ref, sems = refs[-3:]
     count, _, width = out_ref.shape
     step = max(width, PANEL)
     copies = []
     for lane in range(0, count * width, step):
-        product = dot(panels_ref[...], front_ref[:, lane : lane + step], ((0,), (0,)))
+        product = dot(turned_ref[...], front_ref[:, lane : lane + step], ((1,), (0,)))
         for at in range(0, step, width):
             n = (lane + at) // width
             held_ref[n] = product[:, at : at + width]
@@ -289,8 +298,8 @@
         copy.wait()
 
 
-def multiply(panels, front, count, after):
-    both = panels.shape[1]
+def multiply(turned_panels, front, count, after):
+    both = turned_panels.shape[0]
     part = (count, both, front.shape[1] // count)
     return pl.pallas_call(
         multiply_kernel,
@@ -301,7 +310,7 @@
         compiler_params=KERNEL,
         cost_estimate=cost(1000, 1000),
         name="multiply",
-    )(panels, front, *after)
+    )(turned_panels, front, *after)
 
 
 def hold(array, after):
@@ -317,23 +326,24 @@
     )(array, *after)
 
 
-def total_kernel(parts_ref, out_ref):
+def total_kernel(parts_ref, *refs):
+    out_ref = refs[-1]
     total = parts_ref[0]
     for i in range(1, parts_ref.shape[0]):
         total = total + parts_ref[i]
     out_ref[...] = total
 
 
-def total_of(parts):
+def total_of(parts, after):
     return pl.pallas_call(
         total_kernel,
         out_shape=shape(*parts.shape[1:]),
-        in_specs=[VMEM],
+        in_specs=[VMEM] + [ANY] * len(after),
         out_specs=VMEM,
         compiler_params=KERNEL,
         cost_estimate=cost(1000, 1000),
         name="total",
-    )(parts)
+    )(parts, *after)
 
 
 def finish_kernel(masks, inv_ref, basis_ref, front_ref, *refs):
@@ -417,12 +427,12 @@
     return near, lax.ppermute(near, "col", pairs_xor(size, 1))
 
 
-def sum_row_small(value, size):
+def sum_row_small(value, size, after):
     span = 2
-    while span <= size:
+    while span < size:
         value = value + lax.ppermute(value, "row", pairs_xor(size, span - 1))
         span *= 2
-    return value
+    return add_after(value, lax.ppermute(value, "row", pairs_xor(size, size - 1)), after)
 
 
 def per_device(children, block_maps):
@@ -439,17 +449,18 @@
     front = lax.all_to_all(ordered, "col", 0, 0, tiled=True)
     near = stack_after(pieces, [])
     panels, tile = gram_tile(near, lax.ppermute(near, "col", pairs_xor(cols, 1)))
-    tile = sum_row_small(tile, rows)
+    across = turned(panels)
+    tile = sum_row_small(tile, rows, [across])
     tiles = even_pieces(tile, cols)
 
     flat = front.reshape(cols * 2 * part, width)
-    products = multiply(panels, flat, rows, [tile])
+    products = multiply(across, flat, rows, [tile])
     parts = lax.all_to_all(products, "row", 0, 0, tiled=True)
     near = stack_after(tiles, [products])
     state = near, lax.ppermute(near, "col", pairs_xor(cols, 1))
     for lo in range(0, both - LANES, LANES):
         state = stage(lo, state)
-    mine = total_of(parts)
+    mine = total_of(parts, state[1:])
     _, inv = stage(both - LANES, state, [mine])
     basis = dot(panels, inv, ((1,), (1,)))
     masks = sorted(range(1, rows), key=lambda k: (k.bit_length(), -k))

time: 109 us -> 108 us (level)
    ppermute x2 -> x1, waiting for transfers between devices: 7.87 us -> 4.04 us  [sum_row_small(): value = value + lax.ppermute(value, 'row', pairs_xor(size, span - 1))]
    ppermute x0 -> x1, waiting for transfers between devices: none -> 3.49 us  [sum_row_small(): lax.ppermute(value, 'row', pairs_xor(size, size - 1))]
    ppermute x0 -> x1, starting transfers between devices: none -> 1.64 us  [sum_row_small(): lax.ppermute(value, 'row', pairs_xor(size, size - 1))]
    ppermute x2 -> x1, starting transfers between devices: 2.16 us -> 0.51 us  [sum_row_small(): value = value + lax.ppermute(value, 'row', pairs_xor(size, span - 1))]
  transfers between devices with their start and end apart: 15 -> 15, of which waited for: 12 -> 12; matrix products, arithmetic and copies ran while one was open for 2% -> 2% of each run, Pallas kernels for 21% -> 22%
where the time goes in v6:
time: 108 us
  Pallas kernels  33.5 us (31%)
  waiting for transfers between devices  28.4 us (26%)
  starting transfers between devices  23.8 us (22%)
  blocking collectives  18 us (17%)
  matrix products  1.86 us (2%)
  local copies, waits for them, and re-layouts  1.23 us (1%)
    pallas_call x4, Pallas kernels, stage(): pl.pallas_call(lambda *refs: stage_kernel(lo, *refs), out_shape=(shape(si...  18.5 us
    all_to_all x1, blocking collectives, per_device(): spread = lax.all_to_all(pack(children, cols), 'col', 0, 0, tiled=True)  18 us
    ppermute x3, waiting for transfers between devices, per_device(): lax.ppermute(mine, 'row', pairs_xor(rows, k))  12.3 us
    pallas_call x2, Pallas kernels, finish(): pl.pallas_call(lambda *refs: finish_kernel(masks, *refs), out_shape=(shap...  7.43 us
    ppermute x6, starting transfers between devices, even_pieces(): lax.ppermute(piece, 'col', pairs_xor(size, k))  6.98 us
    all_to_all x1, starting transfers between devices, per_device(): parts = lax.all_to_all(products, 'row', 0, 0, tiled=True)  5.33 us
    all_to_all x1, starting transfers between devices, per_device(): front = lax.all_to_all(ordered, 'col', 0, 0, tiled=True)  4.93 us
    ppermute x3, starting transfers between devices, per_device(): lax.ppermute(mine, 'row', pairs_xor(rows, k))  4.29 us
  transfers between devices with their start and end apart: 15, of which 12 were waited for; matrix products, arithmetic and copies ran while one was open for 2% of the time, Pallas kernels for 22%

profile of v6, /device:TPU:10, one launch (start us, length us, event | category | flops | bytes accessed | tf_op | source)
XLA Modules:
  0.0 107.8 jit_solution(9040511774398908370)
XLA Ops:
  0.6 0.0 copy-start.2
  0.6 1.2 %copy-done.2 = f32[2,256,512]{2,1,0:T(8,128)S(1)} copy-done((f32[2,256,512]{2,1,0:T(8,128)S(1)}, f32[2,256,512]{2,1,0:T(8,128)}, u32[]{:S(2)}) %copy-start.2) | copy-done | bytes 1048600
  1.9 0.7 shard_map.41
  2.6 0.0 copy-start.3
  2.6 18.0 %all_to_all.15.spread_ref = f32[8,2,32,512]{3,2,1,0:T(8,128)S(1)} all-to-all(f32[8,2,32,512]{3,2,1,0:T(8,128)S(1)} %shard_map.41), channel_id=1, replica_groups=mesh['row'=4,'col'=8] {'col'}, dimensions={0} | all-to-all | bytes 2097152 | tf_op jit(solution)/shard_map/all_to_all | solution.py:446
  20.6 1.7 %order.1 = (f32[8,2,32,512]{3,2,1,0:T(8,128)}, f32[64,512]{1,0:T(8,128)S(1)}) custom-call(s32[2,16]{1,0:T(2,128)S(1)} %copy-done.3, f32[8,2,32,512]{3,2,1,0:T(8,128)S(1)} %all_to_all.15.spread_ref), custom_call_target="tpu_custom_call" | custom-call | flops 1000 | bytes 1000 | tf_op jit(solution)/shard_map/order/pallas_call | solution.py:84
  22.2 1.5 %collective-permute-start.2 = (f32[64,512]{1,0:T(8,128)S(1)}, f32[64,512]{1,0:T(8,128)S(1)}, u32[]{:S(2)}, u32[]{:S(2)}) collective-permute-start(f32[64,512]{1,0:T(8,128)S(1)} %get-tuple-element.15.refs_0_), channel_id=1, source_target_pairs={{0,6},{1,7},{2,4},{3,5},{4,2},{5,3},{6,0},{7,1},{8,14},{9,15},{10,... | collective-permute-start | bytes 393224 | tf_op jit(solution)/shard_map/ppermute | solution.py:422
  23.7 1.5 %collective-permute-start.1 = (f32[64,512]{1,0:T(8,128)S(1)}, f32[64,512]{1,0:T(8,128)S(1)}, u32[]{:S(2)}, u32[]{:S(2)}) collective-permute-start(f32[64,512]{1,0:T(8,128)S(1)} %get-tuple-element.15.refs_0_), channel_id=1, source_target_pairs={{0,4},{1,5},{2,6},{3,7},{4,0},{5,1},{6,2},{7,3},{8,12},{9,13},{10,... | collective-permute-start | bytes 393224 | tf_op jit(solution)/shard_map/ppermute | solution.py:422
  25.2 0.6 collective-permute-start
  25.7 4.9 %all-to-all-start.1 = ((f32[8,2,32,512]{3,2,1,0:T(8,128)}), f32[8,2,32,512]{3,2,1,0:T(8,128)S(1)}, u32[]{:S(2)}, u32[]{:S(2)}) async-start(f32[8,2,32,512]{3,2,1,0:T(8,128)} %get-tuple-element.18), calls=%async_computation.1 | async-start | bytes 2097152 | tf_op jit(solution)/shard_map/all_to_all | solution.py:449
  30.7 0.0 collective-permute-done.2.refs_3_
  30.7 0.2 collective-permute-done.1.refs_2_
  30.8 0.0 collective-permute-done.refs_1_
  30.9 0.1 collective-permute-start.3
  30.9 1.9 %collective-permute-done.3.far_ref = f32[4,64,512]{2,1,0:T(8,128)S(1)} collective-permute-done((f32[4,64,512]{2,1,0:T(8,128)S(1)}, f32[4,64,512]{2,1,0:T(8,128)S(1)}, u32[]{:S(2)}, u32[]{:S(2)}) %collective-permute-start.3) | collective-permute-done | bytes 524320 | tf_op jit(solution)/shard_map/ppermute | solution.py:451
  32.8 0.7 tile.1
  33.6 0.0 copy-start
  33.6 0.5 collective-permute-start.4
  34.1 4.0 %collective-permute-done.4 = f32[160,128]{1,0:T(8,128)S(1)} collective-permute-done((f32[160,128]{1,0:T(8,128)S(1)}, f32[160,128]{1,0:T(8,128)S(1)}, u32[]{:S(2)}, u32[]{:S(2)}) %collective-permute-start.4) | collective-permute-done | bytes 81952 | tf_op jit(solution)/shard_map/ppermute | solution.py:433
  38.1 1.6 %collective-permute-start.5 = (f32[160,128]{1,0:T(8,128)S(1)}, f32[160,128]{1,0:T(8,128)S(1)}, u32[]{:S(2)}, u32[]{:S(2)}) collective-permute-start(f32[160,128]{1,0:T(8,128)S(1)} %add.4.left_ref), channel_id=1, source_target_pairs={{0,24},{8,16},{16,8},{24,0},{1,25},{9,17},{17,9},{25,1},{2,26},{10... | collective-permute-start | bytes 245768 | tf_op jit(solution)/shard_map/ppermute | solution.py:435
  39.8 0.3 turn.1.refs_0_.turned_ref
  40.1 3.5 %collective-permute-done.5.right_ref = f32[160,128]{1,0:T(8,128)S(1)} collective-permute-done((f32[160,128]{1,0:T(8,128)S(1)}, f32[160,128]{1,0:T(8,128)S(1)}, u32[]{:S(2)}, u32[]{:S(2)}) %collective-permute-start.5) | collective-permute-done | bytes 81952 | tf_op jit(solution)/shard_map/ppermute | solution.py:435
  43.6 1.0 all-to-all-done.1.refs_2_
  44.6 2.8 %multiply.1.refs_4_ = f32[4,512,128]{2,1,0:T(8,128)} custom-call(f32[512,512]{1,0:T(8,128)S(1)} %turn.1.refs_0_.turned_ref, f32[512,512]{1,0:T(8,128)S(1)} %bitcast.3, f32[160,128]{1,0:T(8,128)S(1)} %add.5.refs_0_), custom_call_target="tpu_custom_call" | custom-call | flops 1000 | bytes 1000 | tf_op jit(solution)/shard_map/multiply/pallas_call | solution.py:304
  47.4 5.3 %all-to-all-start.2 = ((f32[4,512,128]{2,1,0:T(8,128)}), f32[4,512,128]{2,1,0:T(8,128)}, u32[]{:S(2)}, u32[]{:S(2)}) async-start(f32[4,512,128]{2,1,0:T(8,128)} %multiply.1.refs_4_), calls=%async_computation.2 | async-start | bytes 2097152 | tf_op jit(solution)/shard_map/all_to_all | solution.py:458
  52.7 1.5 %collective-permute-start.8 = (f32[160,128]{1,0:T(8,128)S(1)}, f32[160,128]{1,0:T(8,128)S(1)}, u32[]{:S(2)}, u32[]{:S(2)}) collective-permute-start(f32[160,128]{1,0:T(8,128)S(1)} %add.5.refs_0_), channel_id=1, source_target_pairs={{0,6},{1,7},{2,4},{3,5},{4,2},{5,3},{6,0},{7,1},{8,14},{9,15},{10,... | collective-permute-start | bytes 245768 | tf_op jit(solution)/shard_map/ppermute | solution.py:422
  54.2 1.5 %collective-permute-start.7 = (f32[160,128]{1,0:T(8,128)S(1)}, f32[160,128]{1,0:T(8,128)S(1)}, u32[]{:S(2)}, u32[]{:S(2)}) collective-permute-start(f32[160,128]{1,0:T(8,128)S(1)} %add.5.refs_0_), channel_id=1, source_target_pairs={{0,4},{1,5},{2,6},{3,7},{4,0},{5,1},{6,2},{7,3},{8,12},{9,13},{10,... | collective-permute-start | bytes 245768 | tf_op jit(solution)/shard_map/ppermute | solution.py:422
  55.7 0.5 collective-permute-start.6
  56.2 2.2 %collective-permute-done.8.refs_3_ = f32[160,128]{1,0:T(8,128)S(1)} collective-permute-done((f32[160,128]{1,0:T(8,128)S(1)}, f32[160,128]{1,0:T(8,128)S(1)}, u32[]{:S(2)}, u32[]{:S(2)}) %collective-permute-start.8) | collective-permute-done | bytes 81952 | tf_op jit(solution)/shard_map/ppermute | solution.py:422
  58.4 0.8 collective-permute-done.7.refs_2_
  59.2 0.9 collective-permute-done.6.refs_1_
  60.2 0.1 collective-permute-start.9
  60.3 1.6 %collective-permute-done.9.refs_1_ = f32[4,160,128]{2,1,0:T(8,128)S(1)} collective-permute-done((f32[4,160,128]{2,1,0:T(8,128)S(1)}, f32[4,160,128]{2,1,0:T(8,128)S(1)}, u32[]{:S(2)}, u32[]{:S(2)}) %collective-permute-start.9) | collective-permute-done | bytes 327712 | tf_op jit(solution)/shard_map/ppermute | solution.py:460
  61.9 4.9 %stage.4 = (f32[512,512]{1,0:T(8,128)S(1)}, f32[512,512]{1,0:T(8,128)S(1)}) custom-call(f32[4,160,128]{2,1,0:T(8,128)S(1)} %stack.3.refs_0_, f32[4,160,128]{2,1,0:T(8,128)S(1)} %collective-permute-done.9.refs_1_), custom_call_target="tpu_custom_call" | custom-call | flops 1000 | bytes 1000 | tf_op jit(solution)/shard_map/stage/pallas_call | solution.py:223
  66.8 4.7 %stage.5 = (f32[512,512]{1,0:T(8,128)S(1)}, f32[512,512]{1,0:T(8,128)S(1)}) custom-call(f32[512,512]{1,0:T(8,128)S(1)} %get-tuple-element.19.refs_0_, f32[512,512]{1,0:T(8,128)S(1)} %get-tuple-element.20.refs_1_), custom_call_target="tpu_custom_call", output_to_operand_aliasing={{0}: (0, {}), {1}: (1, {})} | custom-call | flops 1000 | bytes 1000 | tf_op jit(solution)/shard_map/stage/pallas_call | solution.py:223
  71.5 4.5 %stage.6 = (f32[512,512]{1,0:T(8,128)S(1)}, f32[512,512]{1,0:T(8,128)S(1)}) custom-call(f32[512,512]{1,0:T(8,128)S(1)} %get-tuple-element.21.refs_0_, f32[512,512]{1,0:T(8,128)S(1)} %get-tuple-element.22.refs_1_), custom_call_target="tpu_custom_call", output_to_operand_aliasing={{0}: (0, {}), {1}: (1, {})} | custom-call | flops 1000 | bytes 1000 | tf_op jit(solution)/shard_map/stage/pallas_call | solution.py:223
  76.1 0.0 all-to-all-done.2.parts_ref
  76.1 1.3 %total.1.refs_2_.refs_3_ = f32[512,128]{1,0:T(8,128)S(1)} custom-call(f32[4,512,128]{2,1,0:T(8,128)} %all-to-all-done.2.parts_ref, f32[512,512]{1,0:T(8,128)S(1)} %get-tuple-element.24.refs_0_.refs_1_), custom_call_target="tpu_custom_call" | custom-call | flops 1000 | bytes 1000 | tf_op jit(solution)/shard_map/total/pallas_call | solution.py:338
  77.4 2.7 %collective-permute-start.12 = (f32[512,128]{1,0:T(8,128)S(1)}, f32[512,128]{1,0:T(8,128)S(1)}, u32[]{:S(2)}, u32[]{:S(2)}) collective-permute-start(f32[512,128]{1,0:T(8,128)S(1)} %total.1.refs_2_.refs_3_), channel_id=1, source_target_pairs={{0,8},{8,0},{16,24},{24,16},{1,9},{9,1},{17,25},{25,17},{2,10},{10... | collective-permute-start | bytes 786440 | tf_op jit(solution)/shard_map/ppermute | solution.py:468
  80.1 0.2 collective-permute-start.11
  80.4 1.3 %collective-permute-start.10 = (f32[512,128]{1,0:T(8,128)S(1)}, f32[512,128]{1,0:T(8,128)S(1)}, u32[]{:S(2)}, u32[]{:S(2)}) collective-permute-start(f32[512,128]{1,0:T(8,128)S(1)} %total.1.refs_2_.refs_3_), channel_id=1, source_target_pairs={{0,24},{8,16},{16,8},{24,0},{1,25},{9,17},{17,9},{25,1},{2,26},{10... | collective-permute-start | bytes 786440 | tf_op jit(solution)/shard_map/ppermute | solution.py:468
  81.7 4.3 %stage.7 = (f32[512,512]{1,0:T(8,128)S(1)}, f32[512,512]{1,0:T(8,128)S(1)}) custom-call(f32[512,512]{1,0:T(8,128)S(1)} %get-tuple-element.23.refs_0_, f32[512,512]{1,0:T(8,128)S(1)} %get-tuple-element.24.refs_0_.refs_1_, f32[512,128]{1,0:T(8,128)S(1)} %total.1.refs_2_.refs_3_), custom_call_target="tpu_custom_call", output_to_operand_aliasing={{0}: (0, {}), {1}: (1, {})} | custom-call | flops 1000 | bytes 1000 | tf_op jit(solution)/shard_map/stage/pallas_call | solution.py:223
  86.0 1.9 %fusion.refs_1_ = f32[512,512]{1,0:T(8,128)S(1)} fusion(f32[512,512]{1,0:T(8,128)S(1)} %copy-done.1, f32[512,512]{1,0:T(8,128)S(1)} %get-tuple-element.25.refs_0_), kind=kOutput, calls=%fused_computation | convolution fusion | flops 1610612736 | bytes 3145728 | tf_op jit(solution)/shard_map/dot_general | solution.py:19
  87.8 1.7 %collective-permute-done.12.refs_4_ = f32[512,128]{1,0:T(8,128)S(1)} collective-permute-done((f32[512,128]{1,0:T(8,128)S(1)}, f32[512,128]{1,0:T(8,128)S(1)}, u32[]{:S(2)}, u32[]{:S(2)}) %collective-permute-start.12) | collective-permute-done | bytes 262176 | tf_op jit(solution)/shard_map/ppermute | solution.py:468
  89.5 3.7 %finish.2 = (f32[512,512]{1,0:T(8,128)}, f32[2,256,512]{2,1,0:T(8,128)}) custom-call(f32[512,512]{1,0:T(8,128)S(1)} %get-tuple-element.25.refs_0_, f32[512,512]{1,0:T(8,128)S(1)} %fusion.refs_1_, f32[8,2,32,512]{3,2,1,0:T(8,128)S(1)} %all-to-all-done.1.refs_2_, f32[512,128]{1,0:T(8,128)S(1)} %total.1.refs_2_.refs_3_, ...), custom_call_target="tpu_custom_call" | custom-call | flops 1000 | bytes 1000 | tf_op jit(solution)/shard_map/finish/pallas_call | solution.py:399
  93.2 5.1 %collective-permute-done.11.refs_4_ = f32[512,128]{1,0:T(8,128)S(1)} collective-permute-done((f32[512,128]{1,0:T(8,128)S(1)}, f32[512,128]{1,0:T(8,128)S(1)}, u32[]{:S(2)}, u32[]{:S(2)}) %collective-permute-start.11) | collective-permute-done | bytes 262176 | tf_op jit(solution)/shard_map/ppermute | solution.py:468
  98.3 5.6 %collective-permute-done.10.refs_3_ = f32[512,128]{1,0:T(8,128)S(1)} collective-permute-done((f32[512,128]{1,0:T(8,128)S(1)}, f32[512,128]{1,0:T(8,128)S(1)}, u32[]{:S(2)}, u32[]{:S(2)}) %collective-permute-start.10) | collective-permute-done | bytes 262176 | tf_op jit(solution)/shard_map/ppermute | solution.py:468
  103.9 3.7 %finish.3 = (f32[512,512]{1,0:T(8,128)}, f32[2,256,512]{2,1,0:T(8,128)}) custom-call(f32[512,512]{1,0:T(8,128)S(1)} %get-tuple-element.25.refs_0_, f32[512,512]{1,0:T(8,128)S(1)} %fusion.refs_1_, f32[8,2,32,512]{3,2,1,0:T(8,128)S(1)} %all-to-all-done.1.refs_2_, ...), custom_call_target="tpu_custom_call", output_to_operand_aliasing={{0}: (5, {}), {1}: (6, {})} | custom-call | flops 1000 | bytes 1000 | tf_op jit(solution)/shard_map/finish/pallas_call | solution.py:399
  (8 shorter events, 0.1 us)
Async XLA Ops:
  0.6 1.2 %copy-start.2 = (f32[2,256,512]{2,1,0:T(8,128)S(1)}, f32[2,256,512]{2,1,0:T(8,128)}, u32[]{:S(2)}) copy-start(f32[2,256,512]{2,1,0:T(8,128)} %children_ref.1) | copy-start | bytes 3145732
  2.6 18.0 %copy-start.3 = (s32[2,16]{1,0:T(2,128)S(1)}, s32[2,16]{1,0:T(2,128)}, u32[]{:S(2)}) copy-start(s32[2,16]{1,0:T(2,128)} %maps_ref.1) | copy-start | bytes 388
  22.2 8.4 %collective-permute-start.2 = (f32[64,512]{1,0:T(8,128)S(1)}, f32[64,512]{1,0:T(8,128)S(1)}, u32[]{:S(2)}, u32[]{:S(2)}) collective-permute-start(f32[64,512]{1,0:T(8,128)S(1)} %get-tuple-element.15.refs_0_), channel_id=1, source_target_pairs={{0,6},{1,7},{2,4},{3,5},{4,2},{5,3},{6,0},{7,1},{8,14},{9,15},{10,... | collective-permute-start | bytes 393224 | tf_op jit(solution)/shard_map/ppermute | solution.py:422
  23.7 7.1 %collective-permute-start.1 = (f32[64,512]{1,0:T(8,128)S(1)}, f32[64,512]{1,0:T(8,128)S(1)}, u32[]{:S(2)}, u32[]{:S(2)}) collective-permute-start(f32[64,512]{1,0:T(8,128)S(1)} %get-tuple-element.15.refs_0_), channel_id=1, source_target_pairs={{0,4},{1,5},{2,6},{3,7},{4,0},{5,1},{6,2},{7,3},{8,12},{9,13},{10,... | collective-permute-start | bytes 393224 | tf_op jit(solution)/shard_map/ppermute | solution.py:422
  25.2 5.7 %collective-permute-start = (f32[64,512]{1,0:T(8,128)S(1)}, f32[64,512]{1,0:T(8,128)S(1)}, u32[]{:S(2)}, u32[]{:S(2)}) collective-permute-start(f32[64,512]{1,0:T(8,128)S(1)} %get-tuple-element.15.refs_0_), channel_id=1, source_target_pairs={{0,2},{1,3},{2,0},{3,1},{4,6},{5,7},{6,4},{7,5},{8,10},{9,11},{10,... | collective-permute-start | bytes 393224 | tf_op jit(solution)/shard_map/ppermute | solution.py:422
  25.7 18.8 %all-to-all-start.1 = ((f32[8,2,32,512]{3,2,1,0:T(8,128)}), f32[8,2,32,512]{3,2,1,0:T(8,128)S(1)}, u32[]{:S(2)}, u32[]{:S(2)}) async-start(f32[8,2,32,512]{3,2,1,0:T(8,128)} %get-tuple-element.18), calls=%async_computation.1 | async-start | bytes 2097152 | tf_op jit(solution)/shard_map/all_to_all | solution.py:449
  30.9 2.0 %collective-permute-start.3 = (f32[4,64,512]{2,1,0:T(8,128)S(1)}, f32[4,64,512]{2,1,0:T(8,128)S(1)}, u32[]{:S(2)}, u32[]{:S(2)}) collective-permute-start(f32[4,64,512]{2,1,0:T(8,128)S(1)} %stack.2.near_ref), channel_id=1, source_target_pairs={{0,1},{1,0},{2,3},{3,2},{4,5},{5,4},{6,7},{7,6},{8,9},{9,8},{10,11... | collective-permute-start | bytes 1572872 | tf_op jit(solution)/shard_map/ppermute | solution.py:451
  33.6 6.6 %copy-start = (f32[512,512]{1,0:T(8,128)}, f32[512,512]{1,0:T(8,128)S(1)}, u32[]{:S(2)}) copy-start(f32[512,512]{1,0:T(8,128)S(1)} %get-tuple-element.17.panels_ref) | copy-start | bytes 3145732
  33.6 4.5 %collective-permute-start.4 = (f32[160,128]{1,0:T(8,128)S(1)}, f32[160,128]{1,0:T(8,128)S(1)}, u32[]{:S(2)}, u32[]{:S(2)}) collective-permute-start(f32[160,128]{1,0:T(8,128)S(1)} %get-tuple-element.16), channel_id=1, source_target_pairs={{0,8},{8,0},{16,24},{24,16},{1,9},{9,1},{17,25},{25,17},{2,10},{10... | collective-permute-start | bytes 245768 | tf_op jit(solution)/shard_map/ppermute | solution.py:433
  38.1 5.5 %collective-permute-start.5 = (f32[160,128]{1,0:T(8,128)S(1)}, f32[160,128]{1,0:T(8,128)S(1)}, u32[]{:S(2)}, u32[]{:S(2)}) collective-permute-start(f32[160,128]{1,0:T(8,128)S(1)} %add.4.left_ref), channel_id=1, source_target_pairs={{0,24},{8,16},{16,8},{24,0},{1,25},{9,17},{17,9},{25,1},{2,26},{10... | collective-permute-start | bytes 245768 | tf_op jit(solution)/shard_map/ppermute | solution.py:435
  47.4 28.7 %all-to-all-start.2 = ((f32[4,512,128]{2,1,0:T(8,128)}), f32[4,512,128]{2,1,0:T(8,128)}, u32[]{:S(2)}, u32[]{:S(2)}) async-start(f32[4,512,128]{2,1,0:T(8,128)} %multiply.1.refs_4_), calls=%async_computation.2 | async-start | bytes 2097152 | tf_op jit(solution)/shard_map/all_to_all | solution.py:458
  52.7 5.7 %collective-permute-start.8 = (f32[160,128]{1,0:T(8,128)S(1)}, f32[160,128]{1,0:T(8,128)S(1)}, u32[]{:S(2)}, u32[]{:S(2)}) collective-permute-start(f32[160,128]{1,0:T(8,128)S(1)} %add.5.refs_0_), channel_id=1, source_target_pairs={{0,6},{1,7},{2,4},{3,5},{4,2},{5,3},{6,0},{7,1},{8,14},{9,15},{10,... | collective-permute-start | bytes 245768 | tf_op jit(solution)/shard_map/ppermute | solution.py:422
  54.2 5.0 %collective-permute-start.7 = (f32[160,128]{1,0:T(8,128)S(1)}, f32[160,128]{1,0:T(8,128)S(1)}, u32[]{:S(2)}, u32[]{:S(2)}) collective-permute-start(f32[160,128]{1,0:T(8,128)S(1)} %add.5.refs_0_), channel_id=1, source_target_pairs={{0,4},{1,5},{2,6},{3,7},{4,0},{5,1},{6,2},{7,3},{8,12},{9,13},{10,... | collective-permute-start | bytes 245768 | tf_op jit(solution)/shard_map/ppermute | solution.py:422
  55.7 4.4 %collective-permute-start.6 = (f32[160,128]{1,0:T(8,128)S(1)}, f32[160,128]{1,0:T(8,128)S(1)}, u32[]{:S(2)}, u32[]{:S(2)}) collective-permute-start(f32[160,128]{1,0:T(8,128)S(1)} %add.5.refs_0_), channel_id=1, source_target_pairs={{0,2},{1,3},{2,0},{3,1},{4,6},{5,7},{6,4},{7,5},{8,10},{9,11},{10,... | collective-permute-start | bytes 245768 | tf_op jit(solution)/shard_map/ppermute | solution.py:422
  60.2 1.7 %collective-permute-start.9 = (f32[4,160,128]{2,1,0:T(8,128)S(1)}, f32[4,160,128]{2,1,0:T(8,128)S(1)}, u32[]{:S(2)}, u32[]{:S(2)}) collective-permute-start(f32[4,160,128]{2,1,0:T(8,128)S(1)} %stack.3.refs_0_), channel_id=1, source_target_pairs={{0,1},{1,0},{2,3},{3,2},{4,5},{5,4},{6,7},{7,6},{8,9},{9,8},{10,11... | collective-permute-start | bytes 983048 | tf_op jit(solution)/shard_map/ppermute | solution.py:460
  77.4 12.1 %collective-permute-start.12 = (f32[512,128]{1,0:T(8,128)S(1)}, f32[512,128]{1,0:T(8,128)S(1)}, u32[]{:S(2)}, u32[]{:S(2)}) collective-permute-start(f32[512,128]{1,0:T(8,128)S(1)} %total.1.refs_2_.refs_3_), channel_id=1, source_target_pairs={{0,8},{8,0},{16,24},{24,16},{1,9},{9,1},{17,25},{25,17},{2,10},{10... | collective-permute-start | bytes 786440 | tf_op jit(solution)/shard_map/ppermute | solution.py:468
  80.1 18.2 %collective-permute-start.11 = (f32[512,128]{1,0:T(8,128)S(1)}, f32[512,128]{1,0:T(8,128)S(1)}, u32[]{:S(2)}, u32[]{:S(2)}) collective-permute-start(f32[512,128]{1,0:T(8,128)S(1)} %total.1.refs_2_.refs_3_), channel_id=1, source_target_pairs={{0,16},{8,24},{16,0},{24,8},{1,17},{9,25},{17,1},{25,9},{2,18},{10... | collective-permute-start | bytes 786440 | tf_op jit(solution)/shard_map/ppermute | solution.py:468
  80.4 23.5 %collective-permute-start.10 = (f32[512,128]{1,0:T(8,128)S(1)}, f32[512,128]{1,0:T(8,128)S(1)}, u32[]{:S(2)}, u32[]{:S(2)}) collective-permute-start(f32[512,128]{1,0:T(8,128)S(1)} %total.1.refs_2_.refs_3_), channel_id=1, source_target_pairs={{0,24},{8,16},{16,8},{24,0},{1,25},{9,17},{17,9},{25,1},{2,26},{10... | collective-permute-start | bytes 786440 | tf_op jit(solution)/shard_map/ppermute | solution.py:468
  81.7 4.3 %copy-start.1 = (f32[512,512]{1,0:T(8,128)S(1)}, f32[512,512]{1,0:T(8,128)}, u32[]{:S(2)}) copy-start(f32[512,512]{1,0:T(8,128)} %copy-done) | copy-start | bytes 3145732

commit v7 on v6

--- a/solution.py
+++ b/solution.py
@@ -40,16 +40,10 @@
         copy.wait()
 
 
-def pack_kernel(children_ref, out_ref, sems):
+def pack_kernel(children_ref, out_ref):
     parts, _, part, _ = out_ref.shape
-    run_copies(
-        [
-            pltpu.make_async_copy(
-                children_ref.at[:, pl.ds(part * d, part), :], out_ref.at[d], sems.at[d]
-            )
-            for d in range(parts)
-        ]
-    )
+    for d in range(parts):
+        out_ref[d] = children_ref[:, d * part : (d + 1) * part, :]
 
 
 def pack(children, parts):
@@ -57,11 +51,11 @@
     return pl.pallas_call(
         pack_kernel,
         out_shape=shape(parts, two, rows_dev // parts, width),
-        in_specs=[ANY],
-        out_specs=ANY,
-        scratch_shapes=[pltpu.SemaphoreType.DMA((parts,))],
-        compiler_params=KERNEL,
-        cost_estimate=cost(1000, 1000),
+        in_specs=[VMEM],
+        out_specs=VMEM,
+        compiler_params=KERNEL,
+        cost_estimate=cost(1000, 1000),
+        name="pack",
     )(children)
 
 
@@ -327,10 +321,18 @@
 
 
 def total_kernel(parts_ref, *refs):
-    out_ref = refs[-1]
-    total = parts_ref[0]
-    for i in range(1, parts_ref.shape[0]):
-        total = total + parts_ref[i]
+    out_ref, held_ref, sems = refs[-3:]
+    copies = [
+        pltpu.make_async_copy(parts_ref.at[n], held_ref.at[n], sems.at[n])
+        for n in range(held_ref.shape[0])
+    ]
+    for copy in copies:
+        copy.start()
+    copies[0].wait()
+    total = held_ref[0]
+    for n, copy in enumerate(copies[1:]):
+        copy.wait()
+        total = total + held_ref[n + 1]
     out_ref[...] = total
 
 
@@ -338,8 +340,12 @@
     return pl.pallas_call(
         total_kernel,
         out_shape=shape(*parts.shape[1:]),
-        in_specs=[VMEM] + [ANY] * len(after),
+        in_specs=[ANY] * (1 + len(after)),
         out_specs=VMEM,
+        scratch_shapes=[
+            pltpu.VMEM(parts.shape, F32),
+            pltpu.SemaphoreType.DMA(parts.shape[:1]),
+        ],
         compiler_params=KERNEL,
         cost_estimate=cost(1000, 1000),
         name="total",

time: 108 us -> 107 us (level)
  no operation moved by 1% of the time
where the time goes in v7:
time: 107 us
  Pallas kernels  32.8 us (31%)
  waiting for transfers between devices  28.4 us (27%)
  starting transfers between devices  23.8 us (22%)
  blocking collectives  18 us (17%)
  matrix products  1.86 us (2%)
  local copies, waits for them, and re-layouts  1.23 us (1%)
    pallas_call x4, Pallas kernels, stage(): pl.pallas_call(lambda *refs: stage_kernel(lo, *refs), out_shape=(shape(si...  18.5 us
    all_to_all x1, blocking collectives, per_device(): spread = lax.all_to_all(pack(children, cols), 'col', 0, 0, tiled=True)  18 us
    ppermute x3, waiting for transfers between devices, per_device(): lax.ppermute(mine, 'row', pairs_xor(rows, k))  12.3 us
    pallas_call x2, Pallas kernels, finish(): pl.pallas_call(lambda *refs: finish_kernel(masks, *refs), out_shape=(shap...  7.42 us
    ppermute x6, starting transfers between devices, even_pieces(): lax.ppermute(piece, 'col', pairs_xor(size, k))  6.98 us
    all_to_all x1, starting transfers between devices, per_device(): parts = lax.all_to_all(products, 'row', 0, 0, tiled=True)  5.33 us
    all_to_all x1, starting transfers between devices, per_device(): front = lax.all_to_all(ordered, 'col', 0, 0, tiled=True)  4.93 us
    ppermute x3, starting transfers between devices, per_device(): lax.ppermute(mine, 'row', pairs_xor(rows, k))  4.3 us
  transfers between devices with their start and end apart: 15, of which 12 were waited for; matrix products, arithmetic and copies ran while one was open for 2% of the time, Pallas kernels for 22%

profile of v7, /device:TPU:10, one launch (start us, length us, event | category | flops | bytes accessed | tf_op | source)
XLA Modules:
  0.0 107.1 jit_solution(9083908765326112756)
XLA Ops:
  0.6 1.2 %copy-done.2 = f32[2,256,512]{2,1,0:T(8,128)S(1)} copy-done((f32[2,256,512]{2,1,0:T(8,128)S(1)}, f32[2,256,512]{2,1,0:T(8,128)}, u32[]{:S(2)}) %copy-start.2) | copy-done | bytes 1048600
  1.9 0.1 pack.1
  1.9 0.0 copy-start.3
  1.9 18.0 %all_to_all.15.spread_ref = f32[8,2,32,512]{3,2,1,0:T(8,128)S(1)} all-to-all(f32[8,2,32,512]{3,2,1,0:T(8,128)S(1)} %pack.1), channel_id=1, replica_groups=mesh['row'=4,'col'=8] {'col'}, dimensions={0} | all-to-all | bytes 2097152 | tf_op jit(solution)/shard_map/all_to_all | solution.py:452
  19.9 1.7 %order.1 = (f32[8,2,32,512]{3,2,1,0:T(8,128)}, f32[64,512]{1,0:T(8,128)S(1)}) custom-call(s32[2,16]{1,0:T(2,128)S(1)} %copy-done.3, f32[8,2,32,512]{3,2,1,0:T(8,128)S(1)} %all_to_all.15.spread_ref), custom_call_target="tpu_custom_call" | custom-call | flops 1000 | bytes 1000 | tf_op jit(solution)/shard_map/order/pallas_call | solution.py:78
  21.6 1.5 %collective-permute-start.2 = (f32[64,512]{1,0:T(8,128)S(1)}, f32[64,512]{1,0:T(8,128)S(1)}, u32[]{:S(2)}, u32[]{:S(2)}) collective-permute-start(f32[64,512]{1,0:T(8,128)S(1)} %get-tuple-element.15.refs_0_), channel_id=1, source_target_pairs={{0,6},{1,7},{2,4},{3,5},{4,2},{5,3},{6,0},{7,1},{8,14},{9,15},{10,... | collective-permute-start | bytes 393224 | tf_op jit(solution)/shard_map/ppermute | solution.py:428
  23.0 1.5 %collective-permute-start.1 = (f32[64,512]{1,0:T(8,128)S(1)}, f32[64,512]{1,0:T(8,128)S(1)}, u32[]{:S(2)}, u32[]{:S(2)}) collective-permute-start(f32[64,512]{1,0:T(8,128)S(1)} %get-tuple-element.15.refs_0_), channel_id=1, source_target_pairs={{0,4},{1,5},{2,6},{3,7},{4,0},{5,1},{6,2},{7,3},{8,12},{9,13},{10,... | collective-permute-start | bytes 393224 | tf_op jit(solution)/shard_map/ppermute | solution.py:428
  24.5 0.6 collective-permute-start
  25.0 4.9 %all-to-all-start.1 = ((f32[8,2,32,512]{3,2,1,0:T(8,128)}), f32[8,2,32,512]{3,2,1,0:T(8,128)S(1)}, u32[]{:S(2)}, u32[]{:S(2)}) async-start(f32[8,2,32,512]{3,2,1,0:T(8,128)} %get-tuple-element.18), calls=%async_computation.1 | async-start | bytes 2097152 | tf_op jit(solution)/shard_map/all_to_all | solution.py:455
  30.0 0.0 collective-permute-done.2.refs_3_
  30.0 0.2 collective-permute-done.1.refs_2_
  30.1 0.0 collective-permute-done.refs_1_
  30.2 0.1 collective-permute-start.3
  30.3 1.9 %collective-permute-done.3.far_ref = f32[4,64,512]{2,1,0:T(8,128)S(1)} collective-permute-done((f32[4,64,512]{2,1,0:T(8,128)S(1)}, f32[4,64,512]{2,1,0:T(8,128)S(1)}, u32[]{:S(2)}, u32[]{:S(2)}) %collective-permute-start.3) | collective-permute-done | bytes 524320 | tf_op jit(solution)/shard_map/ppermute | solution.py:457
  32.2 0.7 tile.1
  32.9 0.0 copy-start
  32.9 0.5 collective-permute-start.4
  33.4 4.0 %collective-permute-done.4 = f32[160,128]{1,0:T(8,128)S(1)} collective-permute-done((f32[160,128]{1,0:T(8,128)S(1)}, f32[160,128]{1,0:T(8,128)S(1)}, u32[]{:S(2)}, u32[]{:S(2)}) %collective-permute-start.4) | collective-permute-done | bytes 81952 | tf_op jit(solution)/shard_map/ppermute | solution.py:439
  37.5 1.6 %collective-permute-start.5 = (f32[160,128]{1,0:T(8,128)S(1)}, f32[160,128]{1,0:T(8,128)S(1)}, u32[]{:S(2)}, u32[]{:S(2)}) collective-permute-start(f32[160,128]{1,0:T(8,128)S(1)} %add.4.left_ref), channel_id=1, source_target_pairs={{0,24},{8,16},{16,8},{24,0},{1,25},{9,17},{17,9},{25,1},{2,26},{10... | collective-permute-start | bytes 245768 | tf_op jit(solution)/shard_map/ppermute | solution.py:441
  39.1 0.3 turn.1.refs_0_.turned_ref
  39.4 0.0 copy-done
  39.4 3.5 %collective-permute-done.5.right_ref = f32[160,128]{1,0:T(8,128)S(1)} collective-permute-done((f32[160,128]{1,0:T(8,128)S(1)}, f32[160,128]{1,0:T(8,128)S(1)}, u32[]{:S(2)}, u32[]{:S(2)}) %collective-permute-start.5) | collective-permute-done | bytes 81952 | tf_op jit(solution)/shard_map/ppermute | solution.py:441
  43.0 0.9 all-to-all-done.1.refs_2_
  43.9 2.8 %multiply.1.refs_4_ = f32[4,512,128]{2,1,0:T(8,128)} custom-call(f32[512,512]{1,0:T(8,128)S(1)} %turn.1.refs_0_.turned_ref, f32[512,512]{1,0:T(8,128)S(1)} %bitcast.3, f32[160,128]{1,0:T(8,128)S(1)} %add.5.refs_0_), custom_call_target="tpu_custom_call" | custom-call | flops 1000 | bytes 1000 | tf_op jit(solution)/shard_map/multiply/pallas_call | solution.py:298
  46.7 5.3 %all-to-all-start.2 = ((f32[4,512,128]{2,1,0:T(8,128)}), f32[4,512,128]{2,1,0:T(8,128)}, u32[]{:S(2)}, u32[]{:S(2)}) async-start(f32[4,512,128]{2,1,0:T(8,128)} %multiply.1.refs_4_), calls=%async_computation.2 | async-start | bytes 2097152 | tf_op jit(solution)/shard_map/all_to_all | solution.py:464
  52.0 1.5 %collective-permute-start.8 = (f32[160,128]{1,0:T(8,128)S(1)}, f32[160,128]{1,0:T(8,128)S(1)}, u32[]{:S(2)}, u32[]{:S(2)}) collective-permute-start(f32[160,128]{1,0:T(8,128)S(1)} %add.5.refs_0_), channel_id=1, source_target_pairs={{0,6},{1,7},{2,4},{3,5},{4,2},{5,3},{6,0},{7,1},{8,14},{9,15},{10,... | collective-permute-start | bytes 245768 | tf_op jit(solution)/shard_map/ppermute | solution.py:428
  53.5 1.5 %collective-permute-start.7 = (f32[160,128]{1,0:T(8,128)S(1)}, f32[160,128]{1,0:T(8,128)S(1)}, u32[]{:S(2)}, u32[]{:S(2)}) collective-permute-start(f32[160,128]{1,0:T(8,128)S(1)} %add.5.refs_0_), channel_id=1, source_target_pairs={{0,4},{1,5},{2,6},{3,7},{4,0},{5,1},{6,2},{7,3},{8,12},{9,13},{10,... | collective-permute-start | bytes 245768 | tf_op jit(solution)/shard_map/ppermute | solution.py:428
  55.0 0.5 collective-permute-start.6
  55.5 2.2 %collective-permute-done.8.refs_3_ = f32[160,128]{1,0:T(8,128)S(1)} collective-permute-done((f32[160,128]{1,0:T(8,128)S(1)}, f32[160,128]{1,0:T(8,128)S(1)}, u32[]{:S(2)}, u32[]{:S(2)}) %collective-permute-start.8) | collective-permute-done | bytes 81952 | tf_op jit(solution)/shard_map/ppermute | solution.py:428
  57.7 0.8 collective-permute-done.7.refs_2_
  58.6 0.9 collective-permute-done.6.refs_1_
  59.5 0.1 collective-permute-start.9
  59.6 1.6 %collective-permute-done.9.refs_1_ = f32[4,160,128]{2,1,0:T(8,128)S(1)} collective-permute-done((f32[4,160,128]{2,1,0:T(8,128)S(1)}, f32[4,160,128]{2,1,0:T(8,128)S(1)}, u32[]{:S(2)}, u32[]{:S(2)}) %collective-permute-start.9) | collective-permute-done | bytes 327712 | tf_op jit(solution)/shard_map/ppermute | solution.py:466
  61.2 4.9 %stage.4 = (f32[512,512]{1,0:T(8,128)S(1)}, f32[512,512]{1,0:T(8,128)S(1)}) custom-call(f32[4,160,128]{2,1,0:T(8,128)S(1)} %stack.3.refs_0_, f32[4,160,128]{2,1,0:T(8,128)S(1)} %collective-permute-done.9.refs_1_), custom_call_target="tpu_custom_call" | custom-call | flops 1000 | bytes 1000 | tf_op jit(solution)/shard_map/stage/pallas_call | solution.py:217
  66.1 4.7 %stage.5 = (f32[512,512]{1,0:T(8,128)S(1)}, f32[512,512]{1,0:T(8,128)S(1)}) custom-call(f32[512,512]{1,0:T(8,128)S(1)} %get-tuple-element.19.refs_0_, f32[512,512]{1,0:T(8,128)S(1)} %get-tuple-element.20.refs_1_), custom_call_target="tpu_custom_call", output_to_operand_aliasing={{0}: (0, {}), {1}: (1, {})} | custom-call | flops 1000 | bytes 1000 | tf_op jit(solution)/shard_map/stage/pallas_call | solution.py:217
  70.9 4.5 %stage.6 = (f32[512,512]{1,0:T(8,128)S(1)}, f32[512,512]{1,0:T(8,128)S(1)}) custom-call(f32[512,512]{1,0:T(8,128)S(1)} %get-tuple-element.21.refs_0_, f32[512,512]{1,0:T(8,128)S(1)} %get-tuple-element.22.refs_1_), custom_call_target="tpu_custom_call", output_to_operand_aliasing={{0}: (0, {}), {1}: (1, {})} | custom-call | flops 1000 | bytes 1000 | tf_op jit(solution)/shard_map/stage/pallas_call | solution.py:217
  75.4 0.0 all-to-all-done.2.parts_ref
  75.4 1.2 %total.1.refs_2_.refs_3_ = f32[512,128]{1,0:T(8,128)S(1)} custom-call(f32[4,512,128]{2,1,0:T(8,128)} %all-to-all-done.2.parts_ref, f32[512,512]{1,0:T(8,128)S(1)} %get-tuple-element.24.refs_0_.refs_1_), custom_call_target="tpu_custom_call" | custom-call | flops 1000 | bytes 1000 | tf_op jit(solution)/shard_map/total/pallas_call | solution.py:340
  76.7 2.8 %collective-permute-start.12 = (f32[512,128]{1,0:T(8,128)S(1)}, f32[512,128]{1,0:T(8,128)S(1)}, u32[]{:S(2)}, u32[]{:S(2)}) collective-permute-start(f32[512,128]{1,0:T(8,128)S(1)} %total.1.refs_2_.refs_3_), channel_id=1, source_target_pairs={{0,8},{8,0},{16,24},{24,16},{1,9},{9,1},{17,25},{25,17},{2,10},{10... | collective-permute-start | bytes 786440 | tf_op jit(solution)/shard_map/ppermute | solution.py:474
  79.4 0.2 collective-permute-start.11
  79.7 1.3 %collective-permute-start.10 = (f32[512,128]{1,0:T(8,128)S(1)}, f32[512,128]{1,0:T(8,128)S(1)}, u32[]{:S(2)}, u32[]{:S(2)}) collective-permute-start(f32[512,128]{1,0:T(8,128)S(1)} %total.1.refs_2_.refs_3_), channel_id=1, source_target_pairs={{0,24},{8,16},{16,8},{24,0},{1,25},{9,17},{17,9},{25,1},{2,26},{10... | collective-permute-start | bytes 786440 | tf_op jit(solution)/shard_map/ppermute | solution.py:474
  81.0 4.3 %stage.7 = (f32[512,512]{1,0:T(8,128)S(1)}, f32[512,512]{1,0:T(8,128)S(1)}) custom-call(f32[512,512]{1,0:T(8,128)S(1)} %get-tuple-element.23.refs_0_, f32[512,512]{1,0:T(8,128)S(1)} %get-tuple-element.24.refs_0_.refs_1_, f32[512,128]{1,0:T(8,128)S(1)} %total.1.refs_2_.refs_3_), custom_call_target="tpu_custom_call", output_to_operand_aliasing={{0}: (0, {}), {1}: (1, {})} | custom-call | flops 1000 | bytes 1000 | tf_op jit(solution)/shard_map/stage/pallas_call | solution.py:217
  85.3 1.9 %fusion.refs_1_ = f32[512,512]{1,0:T(8,128)S(1)} fusion(f32[512,512]{1,0:T(8,128)S(1)} %copy-done.1, f32[512,512]{1,0:T(8,128)S(1)} %get-tuple-element.25.refs_0_), kind=kOutput, calls=%fused_computation | convolution fusion | flops 1610612736 | bytes 3145728 | tf_op jit(solution)/shard_map/dot_general | solution.py:19
  87.2 1.7 %collective-permute-done.12.refs_4_ = f32[512,128]{1,0:T(8,128)S(1)} collective-permute-done((f32[512,128]{1,0:T(8,128)S(1)}, f32[512,128]{1,0:T(8,128)S(1)}, u32[]{:S(2)}, u32[]{:S(2)}) %collective-permute-start.12) | collective-permute-done | bytes 262176 | tf_op jit(solution)/shard_map/ppermute | solution.py:474
  88.8 3.7 %finish.2 = (f32[512,512]{1,0:T(8,128)}, f32[2,256,512]{2,1,0:T(8,128)}) custom-call(f32[512,512]{1,0:T(8,128)S(1)} %get-tuple-element.25.refs_0_, f32[512,512]{1,0:T(8,128)S(1)} %fusion.refs_1_, f32[8,2,32,512]{3,2,1,0:T(8,128)S(1)} %all-to-all-done.1.refs_2_, f32[512,128]{1,0:T(8,128)S(1)} %total.1.refs_2_.refs_3_, ...), custom_call_target="tpu_custom_call" | custom-call | flops 1000 | bytes 1000 | tf_op jit(solution)/shard_map/finish/pallas_call | solution.py:405
  92.5 5.1 %collective-permute-done.11.refs_4_ = f32[512,128]{1,0:T(8,128)S(1)} collective-permute-done((f32[512,128]{1,0:T(8,128)S(1)}, f32[512,128]{1,0:T(8,128)S(1)}, u32[]{:S(2)}, u32[]{:S(2)}) %collective-permute-start.11) | collective-permute-done | bytes 262176 | tf_op jit(solution)/shard_map/ppermute | solution.py:474
  97.6 5.6 %collective-permute-done.10.refs_3_ = f32[512,128]{1,0:T(8,128)S(1)} collective-permute-done((f32[512,128]{1,0:T(8,128)S(1)}, f32[512,128]{1,0:T(8,128)S(1)}, u32[]{:S(2)}, u32[]{:S(2)}) %collective-permute-start.10) | collective-permute-done | bytes 262176 | tf_op jit(solution)/shard_map/ppermute | solution.py:474
  103.2 3.7 %finish.3 = (f32[512,512]{1,0:T(8,128)}, f32[2,256,512]{2,1,0:T(8,128)}) custom-call(f32[512,512]{1,0:T(8,128)S(1)} %get-tuple-element.25.refs_0_, f32[512,512]{1,0:T(8,128)S(1)} %fusion.refs_1_, f32[8,2,32,512]{3,2,1,0:T(8,128)S(1)} %all-to-all-done.1.refs_2_, ...), custom_call_target="tpu_custom_call", output_to_operand_aliasing={{0}: (5, {}), {1}: (6, {})} | custom-call | flops 1000 | bytes 1000 | tf_op jit(solution)/shard_map/finish/pallas_call | solution.py:405
  (8 shorter events, 0.1 us)
Async XLA Ops:
  0.6 1.2 %copy-start.2 = (f32[2,256,512]{2,1,0:T(8,128)S(1)}, f32[2,256,512]{2,1,0:T(8,128)}, u32[]{:S(2)}) copy-start(f32[2,256,512]{2,1,0:T(8,128)} %children_ref.1) | copy-start | bytes 3145732
  1.9 18.0 %copy-start.3 = (s32[2,16]{1,0:T(2,128)S(1)}, s32[2,16]{1,0:T(2,128)}, u32[]{:S(2)}) copy-start(s32[2,16]{1,0:T(2,128)} %maps_ref.1) | copy-start | bytes 388
  21.6 8.4 %collective-permute-start.2 = (f32[64,512]{1,0:T(8,128)S(1)}, f32[64,512]{1,0:T(8,128)S(1)}, u32[]{:S(2)}, u32[]{:S(2)}) collective-permute-start(f32[64,512]{1,0:T(8,128)S(1)} %get-tuple-element.15.refs_0_), channel_id=1, source_target_pairs={{0,6},{1,7},{2,4},{3,5},{4,2},{5,3},{6,0},{7,1},{8,14},{9,15},{10,... | collective-permute-start | bytes 393224 | tf_op jit(solution)/shard_map/ppermute | solution.py:428
  23.0 7.1 %collective-permute-start.1 = (f32[64,512]{1,0:T(8,128)S(1)}, f32[64,512]{1,0:T(8,128)S(1)}, u32[]{:S(2)}, u32[]{:S(2)}) collective-permute-start(f32[64,512]{1,0:T(8,128)S(1)} %get-tuple-element.15.refs_0_), channel_id=1, source_target_pairs={{0,4},{1,5},{2,6},{3,7},{4,0},{5,1},{6,2},{7,3},{8,12},{9,13},{10,... | collective-permute-start | bytes 393224 | tf_op jit(solution)/shard_map/ppermute | solution.py:428
  24.5 5.7 %collective-permute-start = (f32[64,512]{1,0:T(8,128)S(1)}, f32[64,512]{1,0:T(8,128)S(1)}, u32[]{:S(2)}, u32[]{:S(2)}) collective-permute-start(f32[64,512]{1,0:T(8,128)S(1)} %get-tuple-element.15.refs_0_), channel_id=1, source_target_pairs={{0,2},{1,3},{2,0},{3,1},{4,6},{5,7},{6,4},{7,5},{8,10},{9,11},{10,... | collective-permute-start | bytes 393224 | tf_op jit(solution)/shard_map/ppermute | solution.py:428
  25.0 18.8 %all-to-all-start.1 = ((f32[8,2,32,512]{3,2,1,0:T(8,128)}), f32[8,2,32,512]{3,2,1,0:T(8,128)S(1)}, u32[]{:S(2)}, u32[]{:S(2)}) async-start(f32[8,2,32,512]{3,2,1,0:T(8,128)} %get-tuple-element.18), calls=%async_computation.1 | async-start | bytes 2097152 | tf_op jit(solution)/shard_map/all_to_all | solution.py:455
  30.2 2.0 %collective-permute-start.3 = (f32[4,64,512]{2,1,0:T(8,128)S(1)}, f32[4,64,512]{2,1,0:T(8,128)S(1)}, u32[]{:S(2)}, u32[]{:S(2)}) collective-permute-start(f32[4,64,512]{2,1,0:T(8,128)S(1)} %stack.2.near_ref), channel_id=1, source_target_pairs={{0,1},{1,0},{2,3},{3,2},{4,5},{5,4},{6,7},{7,6},{8,9},{9,8},{10,11... | collective-permute-start | bytes 1572872 | tf_op jit(solution)/shard_map/ppermute | solution.py:457
  32.9 6.6 %copy-start = (f32[512,512]{1,0:T(8,128)}, f32[512,512]{1,0:T(8,128)S(1)}, u32[]{:S(2)}) copy-start(f32[512,512]{1,0:T(8,128)S(1)} %get-tuple-element.17.panels_ref) | copy-start | bytes 3145732
  32.9 4.6 %collective-permute-start.4 = (f32[160,128]{1,0:T(8,128)S(1)}, f32[160,128]{1,0:T(8,128)S(1)}, u32[]{:S(2)}, u32[]{:S(2)}) collective-permute-start(f32[160,128]{1,0:T(8,128)S(1)} %get-tuple-element.16), channel_id=1, source_target_pairs={{0,8},{8,0},{16,24},{24,16},{1,9},{9,1},{17,25},{25,17},{2,10},{10... | collective-permute-start | bytes 245768 | tf_op jit(solution)/shard_map/ppermute | solution.py:439
  37.5 5.5 %collective-permute-start.5 = (f32[160,128]{1,0:T(8,128)S(1)}, f32[160,128]{1,0:T(8,128)S(1)}, u32[]{:S(2)}, u32[]{:S(2)}) collective-permute-start(f32[160,128]{1,0:T(8,128)S(1)} %add.4.left_ref), channel_id=1, source_target_pairs={{0,24},{8,16},{16,8},{24,0},{1,25},{9,17},{17,9},{25,1},{2,26},{10... | collective-permute-start | bytes 245768 | tf_op jit(solution)/shard_map/ppermute | solution.py:441
  46.7 28.7 %all-to-all-start.2 = ((f32[4,512,128]{2,1,0:T(8,128)}), f32[4,512,128]{2,1,0:T(8,128)}, u32[]{:S(2)}, u32[]{:S(2)}) async-start(f32[4,512,128]{2,1,0:T(8,128)} %multiply.1.refs_4_), calls=%async_computation.2 | async-start | bytes 2097152 | tf_op jit(solution)/shard_map/all_to_all | solution.py:464
  52.0 5.7 %collective-permute-start.8 = (f32[160,128]{1,0:T(8,128)S(1)}, f32[160,128]{1,0:T(8,128)S(1)}, u32[]{:S(2)}, u32[]{:S(2)}) collective-permute-start(f32[160,128]{1,0:T(8,128)S(1)} %add.5.refs_0_), channel_id=1, source_target_pairs={{0,6},{1,7},{2,4},{3,5},{4,2},{5,3},{6,0},{7,1},{8,14},{9,15},{10,... | collective-permute-start | bytes 245768 | tf_op jit(solution)/shard_map/ppermute | solution.py:428
  53.5 5.0 %collective-permute-start.7 = (f32[160,128]{1,0:T(8,128)S(1)}, f32[160,128]{1,0:T(8,128)S(1)}, u32[]{:S(2)}, u32[]{:S(2)}) collective-permute-start(f32[160,128]{1,0:T(8,128)S(1)} %add.5.refs_0_), channel_id=1, source_target_pairs={{0,4},{1,5},{2,6},{3,7},{4,0},{5,1},{6,2},{7,3},{8,12},{9,13},{10,... | collective-permute-start | bytes 245768 | tf_op jit(solution)/shard_map/ppermute | solution.py:428
  55.0 4.4 %collective-permute-start.6 = (f32[160,128]{1,0:T(8,128)S(1)}, f32[160,128]{1,0:T(8,128)S(1)}, u32[]{:S(2)}, u32[]{:S(2)}) collective-permute-start(f32[160,128]{1,0:T(8,128)S(1)} %add.5.refs_0_), channel_id=1, source_target_pairs={{0,2},{1,3},{2,0},{3,1},{4,6},{5,7},{6,4},{7,5},{8,10},{9,11},{10,... | collective-permute-start | bytes 245768 | tf_op jit(solution)/shard_map/ppermute | solution.py:428
  59.5 1.7 %collective-permute-start.9 = (f32[4,160,128]{2,1,0:T(8,128)S(1)}, f32[4,160,128]{2,1,0:T(8,128)S(1)}, u32[]{:S(2)}, u32[]{:S(2)}) collective-permute-start(f32[4,160,128]{2,1,0:T(8,128)S(1)} %stack.3.refs_0_), channel_id=1, source_target_pairs={{0,1},{1,0},{2,3},{3,2},{4,5},{5,4},{6,7},{7,6},{8,9},{9,8},{10,11... | collective-permute-start | bytes 983048 | tf_op jit(solution)/shard_map/ppermute | solution.py:466
  76.7 12.1 %collective-permute-start.12 = (f32[512,128]{1,0:T(8,128)S(1)}, f32[512,128]{1,0:T(8,128)S(1)}, u32[]{:S(2)}, u32[]{:S(2)}) collective-permute-start(f32[512,128]{1,0:T(8,128)S(1)} %total.1.refs_2_.refs_3_), channel_id=1, source_target_pairs={{0,8},{8,0},{16,24},{24,16},{1,9},{9,1},{17,25},{25,17},{2,10},{10... | collective-permute-start | bytes 786440 | tf_op jit(solution)/shard_map/ppermute | solution.py:474
  79.4 18.2 %collective-permute-start.11 = (f32[512,128]{1,0:T(8,128)S(1)}, f32[512,128]{1,0:T(8,128)S(1)}, u32[]{:S(2)}, u32[]{:S(2)}) collective-permute-start(f32[512,128]{1,0:T(8,128)S(1)} %total.1.refs_2_.refs_3_), channel_id=1, source_target_pairs={{0,16},{8,24},{16,0},{24,8},{1,17},{9,25},{17,1},{25,9},{2,18},{10... | collective-permute-start | bytes 786440 | tf_op jit(solution)/shard_map/ppermute | solution.py:474
  79.7 23.5 %collective-permute-start.10 = (f32[512,128]{1,0:T(8,128)S(1)}, f32[512,128]{1,0:T(8,128)S(1)}, u32[]{:S(2)}, u32[]{:S(2)}) collective-permute-start(f32[512,128]{1,0:T(8,128)S(1)} %total.1.refs_2_.refs_3_), channel_id=1, source_target_pairs={{0,24},{8,16},{16,8},{24,0},{1,25},{9,17},{17,9},{25,1},{2,26},{10... | collective-permute-start | bytes 786440 | tf_op jit(solution)/shard_map/ppermute | solution.py:474
  81.0 4.3 %copy-start.1 = (f32[512,512]{1,0:T(8,128)S(1)}, f32[512,512]{1,0:T(8,128)}, u32[]{:S(2)}) copy-start(f32[512,512]{1,0:T(8,128)} %copy-done) | copy-start | bytes 3145732

commit v8 on v7

--- a/solution.py
+++ b/solution.py
@@ -276,48 +276,94 @@
     )(left, right, *after)
 
 
-def multiply_kernel(turned_ref, front_ref, *refs):
+def multiply_kernel(index, turned_ref, front_ref, *refs):
     out_ref, held_ref, sems = refs[-3:]
-    count, _, width = out_ref.shape
-    step = max(width, PANEL)
-    copies = []
-    for lane in range(0, count * width, step):
-        product = dot(turned_ref[...], front_ref[:, lane : lane + step], ((1,), (0,)))
-        for at in range(0, step, width):
-            n = (lane + at) // width
-            held_ref[n] = product[:, at : at + width]
-            copies.append(pltpu.make_async_copy(held_ref.at[n], out_ref.at[n], sems.at[n]))
-            copies[-1].start()
+    count, rows, width = out_ref.shape
+    right = front_ref[:, index * width : (index + 1) * width]
+    held_ref[...] = dot(turned_ref[...], right, ((1,), (0,)))
+    copies = [
+        pltpu.make_async_copy(held_ref.at[pl.ds(n * rows, rows)], out_ref.at[n], sems.at[n])
+        for n in range(count)
+    ]
+    for copy in copies:
+        copy.start()
     for copy in copies:
         copy.wait()
 
 
-def multiply(turned_panels, front, count, after):
+def multiply(index, turned_panels, front, count, after):
     both = turned_panels.shape[0]
-    part = (count, both, front.shape[1] // count)
-    return pl.pallas_call(
-        multiply_kernel,
-        out_shape=shape(*part),
+    return pl.pallas_call(
+        lambda *refs: multiply_kernel(index, *refs),
+        out_shape=shape(count, both // count, PANEL),
         in_specs=[VMEM, VMEM] + [ANY] * len(after),
         out_specs=ANY,
-        scratch_shapes=[pltpu.VMEM(part, F32), pltpu.SemaphoreType.DMA((count,))],
+        scratch_shapes=[pltpu.VMEM((both, PANEL), F32), pltpu.SemaphoreType.DMA((count,))],
         compiler_params=KERNEL,
         cost_estimate=cost(1000, 1000),
         name="multiply",
     )(turned_panels, front, *after)
 
 
-def hold(array, after):
-    return pl.pallas_call(
-        lambda *refs: None,
-        out_shape=shape(*array.shape),
-        in_specs=[ANY] * (1 + len(after)),
-        out_specs=ANY,
-        input_output_aliases={0: 0},
-        compiler_params=KERNEL,
-        cost_estimate=cost(1000, 1000),
-        name="hold",
-    )(array, *after)
+def multiply_apart_kernel(index, masks, turned_ref, front_ref, *refs):
+    out_refs, held_ref = refs[-1 - len(masks) : -1], refs[-1]
+    rows, width = out_refs[0].shape
+    right = front_ref[:, index * width : (index + 1) * width]
+    held_ref[...] = dot(turned_ref[...], right, ((1,), (0,)))
+    place = lax.axis_index("row")
+    for out_ref, mask in zip(out_refs, masks):
+        at = pl.multiple_of(lax.bitwise_xor(place, mask) * rows, rows)
+        out_ref[...] = held_ref[pl.ds(at, rows), :]
+
+
+def multiply_apart(index, turned_panels, front, masks, after):
+    both = turned_panels.shape[0]
+    part = (both // len(masks), PANEL)
+    return pl.pallas_call(
+        lambda *refs: multiply_apart_kernel(index, masks, *refs),
+        out_shape=[shape(*part)] * len(masks),
+        in_specs=[VMEM, VMEM] + [ANY] * len(after),
+        out_specs=[VMEM] * len(masks),
+        scratch_shapes=[pltpu.VMEM((both, PANEL), F32)],
+        compiler_params=KERNEL,
+        cost_estimate=cost(1000, 1000),
+        name="multiply",
+    )(turned_panels, front, *after)
+
+
+def sum_kernel(count, *refs):
+    total = refs[0][...]
+    for ref in refs[1:count]:
+        total = total + ref[...]
+    refs[-1][...] = total
+
+
+def sum_of(parts, after):
+    return pl.pallas_call(
+        lambda *refs: sum_kernel(len(parts), *refs),
+        out_shape=shape(*parts[0].shape),
+        in_specs=[VMEM] * len(parts) + [ANY] * len(after),
+        out_specs=VMEM,
+        compiler_params=KERNEL,
+        cost_estimate=cost(1000, 1000),
+        name="total",
+    )(*parts, *after)
+
+
+def basis_kernel(panels_ref, inv_ref, *refs):
+    refs[-1][...] = dot(panels_ref[...], inv_ref[...], ((1,), (1,)))
+
+
+def basis_of(panels, inv, after):
+    return pl.pallas_call(
+        basis_kernel,
+        out_shape=shape(*panels.shape),
+        in_specs=[VMEM, VMEM] + [ANY] * len(after),
+        out_specs=VMEM,
+        compiler_params=KERNEL,
+        cost_estimate=cost(1000, 1000),
+        name="basis",
+    )(panels, inv, *after)
 
 
 def total_kernel(parts_ref, *refs):
@@ -352,72 +398,65 @@
     )(parts, *after)
 
 
-def finish_kernel(masks, inv_ref, basis_ref, front_ref, *refs):
+def finish_kernel(index, masks, inv_ref, basis_ref, front_ref, *refs):
     upper_ref, trail_ref, m_ref, w_ref, f_ref, sems = refs[-6:]
-    owners, two, part, total = front_ref.shape
-    both = inv_ref.shape[0]
-    width = refs[0].shape[1]
-    columns = []
-    for n, mask in enumerate(masks):
-        m_ref[:, n * width : (n + 1) * width] = refs[n][...]
-        if width == total:
-            columns.append(pl.ds(0, width))
-        else:
-            at = lax.bitwise_xor(lax.axis_index("row"), mask) * width
-            columns.append(pl.ds(pl.multiple_of(at, LANES), width))
+    owners, two, part, _ = front_ref.shape
+    both, width = m_ref.shape
+    place = lax.axis_index("row")
+    for ref, mask in zip(refs, masks):
+        count = ref.shape[0]
+        at = pl.multiple_of(lax.bitwise_xor(place, mask) * count, count)
+        m_ref[pl.ds(at, count), :] = ref[...]
+    columns = pl.ds(index * width, width)
     copies = []
     for step in range(both // LANES):
         lo, hi = step * LANES, (step + 1) * LANES
         w_ref[lo:hi, :] = dot(inv_ref[lo:hi, :hi], m_ref[:hi, :], ((1,), (0,)))
-        for n in range(len(masks)):
-            held = w_ref.at[lo:hi, pl.ds(n * width, width)]
-            goal = upper_ref.at[lo:hi, columns[n]]
-            copies.append(pltpu.make_async_copy(held, goal, sems.at[0, n, step]))
-            copies[-1].start()
+        copies.append(
+            pltpu.make_async_copy(w_ref.at[lo:hi], upper_ref.at[lo:hi, columns], sems.at[0, step])
+        )
+        copies[-1].start()
     rows = LANES // two
     held_owners = rows // part
     for step in range(owners // held_owners):
         lo = step * LANES
         product = dot(basis_ref[lo : lo + LANES, :], w_ref[...], ((1,), (0,)))
-        for n in range(len(masks)):
-            for owner in range(held_owners):
-                for child in range(two):
-                    row = (owner * two + child) * part
-                    at = step * rows + owner * part
-                    f_ref[n, child, at : at + part, :] = (
-                        front_ref[step * held_owners + owner, child, :, columns[n]]
-                        - product[row : row + part, n * width : (n + 1) * width]
-                    )
-            held = f_ref.at[n, :, pl.ds(step * rows, rows), :]
-            goal = trail_ref.at[:, pl.ds(step * rows, rows), columns[n]]
-            copies.append(pltpu.make_async_copy(held, goal, sems.at[1, n, step]))
-            copies[-1].start()
+        for owner in range(held_owners):
+            for child in range(two):
+                row = (owner * two + child) * part
+                at = step * rows + owner * part
+                f_ref[child, at : at + part, :] = (
+                    front_ref[step * held_owners + owner, child, :, columns]
+                    - product[row : row + part, :]
+                )
+        held = f_ref.at[:, pl.ds(step * rows, rows), :]
+        goal = trail_ref.at[:, pl.ds(step * rows, rows), columns]
+        copies.append(pltpu.make_async_copy(held, goal, sems.at[1, step]))
+        copies[-1].start()
     for copy in copies:
         copy.wait()
 
 
-def finish(pieces, inv, basis, front, given):
+def finish(index, inv, basis, front, masks, pieces, given):
     owners, two, part, total = front.shape
-    masks = [mask for mask, _ in pieces]
-    arrays = [array for _, array in pieces]
-    count = len(pieces)
-    both, width = arrays[0].shape
-    return pl.pallas_call(
-        lambda *refs: finish_kernel(masks, *refs),
+    both, width = inv.shape[0], pieces[0].shape[1]
+    taken = 3 + len(pieces)
+    return pl.pallas_call(
+        lambda *refs: finish_kernel(index, masks, *refs),
         out_shape=(shape(both, total), shape(two, owners * part, total)),
-        in_specs=[VMEM] * (3 + count) + [ANY] * len(given),
+        in_specs=[VMEM] * taken + [ANY] * len(given),
         out_specs=(ANY, ANY),
-        input_output_aliases={3 + count: 0, 4 + count: 1} if given else {},
+        input_output_aliases={taken: 0, taken + 1: 1} if given else {},
         scratch_shapes=[
-            pltpu.VMEM((both, count * width), F32),
-            pltpu.VMEM((both, count * width), F32),
-            pltpu.VMEM((count, two, owners * part, width), F32),
-            pltpu.SemaphoreType.DMA((2, count, both // LANES)),
+            pltpu.VMEM((both, width), F32),
+            pltpu.VMEM((both, width), F32),
+            pltpu.VMEM((two, owners * part, width), F32),
+            pltpu.SemaphoreType.DMA((2, both // LANES)),
         ],
         compiler_params=KERNEL,
         cost_estimate=cost(1000, 1000),
         name="finish",
-    )(inv, basis, front, *arrays, *given)
+    )(inv, basis, front, *pieces, *given)
 
 
 def pairs_xor(size, mask):
@@ -460,26 +499,29 @@
     tiles = even_pieces(tile, cols)
 
     flat = front.reshape(cols * 2 * part, width)
-    products = multiply(across, flat, rows, [tile])
+    masks = sorted(range(rows), key=lambda k: (k.bit_length(), -k))
+    products = multiply(0, across, flat, rows, [tile])
     parts = lax.all_to_all(products, "row", 0, 0, tiled=True)
-    near = stack_after(tiles, [products])
+    apart = multiply_apart(1, across, flat, masks, [tile, products])
+    rest = [apart[0]] + [
+        lax.ppermute(x, "row", pairs_xor(rows, k)) for k, x in zip(masks[1:], apart[1:])
+    ]
+    near = stack_after(tiles, [products, apart[0]])
     state = near, lax.ppermute(near, "col", pairs_xor(cols, 1))
-    for lo in range(0, both - LANES, LANES):
-        state = stage(lo, state)
-    mine = total_of(parts, state[1:])
-    _, inv = stage(both - LANES, state, [mine])
-    basis = dot(panels, inv, ((1,), (1,)))
-    masks = sorted(range(1, rows), key=lambda k: (k.bit_length(), -k))
-    pieces = [(0, mine)]
-    pieces += [(k, lax.ppermute(mine, "row", pairs_xor(rows, k))) for k in masks]
-    if mine.shape[1] % LANES:
-        place = lax.axis_index("row")
-        ordered = jnp.stack([piece for _, piece in sorted(pieces, key=lambda p: p[0])])
-        ordered = jnp.take(ordered, jnp.arange(rows, dtype=jnp.int32) ^ place, axis=0)
-        pieces = [(0, ordered.transpose(1, 0, 2).reshape(both, width))]
+    state = stage(0, state)
+    first = total_of(parts, state[1:])
+    state = stage(LANES, state, [first])
+    state = stage(2 * LANES, state)
+    second = sum_of(rest, state[1:])
+    groups = [
+        [total] + [lax.ppermute(total, "row", pairs_xor(rows, k)) for k in masks[1:]]
+        for total in (first, second)
+    ]
+    _, inv = stage(3 * LANES, state, [second])
+    basis = basis_of(panels, inv, groups[0][1:])
     outs = ()
-    for n in range(0, len(pieces), 2):
-        outs = finish(pieces[n : n + 2], inv, basis, front, outs)
+    for n, pieces in enumerate(groups):
+        outs = finish(n, inv, basis, front, masks, pieces, outs)
     return outs
 
 

time: 107 us -> 103 us (0.963)
  waiting for transfers between devices: 28.4 us -> 12.8 us
  starting transfers between devices: 23.8 us -> 33 us
  Pallas kernels: 32.8 us -> 36.3 us
  matrix products: 1.86 us -> 0 us
    ppermute x3 -> x9, waiting for transfers between devices: 12.3 us -> 0.23 us  [the longest x6 0.22 us: per_device(): lax.ppermute(total, 'row', pairs_xor(rows, k))]
    ppermute x3 -> x9, starting transfers between devices: 4.3 us -> 13.4 us  [the longest x6 8.98 us: per_device(): lax.ppermute(total, 'row', pairs_xor(rows, k))]
    pallas_call x3 -> x6, Pallas kernels: 10.2 us -> 13.9 us  [the longest x2 7.35 us: finish(): pl.pallas_call(lambda *refs: finish_kernel(index, masks, *refs), out_shap...]
    ppermute x6, waiting for transfers between devices: 4.09 us -> 2.21 us  [even_pieces(): lax.ppermute(piece, 'col', pairs_xor(size, k))]
    dot_general x1 -> x0, matrix products: 1.86 us -> none  [dot(): lax.dot_general(left, right, (contract, ((), ())), precision=lax.Precisio...]
    ppermute x1, waiting for transfers between devices: 1.62 us -> 0.01 us  [per_device(): state = (near, lax.ppermute(near, 'col', pairs_xor(cols, 1)))]
  transfers between devices with their start and end apart: 15 -> 21, of which waited for: 12 -> 9; matrix products, arithmetic and copies ran while one was open for 2% -> 0% of each run, Pallas kernels for 22% -> 28%
where the time goes in v8:
time: 103 us; the launch traced here: 102 us
  Pallas kernels  36.3 us (35%)
  starting transfers between devices  33 us (32%)
  blocking collectives  18 us (17%)
  waiting for transfers between devices  12.8 us (12%)
  local copies, waits for them, and re-layouts  1.23 us (1%)
    pallas_call x4, Pallas kernels, stage(): pl.pallas_call(lambda *refs: stage_kernel(lo, *refs), out_shape=(shape(si...  18.4 us
    all_to_all x1, blocking collectives, per_device(): spread = lax.all_to_all(pack(children, cols), 'col', 0, 0, tiled=True)  18 us
    ppermute x6, starting transfers between devices, per_device(): lax.ppermute(total, 'row', pairs_xor(rows, k))  8.98 us
    pallas_call x2, Pallas kernels, finish(): pl.pallas_call(lambda *refs: finish_kernel(index, masks, *refs), out_shap...  7.35 us
    ppermute x6, starting transfers between devices, even_pieces(): lax.ppermute(piece, 'col', pairs_xor(size, k))  6.98 us
    all_to_all x1, starting transfers between devices, per_device(): parts = lax.all_to_all(products, 'row', 0, 0, tiled=True)  5.33 us
    all_to_all x1, starting transfers between devices, per_device(): front = lax.all_to_all(ordered, 'col', 0, 0, tiled=True)  4.93 us
    ppermute x3, starting transfers between devices, per_device(): lax.ppermute(x, 'row', pairs_xor(rows, k))  4.45 us
  transfers between devices with their start and end apart: 21, of which 9 were waited for; matrix products, arithmetic and copies ran while one was open for 0% of the time, Pallas kernels for 28%

profile of v8, /device:TPU:10, one launch (start us, length us, event | category | flops | bytes accessed | tf_op | source)
XLA Modules:
  0.0 102.3 jit_solution(16071515501061509464)
XLA Ops:
  0.6 1.2 %copy-done.2 = f32[2,256,512]{2,1,0:T(8,128)S(1)} copy-done((f32[2,256,512]{2,1,0:T(8,128)S(1)}, f32[2,256,512]{2,1,0:T(8,128)}, u32[]{:S(2)}) %copy-start.2) | copy-done | bytes 1048600
  1.9 0.1 pack.1
  1.9 18.0 %all_to_all.15.spread_ref = f32[8,2,32,512]{3,2,1,0:T(8,128)S(1)} all-to-all(f32[8,2,32,512]{3,2,1,0:T(8,128)S(1)} %pack.1), channel_id=1, replica_groups=mesh['row'=4,'col'=8] {'col'}, dimensions={0} | all-to-all | bytes 2097152 | tf_op jit(solution)/shard_map/all_to_all | solution.py:491
  19.9 1.7 %order.1 = (f32[8,2,32,512]{3,2,1,0:T(8,128)}, f32[64,512]{1,0:T(8,128)S(1)}) custom-call(s32[2,16]{1,0:T(2,128)S(1)} %copy-done.3, f32[8,2,32,512]{3,2,1,0:T(8,128)S(1)} %all_to_all.15.spread_ref), custom_call_target="tpu_custom_call" | custom-call | flops 1000 | bytes 1000 | tf_op jit(solution)/shard_map/order/pallas_call | solution.py:78
  21.6 1.5 %collective-permute-start.2 = (f32[64,512]{1,0:T(8,128)S(1)}, f32[64,512]{1,0:T(8,128)S(1)}, u32[]{:S(2)}, u32[]{:S(2)}) collective-permute-start(f32[64,512]{1,0:T(8,128)S(1)} %get-tuple-element.19.refs_0_), channel_id=1, source_target_pairs={{0,6},{1,7},{2,4},{3,5},{4,2},{5,3},{6,0},{7,1},{8,14},{9,15},{10,... | collective-permute-start | bytes 393224 | tf_op jit(solution)/shard_map/ppermute | solution.py:467
  23.0 1.5 %collective-permute-start.1 = (f32[64,512]{1,0:T(8,128)S(1)}, f32[64,512]{1,0:T(8,128)S(1)}, u32[]{:S(2)}, u32[]{:S(2)}) collective-permute-start(f32[64,512]{1,0:T(8,128)S(1)} %get-tuple-element.19.refs_0_), channel_id=1, source_target_pairs={{0,4},{1,5},{2,6},{3,7},{4,0},{5,1},{6,2},{7,3},{8,12},{9,13},{10,... | collective-permute-start | bytes 393224 | tf_op jit(solution)/shard_map/ppermute | solution.py:467
  24.5 0.6 collective-permute-start
  25.0 4.9 %all-to-all-start.1 = ((f32[8,2,32,512]{3,2,1,0:T(8,128)}), f32[8,2,32,512]{3,2,1,0:T(8,128)S(1)}, u32[]{:S(2)}, u32[]{:S(2)}) async-start(f32[8,2,32,512]{3,2,1,0:T(8,128)} %get-tuple-element.22), calls=%async_computation.1 | async-start | bytes 2097152 | tf_op jit(solution)/shard_map/all_to_all | solution.py:494
  30.0 0.2 collective-permute-done.1.refs_2_
  30.2 0.1 collective-permute-start.3
  30.3 1.9 %collective-permute-done.3.far_ref = f32[4,64,512]{2,1,0:T(8,128)S(1)} collective-permute-done((f32[4,64,512]{2,1,0:T(8,128)S(1)}, f32[4,64,512]{2,1,0:T(8,128)S(1)}, u32[]{:S(2)}, u32[]{:S(2)}) %collective-permute-start.3) | collective-permute-done | bytes 524320 | tf_op jit(solution)/shard_map/ppermute | solution.py:496
  32.2 0.7 tile.1
  32.9 0.0 copy-start
  32.9 0.5 collective-permute-start.4
  33.4 4.0 %collective-permute-done.4 = f32[160,128]{1,0:T(8,128)S(1)} collective-permute-done((f32[160,128]{1,0:T(8,128)S(1)}, f32[160,128]{1,0:T(8,128)S(1)}, u32[]{:S(2)}, u32[]{:S(2)}) %collective-permute-start.4) | collective-permute-done | bytes 81952 | tf_op jit(solution)/shard_map/ppermute | solution.py:478
  37.5 1.6 %collective-permute-start.5 = (f32[160,128]{1,0:T(8,128)S(1)}, f32[160,128]{1,0:T(8,128)S(1)}, u32[]{:S(2)}, u32[]{:S(2)}) collective-permute-start(f32[160,128]{1,0:T(8,128)S(1)} %add.4.left_ref), channel_id=1, source_target_pairs={{0,24},{8,16},{16,8},{24,0},{1,25},{9,17},{17,9},{25,1},{2,26},{10... | collective-permute-start | bytes 245768 | tf_op jit(solution)/shard_map/ppermute | solution.py:480
  39.1 0.3 turn.1.refs_0_
  39.4 3.5 %collective-permute-done.5.right_ref = f32[160,128]{1,0:T(8,128)S(1)} collective-permute-done((f32[160,128]{1,0:T(8,128)S(1)}, f32[160,128]{1,0:T(8,128)S(1)}, u32[]{:S(2)}, u32[]{:S(2)}) %collective-permute-start.5) | collective-permute-done | bytes 81952 | tf_op jit(solution)/shard_map/ppermute | solution.py:480
  43.0 0.9 all-to-all-done.1.refs_2_
  43.9 1.9 %multiply.2.refs_3_.refs_4_ = f32[4,128,256]{2,1,0:T(8,128)} custom-call(f32[512,512]{1,0:T(8,128)S(1)} %turn.1.refs_0_, f32[512,512]{1,0:T(8,128)S(1)} %bitcast.1, f32[160,128]{1,0:T(8,128)S(1)} %add.5.refs_2_.refs_0_), custom_call_target="tpu_custom_call" | custom-call | flops 1000 | bytes 1000 | tf_op jit(solution)/shard_map/multiply/pallas_call | solution.py:296
  45.8 5.3 %all-to-all-start.2 = ((f32[4,128,256]{2,1,0:T(8,128)}), f32[4,128,256]{2,1,0:T(8,128)}, u32[]{:S(2)}, u32[]{:S(2)}) async-start(f32[4,128,256]{2,1,0:T(8,128)} %multiply.2.refs_3_.refs_4_), calls=%async_computation.2 | async-start | bytes 1048576 | tf_op jit(solution)/shard_map/all_to_all | solution.py:504
  51.1 1.5 %collective-permute-start.8 = (f32[160,128]{1,0:T(8,128)S(1)}, f32[160,128]{1,0:T(8,128)S(1)}, u32[]{:S(2)}, u32[]{:S(2)}) collective-permute-start(f32[160,128]{1,0:T(8,128)S(1)} %add.5.refs_2_.refs_0_), channel_id=1, source_target_pairs={{0,6},{1,7},{2,4},{3,5},{4,2},{5,3},{6,0},{7,1},{8,14},{9,15},{10,... | collective-permute-start | bytes 245768 | tf_op jit(solution)/shard_map/ppermute | solution.py:467
  52.6 1.5 %collective-permute-start.7 = (f32[160,128]{1,0:T(8,128)S(1)}, f32[160,128]{1,0:T(8,128)S(1)}, u32[]{:S(2)}, u32[]{:S(2)}) collective-permute-start(f32[160,128]{1,0:T(8,128)S(1)} %add.5.refs_2_.refs_0_), channel_id=1, source_target_pairs={{0,4},{1,5},{2,6},{3,7},{4,0},{5,1},{6,2},{7,3},{8,12},{9,13},{10,... | collective-permute-start | bytes 245768 | tf_op jit(solution)/shard_map/ppermute | solution.py:467
  54.1 0.5 collective-permute-start.6
  54.6 1.9 %multiply.3 = (f32[128,256]{1,0:T(8,128)S(1)}, f32[128,256]{1,0:T(8,128)}, f32[128,256]{1,0:T(8,128)}, f32[128,256]{1,0:T(8,128)}) custom-call(f32[512,512]{1,0:T(8,128)S(1)} %turn.1.refs_0_, f32[512,512]{1,0:T(8,128)S(1)} %bitcast.2, f32[160,128]{1,0:T(8,128)S(1)} %add.5.refs_2_.refs_0_, f32[4,128,256]{2,1,0:T(8,128)} %multiply.2.refs_3_.refs_4_), custom_call_target="tpu_custom_call" | custom-call | flops 1000 | bytes 1000 | tf_op jit(solution)/shard_map/multiply/pallas_call | solution.py:322
  56.5 0.3 collective-permute-done.8.refs_3_
  56.8 0.8 collective-permute-done.7.refs_2_
  57.6 0.9 collective-permute-done.6.refs_1_
  58.6 0.1 collective-permute-start.9
  58.7 0.1 collective-permute-start.10
  58.7 2.9 %collective-permute-start.11 = (f32[128,256]{1,0:T(8,128)}, f32[128,256]{1,0:T(8,128)S(1)}, u32[]{:S(2)}, u32[]{:S(2)}) collective-permute-start(f32[128,256]{1,0:T(8,128)} %get-tuple-element.31), channel_id=1, source_target_pairs={{0,24},{8,16},{16,8},{24,0},{1,25},{9,17},{17,9},{25,1},{2,26},{10... | collective-permute-start | bytes 393224 | tf_op jit(solution)/shard_map/ppermute | solution.py:507
  61.7 1.5 %collective-permute-start.12 = (f32[128,256]{1,0:T(8,128)}, f32[128,256]{1,0:T(8,128)}, u32[]{:S(2)}, u32[]{:S(2)}) collective-permute-start(f32[128,256]{1,0:T(8,128)} %get-tuple-element.32), channel_id=1, source_target_pairs={{0,16},{8,24},{16,0},{24,8},{1,17},{9,25},{17,1},{25,9},{2,18},{10... | collective-permute-start | bytes 393224 | tf_op jit(solution)/shard_map/ppermute | solution.py:507
  63.1 4.9 %stage.4 = (f32[512,512]{1,0:T(8,128)S(1)}, f32[512,512]{1,0:T(8,128)S(1)}) custom-call(f32[4,160,128]{2,1,0:T(8,128)S(1)} %stack.3.refs_0_, f32[4,160,128]{2,1,0:T(8,128)S(1)} %collective-permute-done.9.refs_1_), custom_call_target="tpu_custom_call" | custom-call | flops 1000 | bytes 1000 | tf_op jit(solution)/shard_map/stage/pallas_call | solution.py:217
  68.1 1.1 %total.2.refs_2_.refs_3_ = f32[128,256]{1,0:T(8,128)S(1)} custom-call(f32[4,128,256]{2,1,0:T(8,128)} %all-to-all-done.2.parts_ref, f32[512,512]{1,0:T(8,128)S(1)} %get-tuple-element.25.refs_0_.refs_1_), custom_call_target="tpu_custom_call" | custom-call | flops 1000 | bytes 1000 | tf_op jit(solution)/shard_map/total/pallas_call | solution.py:386
  69.2 1.5 %collective-permute-start.15 = (f32[128,256]{1,0:T(8,128)S(1)}, f32[128,256]{1,0:T(8,128)S(1)}, u32[]{:S(2)}, u32[]{:S(2)}) collective-permute-start(f32[128,256]{1,0:T(8,128)S(1)} %total.2.refs_2_.refs_3_), channel_id=1, source_target_pairs={{0,16},{8,24},{16,0},{24,8},{1,17},{9,25},{17,1},{25,9},{2,18},{10... | collective-permute-start | bytes 393224 | tf_op jit(solution)/shard_map/ppermute | solution.py:517
  70.7 0.1 collective-permute-start.14
  70.8 4.7 %stage.5 = (f32[512,512]{1,0:T(8,128)S(1)}, f32[512,512]{1,0:T(8,128)S(1)}) custom-call(f32[512,512]{1,0:T(8,128)S(1)} %get-tuple-element.24.refs_0_, f32[512,512]{1,0:T(8,128)S(1)} %get-tuple-element.25.refs_0_.refs_1_, f32[128,256]{1,0:T(8,128)S(1)} %total.2.refs_2_.refs_3_), custom_call_target="tpu_custom_call", output_to_operand_aliasing={{0}: (0, {}), {1}: (1, {})} | custom-call | flops 1000 | bytes 1000 | tf_op jit(solution)/shard_map/stage/pallas_call | solution.py:217
  75.6 4.5 %stage.6 = (f32[512,512]{1,0:T(8,128)S(1)}, f32[512,512]{1,0:T(8,128)S(1)}) custom-call(f32[512,512]{1,0:T(8,128)S(1)} %get-tuple-element.26.refs_0_, f32[512,512]{1,0:T(8,128)S(1)} %get-tuple-element.27.refs_1_), custom_call_target="tpu_custom_call", output_to_operand_aliasing={{0}: (0, {}), {1}: (1, {})} | custom-call | flops 1000 | bytes 1000 | tf_op jit(solution)/shard_map/stage/pallas_call | solution.py:217
  80.1 2.9 %collective-permute-start.13 = (f32[128,256]{1,0:T(8,128)S(1)}, f32[128,256]{1,0:T(8,128)S(1)}, u32[]{:S(2)}, u32[]{:S(2)}) collective-permute-start(f32[128,256]{1,0:T(8,128)S(1)} %total.2.refs_2_.refs_3_), channel_id=1, source_target_pairs={{0,8},{8,0},{16,24},{24,16},{1,9},{9,1},{17,25},{25,17},{2,10},{10... | collective-permute-start | bytes 393224 | tf_op jit(solution)/shard_map/ppermute | solution.py:517
  83.0 0.9 total.3.refs_2_.refs_3_
  84.0 1.0 collective-permute-start.18
  85.0 1.3 %collective-permute-start.17 = (f32[128,256]{1,0:T(8,128)S(1)}, f32[128,256]{1,0:T(8,128)S(1)}, u32[]{:S(2)}, u32[]{:S(2)}) collective-permute-start(f32[128,256]{1,0:T(8,128)S(1)} %total.3.refs_2_.refs_3_), channel_id=1, source_target_pairs={{0,24},{8,16},{16,8},{24,0},{1,25},{9,17},{17,9},{25,1},{2,26},{10... | collective-permute-start | bytes 393224 | tf_op jit(solution)/shard_map/ppermute | solution.py:517
  86.3 2.1 %collective-permute-start.16 = (f32[128,256]{1,0:T(8,128)S(1)}, f32[128,256]{1,0:T(8,128)S(1)}, u32[]{:S(2)}, u32[]{:S(2)}) collective-permute-start(f32[128,256]{1,0:T(8,128)S(1)} %total.3.refs_2_.refs_3_), channel_id=1, source_target_pairs={{0,8},{8,0},{16,24},{24,16},{1,9},{9,1},{17,25},{25,17},{2,10},{10... | collective-permute-start | bytes 393224 | tf_op jit(solution)/shard_map/ppermute | solution.py:517
  88.4 4.2 %stage.7 = (f32[512,512]{1,0:T(8,128)S(1)}, f32[512,512]{1,0:T(8,128)S(1)}) custom-call(f32[512,512]{1,0:T(8,128)S(1)} %get-tuple-element.28.refs_0_, f32[512,512]{1,0:T(8,128)S(1)} %get-tuple-element.29.refs_4_.refs_1_, f32[128,256]{1,0:T(8,128)S(1)} %total.3.refs_2_.refs_3_), custom_call_target="tpu_custom_call", output_to_operand_aliasing={{0}: (0, {}), {1}: (1, {})} | custom-call | flops 1000 | bytes 1000 | tf_op jit(solution)/shard_map/stage/pallas_call | solution.py:217
  92.7 0.2 collective-permute-done.14.refs_1_.refs_5_
  92.9 1.8 %basis.1.refs_1_ = f32[512,512]{1,0:T(8,128)S(1)} custom-call(f32[512,512]{1,0:T(8,128)S(1)} %copy-done.1, f32[512,512]{1,0:T(8,128)S(1)} %get-tuple-element.33.inv_ref.refs_0_, f32[128,256]{1,0:T(8,128)S(1)} %collective-permute-done.13.refs_0_.refs_4_, f32[128,256]{1,0:T(8,128)S(1)} %collective-permute-done.14.refs_1_.refs_5_, ...), custom_call_target="tpu_custom_call" | custom-call | flops 1000 | bytes 1000 | tf_op jit(solution)/shard_map/basis/pallas_call | solution.py:358
  94.7 3.7 %finish.2 = (f32[512,512]{1,0:T(8,128)}, f32[2,256,512]{2,1,0:T(8,128)}) custom-call(f32[512,512]{1,0:T(8,128)S(1)} %get-tuple-element.33.inv_ref.refs_0_, f32[512,512]{1,0:T(8,128)S(1)} %basis.1.refs_1_, f32[8,2,32,512]{3,2,1,0:T(8,128)S(1)} %all-to-all-done.1.refs_2_, f32[128,256]{1,0:T(8,128)S(1)} %total.2.refs_2_.refs_3_, ...), custom_call_target="tpu_custom_call" | custom-call | flops 1000 | bytes 1000 | tf_op jit(solution)/shard_map/finish/pallas_call | solution.py:444
  98.4 3.7 %finish.3 = (f32[512,512]{1,0:T(8,128)}, f32[2,256,512]{2,1,0:T(8,128)}) custom-call(f32[512,512]{1,0:T(8,128)S(1)} %get-tuple-element.33.inv_ref.refs_0_, f32[512,512]{1,0:T(8,128)S(1)} %basis.1.refs_1_, f32[8,2,32,512]{3,2,1,0:T(8,128)S(1)} %all-to-all-done.1.refs_2_, ...), custom_call_target="tpu_custom_call", output_to_operand_aliasing={{0}: (7, {}), {1}: (8, {})} | custom-call | flops 1000 | bytes 1000 | tf_op jit(solution)/shard_map/finish/pallas_call | solution.py:444
  (22 shorter events, 0.1 us)
Async XLA Ops:
  0.6 1.2 %copy-start.2 = (f32[2,256,512]{2,1,0:T(8,128)S(1)}, f32[2,256,512]{2,1,0:T(8,128)}, u32[]{:S(2)}) copy-start(f32[2,256,512]{2,1,0:T(8,128)} %children_ref.1) | copy-start | bytes 3145732
  1.9 18.0 %copy-start.3 = (s32[2,16]{1,0:T(2,128)S(1)}, s32[2,16]{1,0:T(2,128)}, u32[]{:S(2)}) copy-start(s32[2,16]{1,0:T(2,128)} %maps_ref.1) | copy-start | bytes 388
  21.6 8.4 %collective-permute-start.2 = (f32[64,512]{1,0:T(8,128)S(1)}, f32[64,512]{1,0:T(8,128)S(1)}, u32[]{:S(2)}, u32[]{:S(2)}) collective-permute-start(f32[64,512]{1,0:T(8,128)S(1)} %get-tuple-element.19.refs_0_), channel_id=1, source_target_pairs={{0,6},{1,7},{2,4},{3,5},{4,2},{5,3},{6,0},{7,1},{8,14},{9,15},{10,... | collective-permute-start | bytes 393224 | tf_op jit(solution)/shard_map/ppermute | solution.py:467
  23.0 7.1 %collective-permute-start.1 = (f32[64,512]{1,0:T(8,128)S(1)}, f32[64,512]{1,0:T(8,128)S(1)}, u32[]{:S(2)}, u32[]{:S(2)}) collective-permute-start(f32[64,512]{1,0:T(8,128)S(1)} %get-tuple-element.19.refs_0_), channel_id=1, source_target_pairs={{0,4},{1,5},{2,6},{3,7},{4,0},{5,1},{6,2},{7,3},{8,12},{9,13},{10,... | collective-permute-start | bytes 393224 | tf_op jit(solution)/shard_map/ppermute | solution.py:467
  24.5 5.7 %collective-permute-start = (f32[64,512]{1,0:T(8,128)S(1)}, f32[64,512]{1,0:T(8,128)S(1)}, u32[]{:S(2)}, u32[]{:S(2)}) collective-permute-start(f32[64,512]{1,0:T(8,128)S(1)} %get-tuple-element.19.refs_0_), channel_id=1, source_target_pairs={{0,2},{1,3},{2,0},{3,1},{4,6},{5,7},{6,4},{7,5},{8,10},{9,11},{10,... | collective-permute-start | bytes 393224 | tf_op jit(solution)/shard_map/ppermute | solution.py:467
  25.0 18.8 %all-to-all-start.1 = ((f32[8,2,32,512]{3,2,1,0:T(8,128)}), f32[8,2,32,512]{3,2,1,0:T(8,128)S(1)}, u32[]{:S(2)}, u32[]{:S(2)}) async-start(f32[8,2,32,512]{3,2,1,0:T(8,128)} %get-tuple-element.22), calls=%async_computation.1 | async-start | bytes 2097152 | tf_op jit(solution)/shard_map/all_to_all | solution.py:494
  30.2 2.0 %collective-permute-start.3 = (f32[4,64,512]{2,1,0:T(8,128)S(1)}, f32[4,64,512]{2,1,0:T(8,128)S(1)}, u32[]{:S(2)}, u32[]{:S(2)}) collective-permute-start(f32[4,64,512]{2,1,0:T(8,128)S(1)} %stack.2.near_ref), channel_id=1, source_target_pairs={{0,1},{1,0},{2,3},{3,2},{4,5},{5,4},{6,7},{7,6},{8,9},{9,8},{10,11... | collective-permute-start | bytes 1572872 | tf_op jit(solution)/shard_map/ppermute | solution.py:496
  32.9 6.6 %copy-start = (f32[512,512]{1,0:T(8,128)}, f32[512,512]{1,0:T(8,128)S(1)}, u32[]{:S(2)}) copy-start(f32[512,512]{1,0:T(8,128)S(1)} %get-tuple-element.21.panels_ref) | copy-start | bytes 3145732
  32.9 4.6 %collective-permute-start.4 = (f32[160,128]{1,0:T(8,128)S(1)}, f32[160,128]{1,0:T(8,128)S(1)}, u32[]{:S(2)}, u32[]{:S(2)}) collective-permute-start(f32[160,128]{1,0:T(8,128)S(1)} %get-tuple-element.20), channel_id=1, source_target_pairs={{0,8},{8,0},{16,24},{24,16},{1,9},{9,1},{17,25},{25,17},{2,10},{10... | collective-permute-start | bytes 245768 | tf_op jit(solution)/shard_map/ppermute | solution.py:478
  37.5 5.5 %collective-permute-start.5 = (f32[160,128]{1,0:T(8,128)S(1)}, f32[160,128]{1,0:T(8,128)S(1)}, u32[]{:S(2)}, u32[]{:S(2)}) collective-permute-start(f32[160,128]{1,0:T(8,128)S(1)} %add.4.left_ref), channel_id=1, source_target_pairs={{0,24},{8,16},{16,8},{24,0},{1,25},{9,17},{17,9},{25,1},{2,26},{10... | collective-permute-start | bytes 245768 | tf_op jit(solution)/shard_map/ppermute | solution.py:480
  45.8 22.3 %all-to-all-start.2 = ((f32[4,128,256]{2,1,0:T(8,128)}), f32[4,128,256]{2,1,0:T(8,128)}, u32[]{:S(2)}, u32[]{:S(2)}) async-start(f32[4,128,256]{2,1,0:T(8,128)} %multiply.2.refs_3_.refs_4_), calls=%async_computation.2 | async-start | bytes 1048576 | tf_op jit(solution)/shard_map/all_to_all | solution.py:504
  51.1 5.7 %collective-permute-start.8 = (f32[160,128]{1,0:T(8,128)S(1)}, f32[160,128]{1,0:T(8,128)S(1)}, u32[]{:S(2)}, u32[]{:S(2)}) collective-permute-start(f32[160,128]{1,0:T(8,128)S(1)} %add.5.refs_2_.refs_0_), channel_id=1, source_target_pairs={{0,6},{1,7},{2,4},{3,5},{4,2},{5,3},{6,0},{7,1},{8,14},{9,15},{10,... | collective-permute-start | bytes 245768 | tf_op jit(solution)/shard_map/ppermute | solution.py:467
  52.6 5.0 %collective-permute-start.7 = (f32[160,128]{1,0:T(8,128)S(1)}, f32[160,128]{1,0:T(8,128)S(1)}, u32[]{:S(2)}, u32[]{:S(2)}) collective-permute-start(f32[160,128]{1,0:T(8,128)S(1)} %add.5.refs_2_.refs_0_), channel_id=1, source_target_pairs={{0,4},{1,5},{2,6},{3,7},{4,0},{5,1},{6,2},{7,3},{8,12},{9,13},{10,... | collective-permute-start | bytes 245768 | tf_op jit(solution)/shard_map/ppermute | solution.py:467
  54.1 4.4 %collective-permute-start.6 = (f32[160,128]{1,0:T(8,128)S(1)}, f32[160,128]{1,0:T(8,128)S(1)}, u32[]{:S(2)}, u32[]{:S(2)}) collective-permute-start(f32[160,128]{1,0:T(8,128)S(1)} %add.5.refs_2_.refs_0_), channel_id=1, source_target_pairs={{0,2},{1,3},{2,0},{3,1},{4,6},{5,7},{6,4},{7,5},{8,10},{9,11},{10,... | collective-permute-start | bytes 245768 | tf_op jit(solution)/shard_map/ppermute | solution.py:467
  58.6 4.5 %collective-permute-start.9 = (f32[4,160,128]{2,1,0:T(8,128)S(1)}, f32[4,160,128]{2,1,0:T(8,128)S(1)}, u32[]{:S(2)}, u32[]{:S(2)}) collective-permute-start(f32[4,160,128]{2,1,0:T(8,128)S(1)} %stack.3.refs_0_), channel_id=1, source_target_pairs={{0,1},{1,0},{2,3},{3,2},{4,5},{5,4},{6,7},{7,6},{8,9},{9,8},{10,11... | collective-permute-start | bytes 983048 | tf_op jit(solution)/shard_map/ppermute | solution.py:510
  58.7 21.4 %collective-permute-start.10 = (f32[128,256]{1,0:T(8,128)}, f32[128,256]{1,0:T(8,128)S(1)}, u32[]{:S(2)}, u32[]{:S(2)}) collective-permute-start(f32[128,256]{1,0:T(8,128)} %get-tuple-element.30), channel_id=1, source_target_pairs={{0,8},{8,0},{16,24},{24,16},{1,9},{9,1},{17,25},{25,17},{2,10},{10... | collective-permute-start | bytes 393224 | tf_op jit(solution)/shard_map/ppermute | solution.py:507
  58.7 24.3 %collective-permute-start.11 = (f32[128,256]{1,0:T(8,128)}, f32[128,256]{1,0:T(8,128)S(1)}, u32[]{:S(2)}, u32[]{:S(2)}) collective-permute-start(f32[128,256]{1,0:T(8,128)} %get-tuple-element.31), channel_id=1, source_target_pairs={{0,24},{8,16},{16,8},{24,0},{1,25},{9,17},{17,9},{25,1},{2,26},{10... | collective-permute-start | bytes 393224 | tf_op jit(solution)/shard_map/ppermute | solution.py:507
  61.7 21.4 %collective-permute-start.12 = (f32[128,256]{1,0:T(8,128)}, f32[128,256]{1,0:T(8,128)}, u32[]{:S(2)}, u32[]{:S(2)}) collective-permute-start(f32[128,256]{1,0:T(8,128)} %get-tuple-element.32), channel_id=1, source_target_pairs={{0,16},{8,24},{16,0},{24,8},{1,17},{9,25},{17,1},{25,9},{2,18},{10... | collective-permute-start | bytes 393224 | tf_op jit(solution)/shard_map/ppermute | solution.py:507
  69.2 17.1 %collective-permute-start.15 = (f32[128,256]{1,0:T(8,128)S(1)}, f32[128,256]{1,0:T(8,128)S(1)}, u32[]{:S(2)}, u32[]{:S(2)}) collective-permute-start(f32[128,256]{1,0:T(8,128)S(1)} %total.2.refs_2_.refs_3_), channel_id=1, source_target_pairs={{0,16},{8,24},{16,0},{24,8},{1,17},{9,25},{17,1},{25,9},{2,18},{10... | collective-permute-start | bytes 393224 | tf_op jit(solution)/shard_map/ppermute | solution.py:517
  70.7 22.1 %collective-permute-start.14 = (f32[128,256]{1,0:T(8,128)S(1)}, f32[128,256]{1,0:T(8,128)S(1)}, u32[]{:S(2)}, u32[]{:S(2)}) collective-permute-start(f32[128,256]{1,0:T(8,128)S(1)} %total.2.refs_2_.refs_3_), channel_id=1, source_target_pairs={{0,24},{8,16},{16,8},{24,0},{1,25},{9,17},{17,9},{25,1},{2,26},{10... | collective-permute-start | bytes 393224 | tf_op jit(solution)/shard_map/ppermute | solution.py:517
  80.1 12.8 %collective-permute-start.13 = (f32[128,256]{1,0:T(8,128)S(1)}, f32[128,256]{1,0:T(8,128)S(1)}, u32[]{:S(2)}, u32[]{:S(2)}) collective-permute-start(f32[128,256]{1,0:T(8,128)S(1)} %total.2.refs_2_.refs_3_), channel_id=1, source_target_pairs={{0,8},{8,0},{16,24},{24,16},{1,9},{9,1},{17,25},{25,17},{2,10},{10... | collective-permute-start | bytes 393224 | tf_op jit(solution)/shard_map/ppermute | solution.py:517
  84.0 14.4 %collective-permute-start.18 = (f32[128,256]{1,0:T(8,128)S(1)}, f32[128,256]{1,0:T(8,128)S(1)}, u32[]{:S(2)}, u32[]{:S(2)}) collective-permute-start(f32[128,256]{1,0:T(8,128)S(1)} %total.3.refs_2_.refs_3_), channel_id=1, source_target_pairs={{0,16},{8,24},{16,0},{24,8},{1,17},{9,25},{17,1},{25,9},{2,18},{10... | collective-permute-start | bytes 393224 | tf_op jit(solution)/shard_map/ppermute | solution.py:517
  85.0 13.5 %collective-permute-start.17 = (f32[128,256]{1,0:T(8,128)S(1)}, f32[128,256]{1,0:T(8,128)S(1)}, u32[]{:S(2)}, u32[]{:S(2)}) collective-permute-start(f32[128,256]{1,0:T(8,128)S(1)} %total.3.refs_2_.refs_3_), channel_id=1, source_target_pairs={{0,24},{8,16},{16,8},{24,0},{1,25},{9,17},{17,9},{25,1},{2,26},{10... | collective-permute-start | bytes 393224 | tf_op jit(solution)/shard_map/ppermute | solution.py:517
  86.3 12.1 %collective-permute-start.16 = (f32[128,256]{1,0:T(8,128)S(1)}, f32[128,256]{1,0:T(8,128)S(1)}, u32[]{:S(2)}, u32[]{:S(2)}) collective-permute-start(f32[128,256]{1,0:T(8,128)S(1)} %total.3.refs_2_.refs_3_), channel_id=1, source_target_pairs={{0,8},{8,0},{16,24},{24,16},{1,9},{9,1},{17,25},{25,17},{2,10},{10... | collective-permute-start | bytes 393224 | tf_op jit(solution)/shard_map/ppermute | solution.py:517
  88.4 4.5 %copy-start.1 = (f32[512,512]{1,0:T(8,128)S(1)}, f32[512,512]{1,0:T(8,128)}, u32[]{:S(2)}) copy-start(f32[512,512]{1,0:T(8,128)} %copy-done) | copy-start | bytes 3145732

commit v9 on v8

--- a/solution.py
+++ b/solution.py
@@ -409,18 +409,18 @@
         m_ref[pl.ds(at, count), :] = ref[...]
     columns = pl.ds(index * width, width)
     copies = []
-    for step in range(both // LANES):
-        lo, hi = step * LANES, (step + 1) * LANES
+    for step in range(both // PANEL):
+        lo, hi = step * PANEL, (step + 1) * PANEL
         w_ref[lo:hi, :] = dot(inv_ref[lo:hi, :hi], m_ref[:hi, :], ((1,), (0,)))
         copies.append(
             pltpu.make_async_copy(w_ref.at[lo:hi], upper_ref.at[lo:hi, columns], sems.at[0, step])
         )
         copies[-1].start()
-    rows = LANES // two
+    rows = PANEL // two
     held_owners = rows // part
     for step in range(owners // held_owners):
-        lo = step * LANES
-        product = dot(basis_ref[lo : lo + LANES, :], w_ref[...], ((1,), (0,)))
+        lo = step * PANEL
+        product = dot(basis_ref[lo : lo + PANEL, :], w_ref[...], ((1,), (0,)))
         for owner in range(held_owners):
             for child in range(two):
                 row = (owner * two + child) * part

time: 103 us -> 103 us (level)
  no operation moved by 1% of the time
where the time goes in v9:
time: 103 us; the launch traced here: 102 us
  Pallas kernels  35.9 us (35%)
  starting transfers between devices  33 us (32%)
  blocking collectives  18 us (17%)
  waiting for transfers between devices  12.8 us (12%)
  local copies, waits for them, and re-layouts  1.23 us (1%)
    pallas_call x4, Pallas kernels, stage(): pl.pallas_call(lambda *refs: stage_kernel(lo, *refs), out_shape=(shape(si...  18.4 us
    all_to_all x1, blocking collectives, per_device(): spread = lax.all_to_all(pack(children, cols), 'col', 0, 0, tiled=True)  18 us
    ppermute x6, starting transfers between devices, per_device(): lax.ppermute(total, 'row', pairs_xor(rows, k))  8.98 us
    ppermute x6, starting transfers between devices, even_pieces(): lax.ppermute(piece, 'col', pairs_xor(size, k))  6.98 us
    pallas_call x2, Pallas kernels, finish(): pl.pallas_call(lambda *refs: finish_kernel(index, masks, *refs), out_shap...  6.97 us
    all_to_all x1, starting transfers between devices, per_device(): parts = lax.all_to_all(products, 'row', 0, 0, tiled=True)  5.33 us
    all_to_all x1, starting transfers between devices, per_device(): front = lax.all_to_all(ordered, 'col', 0, 0, tiled=True)  4.93 us
    ppermute x3, starting transfers between devices, per_device(): lax.ppermute(x, 'row', pairs_xor(rows, k))  4.45 us
  transfers between devices with their start and end apart: 21, of which 9 were waited for; matrix products, arithmetic and copies ran while one was open for 0% of the time, Pallas kernels for 28%

profile of v9, /device:TPU:10, one launch (start us, length us, event | category | flops | bytes accessed | tf_op | source)
XLA Modules:
  0.0 101.9 jit_solution(14489445273627947875)
XLA Ops:
  0.6 1.2 %copy-done.2 = f32[2,256,512]{2,1,0:T(8,128)S(1)} copy-done((f32[2,256,512]{2,1,0:T(8,128)S(1)}, f32[2,256,512]{2,1,0:T(8,128)}, u32[]{:S(2)}) %copy-start.2) | copy-done | bytes 1048600
  1.9 0.1 pack.1
  1.9 0.0 copy-start.3
  1.9 18.0 %all_to_all.15.spread_ref = f32[8,2,32,512]{3,2,1,0:T(8,128)S(1)} all-to-all(f32[8,2,32,512]{3,2,1,0:T(8,128)S(1)} %pack.1), channel_id=1, replica_groups=mesh['row'=4,'col'=8] {'col'}, dimensions={0} | all-to-all | bytes 2097152 | tf_op jit(solution)/shard_map/all_to_all | solution.py:491
  19.9 1.7 %order.1 = (f32[8,2,32,512]{3,2,1,0:T(8,128)}, f32[64,512]{1,0:T(8,128)S(1)}) custom-call(s32[2,16]{1,0:T(2,128)S(1)} %copy-done.3, f32[8,2,32,512]{3,2,1,0:T(8,128)S(1)} %all_to_all.15.spread_ref), custom_call_target="tpu_custom_call" | custom-call | flops 1000 | bytes 1000 | tf_op jit(solution)/shard_map/order/pallas_call | solution.py:78
  21.6 1.5 %collective-permute-start.2 = (f32[64,512]{1,0:T(8,128)S(1)}, f32[64,512]{1,0:T(8,128)S(1)}, u32[]{:S(2)}, u32[]{:S(2)}) collective-permute-start(f32[64,512]{1,0:T(8,128)S(1)} %get-tuple-element.19.refs_0_), channel_id=1, source_target_pairs={{0,6},{1,7},{2,4},{3,5},{4,2},{5,3},{6,0},{7,1},{8,14},{9,15},{10,... | collective-permute-start | bytes 393224 | tf_op jit(solution)/shard_map/ppermute | solution.py:467
  23.0 1.5 %collective-permute-start.1 = (f32[64,512]{1,0:T(8,128)S(1)}, f32[64,512]{1,0:T(8,128)S(1)}, u32[]{:S(2)}, u32[]{:S(2)}) collective-permute-start(f32[64,512]{1,0:T(8,128)S(1)} %get-tuple-element.19.refs_0_), channel_id=1, source_target_pairs={{0,4},{1,5},{2,6},{3,7},{4,0},{5,1},{6,2},{7,3},{8,12},{9,13},{10,... | collective-permute-start | bytes 393224 | tf_op jit(solution)/shard_map/ppermute | solution.py:467
  24.5 0.6 collective-permute-start
  25.0 4.9 %all-to-all-start.1 = ((f32[8,2,32,512]{3,2,1,0:T(8,128)}), f32[8,2,32,512]{3,2,1,0:T(8,128)S(1)}, u32[]{:S(2)}, u32[]{:S(2)}) async-start(f32[8,2,32,512]{3,2,1,0:T(8,128)} %get-tuple-element.22), calls=%async_computation.1 | async-start | bytes 2097152 | tf_op jit(solution)/shard_map/all_to_all | solution.py:494
  30.0 0.2 collective-permute-done.1.refs_2_
  30.2 0.1 collective-permute-start.3
  30.3 1.9 %collective-permute-done.3.far_ref = f32[4,64,512]{2,1,0:T(8,128)S(1)} collective-permute-done((f32[4,64,512]{2,1,0:T(8,128)S(1)}, f32[4,64,512]{2,1,0:T(8,128)S(1)}, u32[]{:S(2)}, u32[]{:S(2)}) %collective-permute-start.3) | collective-permute-done | bytes 524320 | tf_op jit(solution)/shard_map/ppermute | solution.py:496
  32.2 0.7 tile.1
  32.9 0.5 collective-permute-start.4
  33.4 4.0 %collective-permute-done.4 = f32[160,128]{1,0:T(8,128)S(1)} collective-permute-done((f32[160,128]{1,0:T(8,128)S(1)}, f32[160,128]{1,0:T(8,128)S(1)}, u32[]{:S(2)}, u32[]{:S(2)}) %collective-permute-start.4) | collective-permute-done | bytes 81952 | tf_op jit(solution)/shard_map/ppermute | solution.py:478
  37.5 1.6 %collective-permute-start.5 = (f32[160,128]{1,0:T(8,128)S(1)}, f32[160,128]{1,0:T(8,128)S(1)}, u32[]{:S(2)}, u32[]{:S(2)}) collective-permute-start(f32[160,128]{1,0:T(8,128)S(1)} %add.4.left_ref), channel_id=1, source_target_pairs={{0,24},{8,16},{16,8},{24,0},{1,25},{9,17},{17,9},{25,1},{2,26},{10... | collective-permute-start | bytes 245768 | tf_op jit(solution)/shard_map/ppermute | solution.py:480
  39.1 0.3 turn.1.refs_0_
  39.4 3.5 %collective-permute-done.5.right_ref = f32[160,128]{1,0:T(8,128)S(1)} collective-permute-done((f32[160,128]{1,0:T(8,128)S(1)}, f32[160,128]{1,0:T(8,128)S(1)}, u32[]{:S(2)}, u32[]{:S(2)}) %collective-permute-start.5) | collective-permute-done | bytes 81952 | tf_op jit(solution)/shard_map/ppermute | solution.py:480
  43.0 0.9 all-to-all-done.1.refs_2_
  43.9 1.9 %multiply.2.refs_3_.refs_4_ = f32[4,128,256]{2,1,0:T(8,128)} custom-call(f32[512,512]{1,0:T(8,128)S(1)} %turn.1.refs_0_, f32[512,512]{1,0:T(8,128)S(1)} %bitcast.1, f32[160,128]{1,0:T(8,128)S(1)} %add.5.refs_2_.refs_0_), custom_call_target="tpu_custom_call" | custom-call | flops 1000 | bytes 1000 | tf_op jit(solution)/shard_map/multiply/pallas_call | solution.py:296
  45.8 5.3 %all-to-all-start.2 = ((f32[4,128,256]{2,1,0:T(8,128)}), f32[4,128,256]{2,1,0:T(8,128)}, u32[]{:S(2)}, u32[]{:S(2)}) async-start(f32[4,128,256]{2,1,0:T(8,128)} %multiply.2.refs_3_.refs_4_), calls=%async_computation.2 | async-start | bytes 1048576 | tf_op jit(solution)/shard_map/all_to_all | solution.py:504
  51.1 1.5 %collective-permute-start.8 = (f32[160,128]{1,0:T(8,128)S(1)}, f32[160,128]{1,0:T(8,128)S(1)}, u32[]{:S(2)}, u32[]{:S(2)}) collective-permute-start(f32[160,128]{1,0:T(8,128)S(1)} %add.5.refs_2_.refs_0_), channel_id=1, source_target_pairs={{0,6},{1,7},{2,4},{3,5},{4,2},{5,3},{6,0},{7,1},{8,14},{9,15},{10,... | collective-permute-start | bytes 245768 | tf_op jit(solution)/shard_map/ppermute | solution.py:467
  52.6 1.5 %collective-permute-start.7 = (f32[160,128]{1,0:T(8,128)S(1)}, f32[160,128]{1,0:T(8,128)S(1)}, u32[]{:S(2)}, u32[]{:S(2)}) collective-permute-start(f32[160,128]{1,0:T(8,128)S(1)} %add.5.refs_2_.refs_0_), channel_id=1, source_target_pairs={{0,4},{1,5},{2,6},{3,7},{4,0},{5,1},{6,2},{7,3},{8,12},{9,13},{10,... | collective-permute-start | bytes 245768 | tf_op jit(solution)/shard_map/ppermute | solution.py:467
  54.1 0.5 collective-permute-start.6
  54.6 1.9 %multiply.3 = (f32[128,256]{1,0:T(8,128)S(1)}, f32[128,256]{1,0:T(8,128)}, f32[128,256]{1,0:T(8,128)}, f32[128,256]{1,0:T(8,128)}) custom-call(f32[512,512]{1,0:T(8,128)S(1)} %turn.1.refs_0_, f32[512,512]{1,0:T(8,128)S(1)} %bitcast.2, f32[160,128]{1,0:T(8,128)S(1)} %add.5.refs_2_.refs_0_, f32[4,128,256]{2,1,0:T(8,128)} %multiply.2.refs_3_.refs_4_), custom_call_target="tpu_custom_call" | custom-call | flops 1000 | bytes 1000 | tf_op jit(solution)/shard_map/multiply/pallas_call | solution.py:322
  56.5 0.3 collective-permute-done.8.refs_3_
  56.8 0.8 collective-permute-done.7.refs_2_
  57.6 0.9 collective-permute-done.6.refs_1_
  58.6 0.1 collective-permute-start.9
  58.7 0.1 collective-permute-start.10
  58.7 2.9 %collective-permute-start.11 = (f32[128,256]{1,0:T(8,128)}, f32[128,256]{1,0:T(8,128)S(1)}, u32[]{:S(2)}, u32[]{:S(2)}) collective-permute-start(f32[128,256]{1,0:T(8,128)} %get-tuple-element.31), channel_id=1, source_target_pairs={{0,24},{8,16},{16,8},{24,0},{1,25},{9,17},{17,9},{25,1},{2,26},{10... | collective-permute-start | bytes 393224 | tf_op jit(solution)/shard_map/ppermute | solution.py:507
  61.7 1.5 %collective-permute-start.12 = (f32[128,256]{1,0:T(8,128)}, f32[128,256]{1,0:T(8,128)}, u32[]{:S(2)}, u32[]{:S(2)}) collective-permute-start(f32[128,256]{1,0:T(8,128)} %get-tuple-element.32), channel_id=1, source_target_pairs={{0,16},{8,24},{16,0},{24,8},{1,17},{9,25},{17,1},{25,9},{2,18},{10... | collective-permute-start | bytes 393224 | tf_op jit(solution)/shard_map/ppermute | solution.py:507
  63.1 4.9 %stage.4 = (f32[512,512]{1,0:T(8,128)S(1)}, f32[512,512]{1,0:T(8,128)S(1)}) custom-call(f32[4,160,128]{2,1,0:T(8,128)S(1)} %stack.3.refs_0_, f32[4,160,128]{2,1,0:T(8,128)S(1)} %collective-permute-done.9.refs_1_), custom_call_target="tpu_custom_call" | custom-call | flops 1000 | bytes 1000 | tf_op jit(solution)/shard_map/stage/pallas_call | solution.py:217
  68.1 1.1 %total.2.refs_2_.refs_3_ = f32[128,256]{1,0:T(8,128)S(1)} custom-call(f32[4,128,256]{2,1,0:T(8,128)} %all-to-all-done.2.parts_ref, f32[512,512]{1,0:T(8,128)S(1)} %get-tuple-element.25.refs_0_.refs_1_), custom_call_target="tpu_custom_call" | custom-call | flops 1000 | bytes 1000 | tf_op jit(solution)/shard_map/total/pallas_call | solution.py:386
  69.2 1.5 %collective-permute-start.15 = (f32[128,256]{1,0:T(8,128)S(1)}, f32[128,256]{1,0:T(8,128)S(1)}, u32[]{:S(2)}, u32[]{:S(2)}) collective-permute-start(f32[128,256]{1,0:T(8,128)S(1)} %total.2.refs_2_.refs_3_), channel_id=1, source_target_pairs={{0,16},{8,24},{16,0},{24,8},{1,17},{9,25},{17,1},{25,9},{2,18},{10... | collective-permute-start | bytes 393224 | tf_op jit(solution)/shard_map/ppermute | solution.py:517
  70.7 0.1 collective-permute-start.14
  70.8 4.7 %stage.5 = (f32[512,512]{1,0:T(8,128)S(1)}, f32[512,512]{1,0:T(8,128)S(1)}) custom-call(f32[512,512]{1,0:T(8,128)S(1)} %get-tuple-element.24.refs_0_, f32[512,512]{1,0:T(8,128)S(1)} %get-tuple-element.25.refs_0_.refs_1_, f32[128,256]{1,0:T(8,128)S(1)} %total.2.refs_2_.refs_3_), custom_call_target="tpu_custom_call", output_to_operand_aliasing={{0}: (0, {}), {1}: (1, {})} | custom-call | flops 1000 | bytes 1000 | tf_op jit(solution)/shard_map/stage/pallas_call | solution.py:217
  75.6 4.5 %stage.6 = (f32[512,512]{1,0:T(8,128)S(1)}, f32[512,512]{1,0:T(8,128)S(1)}) custom-call(f32[512,512]{1,0:T(8,128)S(1)} %get-tuple-element.26.refs_0_, f32[512,512]{1,0:T(8,128)S(1)} %get-tuple-element.27.refs_1_), custom_call_target="tpu_custom_call", output_to_operand_aliasing={{0}: (0, {}), {1}: (1, {})} | custom-call | flops 1000 | bytes 1000 | tf_op jit(solution)/shard_map/stage/pallas_call | solution.py:217
  80.1 2.9 %collective-permute-start.13 = (f32[128,256]{1,0:T(8,128)S(1)}, f32[128,256]{1,0:T(8,128)S(1)}, u32[]{:S(2)}, u32[]{:S(2)}) collective-permute-start(f32[128,256]{1,0:T(8,128)S(1)} %total.2.refs_2_.refs_3_), channel_id=1, source_target_pairs={{0,8},{8,0},{16,24},{24,16},{1,9},{9,1},{17,25},{25,17},{2,10},{10... | collective-permute-start | bytes 393224 | tf_op jit(solution)/shard_map/ppermute | solution.py:517
  83.0 0.9 total.3.refs_2_.refs_3_
  84.0 1.0 collective-permute-start.18
  85.0 1.3 %collective-permute-start.17 = (f32[128,256]{1,0:T(8,128)S(1)}, f32[128,256]{1,0:T(8,128)S(1)}, u32[]{:S(2)}, u32[]{:S(2)}) collective-permute-start(f32[128,256]{1,0:T(8,128)S(1)} %total.3.refs_2_.refs_3_), channel_id=1, source_target_pairs={{0,24},{8,16},{16,8},{24,0},{1,25},{9,17},{17,9},{25,1},{2,26},{10... | collective-permute-start | bytes 393224 | tf_op jit(solution)/shard_map/ppermute | solution.py:517
  86.3 2.1 %collective-permute-start.16 = (f32[128,256]{1,0:T(8,128)S(1)}, f32[128,256]{1,0:T(8,128)S(1)}, u32[]{:S(2)}, u32[]{:S(2)}) collective-permute-start(f32[128,256]{1,0:T(8,128)S(1)} %total.3.refs_2_.refs_3_), channel_id=1, source_target_pairs={{0,8},{8,0},{16,24},{24,16},{1,9},{9,1},{17,25},{25,17},{2,10},{10... | collective-permute-start | bytes 393224 | tf_op jit(solution)/shard_map/ppermute | solution.py:517
  88.4 4.2 %stage.7 = (f32[512,512]{1,0:T(8,128)S(1)}, f32[512,512]{1,0:T(8,128)S(1)}) custom-call(f32[512,512]{1,0:T(8,128)S(1)} %get-tuple-element.28.refs_0_, f32[512,512]{1,0:T(8,128)S(1)} %get-tuple-element.29.refs_4_.refs_1_, f32[128,256]{1,0:T(8,128)S(1)} %total.3.refs_2_.refs_3_), custom_call_target="tpu_custom_call", output_to_operand_aliasing={{0}: (0, {}), {1}: (1, {})} | custom-call | flops 1000 | bytes 1000 | tf_op jit(solution)/shard_map/stage/pallas_call | solution.py:217
  92.7 0.2 collective-permute-done.14.refs_1_.refs_5_
  92.9 1.8 %basis.1.refs_1_ = f32[512,512]{1,0:T(8,128)S(1)} custom-call(f32[512,512]{1,0:T(8,128)S(1)} %copy-done.1, f32[512,512]{1,0:T(8,128)S(1)} %get-tuple-element.33.inv_ref.refs_0_, f32[128,256]{1,0:T(8,128)S(1)} %collective-permute-done.13.refs_0_.refs_4_, f32[128,256]{1,0:T(8,128)S(1)} %collective-permute-done.14.refs_1_.refs_5_, ...), custom_call_target="tpu_custom_call" | custom-call | flops 1000 | bytes 1000 | tf_op jit(solution)/shard_map/basis/pallas_call | solution.py:358
  94.7 3.5 %finish.2 = (f32[512,512]{1,0:T(8,128)}, f32[2,256,512]{2,1,0:T(8,128)}) custom-call(f32[512,512]{1,0:T(8,128)S(1)} %get-tuple-element.33.inv_ref.refs_0_, f32[512,512]{1,0:T(8,128)S(1)} %basis.1.refs_1_, f32[8,2,32,512]{3,2,1,0:T(8,128)S(1)} %all-to-all-done.1.refs_2_, f32[128,256]{1,0:T(8,128)S(1)} %total.2.refs_2_.refs_3_, ...), custom_call_target="tpu_custom_call" | custom-call | flops 1000 | bytes 1000 | tf_op jit(solution)/shard_map/finish/pallas_call | solution.py:444
  98.3 3.5 %finish.3 = (f32[512,512]{1,0:T(8,128)}, f32[2,256,512]{2,1,0:T(8,128)}) custom-call(f32[512,512]{1,0:T(8,128)S(1)} %get-tuple-element.33.inv_ref.refs_0_, f32[512,512]{1,0:T(8,128)S(1)} %basis.1.refs_1_, f32[8,2,32,512]{3,2,1,0:T(8,128)S(1)} %all-to-all-done.1.refs_2_, ...), custom_call_target="tpu_custom_call", output_to_operand_aliasing={{0}: (7, {}), {1}: (8, {})} | custom-call | flops 1000 | bytes 1000 | tf_op jit(solution)/shard_map/finish/pallas_call | solution.py:444
  (22 shorter events, 0.1 us)
Async XLA Ops:
  0.6 1.2 %copy-start.2 = (f32[2,256,512]{2,1,0:T(8,128)S(1)}, f32[2,256,512]{2,1,0:T(8,128)}, u32[]{:S(2)}) copy-start(f32[2,256,512]{2,1,0:T(8,128)} %children_ref.1) | copy-start | bytes 3145732
  1.9 18.0 %copy-start.3 = (s32[2,16]{1,0:T(2,128)S(1)}, s32[2,16]{1,0:T(2,128)}, u32[]{:S(2)}) copy-start(s32[2,16]{1,0:T(2,128)} %maps_ref.1) | copy-start | bytes 388
  21.6 8.4 %collective-permute-start.2 = (f32[64,512]{1,0:T(8,128)S(1)}, f32[64,512]{1,0:T(8,128)S(1)}, u32[]{:S(2)}, u32[]{:S(2)}) collective-permute-start(f32[64,512]{1,0:T(8,128)S(1)} %get-tuple-element.19.refs_0_), channel_id=1, source_target_pairs={{0,6},{1,7},{2,4},{3,5},{4,2},{5,3},{6,0},{7,1},{8,14},{9,15},{10,... | collective-permute-start | bytes 393224 | tf_op jit(solution)/shard_map/ppermute | solution.py:467
  23.0 7.1 %collective-permute-start.1 = (f32[64,512]{1,0:T(8,128)S(1)}, f32[64,512]{1,0:T(8,128)S(1)}, u32[]{:S(2)}, u32[]{:S(2)}) collective-permute-start(f32[64,512]{1,0:T(8,128)S(1)} %get-tuple-element.19.refs_0_), channel_id=1, source_target_pairs={{0,4},{1,5},{2,6},{3,7},{4,0},{5,1},{6,2},{7,3},{8,12},{9,13},{10,... | collective-permute-start | bytes 393224 | tf_op jit(solution)/shard_map/ppermute | solution.py:467
  24.5 5.7 %collective-permute-start = (f32[64,512]{1,0:T(8,128)S(1)}, f32[64,512]{1,0:T(8,128)S(1)}, u32[]{:S(2)}, u32[]{:S(2)}) collective-permute-start(f32[64,512]{1,0:T(8,128)S(1)} %get-tuple-element.19.refs_0_), channel_id=1, source_target_pairs={{0,2},{1,3},{2,0},{3,1},{4,6},{5,7},{6,4},{7,5},{8,10},{9,11},{10,... | collective-permute-start | bytes 393224 | tf_op jit(solution)/shard_map/ppermute | solution.py:467
  25.0 18.8 %all-to-all-start.1 = ((f32[8,2,32,512]{3,2,1,0:T(8,128)}), f32[8,2,32,512]{3,2,1,0:T(8,128)S(1)}, u32[]{:S(2)}, u32[]{:S(2)}) async-start(f32[8,2,32,512]{3,2,1,0:T(8,128)} %get-tuple-element.22), calls=%async_computation.1 | async-start | bytes 2097152 | tf_op jit(solution)/shard_map/all_to_all | solution.py:494
  30.2 2.0 %collective-permute-start.3 = (f32[4,64,512]{2,1,0:T(8,128)S(1)}, f32[4,64,512]{2,1,0:T(8,128)S(1)}, u32[]{:S(2)}, u32[]{:S(2)}) collective-permute-start(f32[4,64,512]{2,1,0:T(8,128)S(1)} %stack.2.near_ref), channel_id=1, source_target_pairs={{0,1},{1,0},{2,3},{3,2},{4,5},{5,4},{6,7},{7,6},{8,9},{9,8},{10,11... | collective-permute-start | bytes 1572872 | tf_op jit(solution)/shard_map/ppermute | solution.py:496
  32.9 6.6 %copy-start = (f32[512,512]{1,0:T(8,128)}, f32[512,512]{1,0:T(8,128)S(1)}, u32[]{:S(2)}) copy-start(f32[512,512]{1,0:T(8,128)S(1)} %get-tuple-element.21.panels_ref) | copy-start | bytes 3145732
  32.9 4.6 %collective-permute-start.4 = (f32[160,128]{1,0:T(8,128)S(1)}, f32[160,128]{1,0:T(8,128)S(1)}, u32[]{:S(2)}, u32[]{:S(2)}) collective-permute-start(f32[160,128]{1,0:T(8,128)S(1)} %get-tuple-element.20), channel_id=1, source_target_pairs={{0,8},{8,0},{16,24},{24,16},{1,9},{9,1},{17,25},{25,17},{2,10},{10... | collective-permute-start | bytes 245768 | tf_op jit(solution)/shard_map/ppermute | solution.py:478
  37.5 5.5 %collective-permute-start.5 = (f32[160,128]{1,0:T(8,128)S(1)}, f32[160,128]{1,0:T(8,128)S(1)}, u32[]{:S(2)}, u32[]{:S(2)}) collective-permute-start(f32[160,128]{1,0:T(8,128)S(1)} %add.4.left_ref), channel_id=1, source_target_pairs={{0,24},{8,16},{16,8},{24,0},{1,25},{9,17},{17,9},{25,1},{2,26},{10... | collective-permute-start | bytes 245768 | tf_op jit(solution)/shard_map/ppermute | solution.py:480
  45.8 22.3 %all-to-all-start.2 = ((f32[4,128,256]{2,1,0:T(8,128)}), f32[4,128,256]{2,1,0:T(8,128)}, u32[]{:S(2)}, u32[]{:S(2)}) async-start(f32[4,128,256]{2,1,0:T(8,128)} %multiply.2.refs_3_.refs_4_), calls=%async_computation.2 | async-start | bytes 1048576 | tf_op jit(solution)/shard_map/all_to_all | solution.py:504
  51.1 5.7 %collective-permute-start.8 = (f32[160,128]{1,0:T(8,128)S(1)}, f32[160,128]{1,0:T(8,128)S(1)}, u32[]{:S(2)}, u32[]{:S(2)}) collective-permute-start(f32[160,128]{1,0:T(8,128)S(1)} %add.5.refs_2_.refs_0_), channel_id=1, source_target_pairs={{0,6},{1,7},{2,4},{3,5},{4,2},{5,3},{6,0},{7,1},{8,14},{9,15},{10,... | collective-permute-start | bytes 245768 | tf_op jit(solution)/shard_map/ppermute | solution.py:467
  52.6 5.0 %collective-permute-start.7 = (f32[160,128]{1,0:T(8,128)S(1)}, f32[160,128]{1,0:T(8,128)S(1)}, u32[]{:S(2)}, u32[]{:S(2)}) collective-permute-start(f32[160,128]{1,0:T(8,128)S(1)} %add.5.refs_2_.refs_0_), channel_id=1, source_target_pairs={{0,4},{1,5},{2,6},{3,7},{4,0},{5,1},{6,2},{7,3},{8,12},{9,13},{10,... | collective-permute-start | bytes 245768 | tf_op jit(solution)/shard_map/ppermute | solution.py:467
  54.1 4.4 %collective-permute-start.6 = (f32[160,128]{1,0:T(8,128)S(1)}, f32[160,128]{1,0:T(8,128)S(1)}, u32[]{:S(2)}, u32[]{:S(2)}) collective-permute-start(f32[160,128]{1,0:T(8,128)S(1)} %add.5.refs_2_.refs_0_), channel_id=1, source_target_pairs={{0,2},{1,3},{2,0},{3,1},{4,6},{5,7},{6,4},{7,5},{8,10},{9,11},{10,... | collective-permute-start | bytes 245768 | tf_op jit(solution)/shard_map/ppermute | solution.py:467
  58.6 4.5 %collective-permute-start.9 = (f32[4,160,128]{2,1,0:T(8,128)S(1)}, f32[4,160,128]{2,1,0:T(8,128)S(1)}, u32[]{:S(2)}, u32[]{:S(2)}) collective-permute-start(f32[4,160,128]{2,1,0:T(8,128)S(1)} %stack.3.refs_0_), channel_id=1, source_target_pairs={{0,1},{1,0},{2,3},{3,2},{4,5},{5,4},{6,7},{7,6},{8,9},{9,8},{10,11... | collective-permute-start | bytes 983048 | tf_op jit(solution)/shard_map/ppermute | solution.py:510
  58.7 21.4 %collective-permute-start.10 = (f32[128,256]{1,0:T(8,128)}, f32[128,256]{1,0:T(8,128)S(1)}, u32[]{:S(2)}, u32[]{:S(2)}) collective-permute-start(f32[128,256]{1,0:T(8,128)} %get-tuple-element.30), channel_id=1, source_target_pairs={{0,8},{8,0},{16,24},{24,16},{1,9},{9,1},{17,25},{25,17},{2,10},{10... | collective-permute-start | bytes 393224 | tf_op jit(solution)/shard_map/ppermute | solution.py:507
  58.7 24.3 %collective-permute-start.11 = (f32[128,256]{1,0:T(8,128)}, f32[128,256]{1,0:T(8,128)S(1)}, u32[]{:S(2)}, u32[]{:S(2)}) collective-permute-start(f32[128,256]{1,0:T(8,128)} %get-tuple-element.31), channel_id=1, source_target_pairs={{0,24},{8,16},{16,8},{24,0},{1,25},{9,17},{17,9},{25,1},{2,26},{10... | collective-permute-start | bytes 393224 | tf_op jit(solution)/shard_map/ppermute | solution.py:507
  61.7 21.4 %collective-permute-start.12 = (f32[128,256]{1,0:T(8,128)}, f32[128,256]{1,0:T(8,128)}, u32[]{:S(2)}, u32[]{:S(2)}) collective-permute-start(f32[128,256]{1,0:T(8,128)} %get-tuple-element.32), channel_id=1, source_target_pairs={{0,16},{8,24},{16,0},{24,8},{1,17},{9,25},{17,1},{25,9},{2,18},{10... | collective-permute-start | bytes 393224 | tf_op jit(solution)/shard_map/ppermute | solution.py:507
  69.2 17.1 %collective-permute-start.15 = (f32[128,256]{1,0:T(8,128)S(1)}, f32[128,256]{1,0:T(8,128)S(1)}, u32[]{:S(2)}, u32[]{:S(2)}) collective-permute-start(f32[128,256]{1,0:T(8,128)S(1)} %total.2.refs_2_.refs_3_), channel_id=1, source_target_pairs={{0,16},{8,24},{16,0},{24,8},{1,17},{9,25},{17,1},{25,9},{2,18},{10... | collective-permute-start | bytes 393224 | tf_op jit(solution)/shard_map/ppermute | solution.py:517
  70.7 22.1 %collective-permute-start.14 = (f32[128,256]{1,0:T(8,128)S(1)}, f32[128,256]{1,0:T(8,128)S(1)}, u32[]{:S(2)}, u32[]{:S(2)}) collective-permute-start(f32[128,256]{1,0:T(8,128)S(1)} %total.2.refs_2_.refs_3_), channel_id=1, source_target_pairs={{0,24},{8,16},{16,8},{24,0},{1,25},{9,17},{17,9},{25,1},{2,26},{10... | collective-permute-start | bytes 393224 | tf_op jit(solution)/shard_map/ppermute | solution.py:517
  80.1 12.8 %collective-permute-start.13 = (f32[128,256]{1,0:T(8,128)S(1)}, f32[128,256]{1,0:T(8,128)S(1)}, u32[]{:S(2)}, u32[]{:S(2)}) collective-permute-start(f32[128,256]{1,0:T(8,128)S(1)} %total.2.refs_2_.refs_3_), channel_id=1, source_target_pairs={{0,8},{8,0},{16,24},{24,16},{1,9},{9,1},{17,25},{25,17},{2,10},{10... | collective-permute-start | bytes 393224 | tf_op jit(solution)/shard_map/ppermute | solution.py:517
  84.0 14.3 %collective-permute-start.18 = (f32[128,256]{1,0:T(8,128)S(1)}, f32[128,256]{1,0:T(8,128)S(1)}, u32[]{:S(2)}, u32[]{:S(2)}) collective-permute-start(f32[128,256]{1,0:T(8,128)S(1)} %total.3.refs_2_.refs_3_), channel_id=1, source_target_pairs={{0,16},{8,24},{16,0},{24,8},{1,17},{9,25},{17,1},{25,9},{2,18},{10... | collective-permute-start | bytes 393224 | tf_op jit(solution)/shard_map/ppermute | solution.py:517
  85.0 13.3 %collective-permute-start.17 = (f32[128,256]{1,0:T(8,128)S(1)}, f32[128,256]{1,0:T(8,128)S(1)}, u32[]{:S(2)}, u32[]{:S(2)}) collective-permute-start(f32[128,256]{1,0:T(8,128)S(1)} %total.3.refs_2_.refs_3_), channel_id=1, source_target_pairs={{0,24},{8,16},{16,8},{24,0},{1,25},{9,17},{17,9},{25,1},{2,26},{10... | collective-permute-start | bytes 393224 | tf_op jit(solution)/shard_map/ppermute | solution.py:517
  86.3 12.0 %collective-permute-start.16 = (f32[128,256]{1,0:T(8,128)S(1)}, f32[128,256]{1,0:T(8,128)S(1)}, u32[]{:S(2)}, u32[]{:S(2)}) collective-permute-start(f32[128,256]{1,0:T(8,128)S(1)} %total.3.refs_2_.refs_3_), channel_id=1, source_target_pairs={{0,8},{8,0},{16,24},{24,16},{1,9},{9,1},{17,25},{25,17},{2,10},{10... | collective-permute-start | bytes 393224 | tf_op jit(solution)/shard_map/ppermute | solution.py:517
  88.4 4.5 %copy-start.1 = (f32[512,512]{1,0:T(8,128)S(1)}, f32[512,512]{1,0:T(8,128)}, u32[]{:S(2)}) copy-start(f32[512,512]{1,0:T(8,128)} %copy-done) | copy-start | bytes 3145732
